TPU v7x, 1024 devices: a whole 4x8x16 slice. The times are simulated.
1024 devices in a mesh: gx: 256 (over z, y, core), gy: 4 (over x).
Axes of the slice: x: 4, y: 8, z: 16, core: 2. Of those that a mesh axis runs over, the one named last changes fastest.
Arguments:
- rhs: float32 [8, 512, 32, 128], P(None, 'gx', 'gy'), may hold values from -6 to 6
- classes: int32 [512, 32, 128], P('gx', 'gy'), may hold values from 0 to 3
- supports: int32 [512, 32, 128], P('gx', 'gy'), may hold values 0 or 1
Outputs:
- solution: float32 [8, 512, 32, 128], P(None, 'gx', 'gy')
- residual: float32 [8, 512, 32, 128], P(None, 'gx', 'gy')
- new_direction: float32 [8, 512, 32, 128], P(None, 'gx', 'gy')
Inputs may be any that keep to these rules, and one draw needn't show every extreme that they name: `supports`: 1 marks a grounded node.
All inputs are finite; a program needn't handle non-finite values. No bound on the sum of `supports` on one device may be relied on, other than what follows from the above.
Results may differ from a plain program's by a relative error of at most 0.0003.
Values sent between devices are 32-bit elements; how exact they have to be, the bound alone decides.
No kernel may reach another device: no remote copies, remote signals or barrier semaphores. Data moves between devices by JAX's collectives and lax.ppermute only.
A program may use at most 32 MiB of HBM per device.

v0:
```python
import jax
import jax.numpy as jnp
from jax import lax
from jax.sharding import PartitionSpec as P

COARSE_SWEEPS = 2


SPRING = 8.0
OMEGA = 0.6
DAMP = 0.5
SELF_WEIGHT = 5.0 / 12.0


def passed_along(shard, axis, by):
    devices = lax.axis_size(axis)
    pairs = [(i, i + by) for i in range(devices) if 0 <= i + by < devices]
    return lax.ppermute(shard, axis, pairs)


def with_halo(shard, sides, width):
    for axis, dim in sides:
        devices, length = (lax.axis_size(axis), shard.shape[dim])
        up = [(i, (i + 1) % devices) for i in range(devices - 1)]
        down = [(j, i) for i, j in up]
        last = lax.slice_in_dim(shard, length - width, length, axis=dim)
        first = lax.slice_in_dim(shard, 0, width, axis=dim)
        before = lax.ppermute(last, axis, up)
        after = lax.ppermute(first, axis, down)
        shard = jnp.concatenate([before, shard, after], axis=dim)
    return shard


def stiffness(classes):
    density = (classes.astype(jnp.float32) + 1.0) / 4.0
    return 0.001 + density * density * density


def hex_product(padded, scale_ext):
    nx = scale_ext.shape[0] - 1
    ny = scale_ext.shape[1] - 1
    nz = scale_ext.shape[2] - 1
    corners = {}
    for a in (0, 1):
        for b in (0, 1):
            for c in (0, 1):
                corners[a, b, c] = padded[..., a : a + nx + 1, b : b + ny + 1, c : c + nz + 1]
    summed = sum(corners.values())
    result = None
    for key in corners:
        a, b, c = key
        corner = corners[key]
        adjacent = corners[1 - a, b, c] + corners[a, 1 - b, c] + corners[a, b, 1 - c]
        weighted = scale_ext * (SELF_WEIGHT * corner + adjacent / 12.0 - summed / 12.0)
        piece = weighted[..., 1 - a : 1 - a + nx, 1 - b : 1 - b + ny, 1 - c : 1 - c + nz]
        result = piece if result is None else result + piece
    return result


def prolong(field):
    k, a, b, c = field.shape
    wide = jnp.broadcast_to(field[:, :, None, :, None, :, None], (k, a, 2, b, 2, c, 2))
    return wide.reshape(k, 2 * a, 2 * b, 2 * c)


def restrict(field):
    k, a, b, c = field.shape
    return field.reshape(k, a // 2, 2, b // 2, 2, c // 2, 2).sum(axis=(2, 4, 6))


def inner_block(left, right):
    count = left.shape[0]
    return jnp.dot(
        left.reshape(count, -1), right.reshape(count, -1).T, precision=lax.Precision.HIGHEST
    )


def recombine(coef, field):
    count = field.shape[0]
    return jnp.dot(coef.T, field.reshape(count, -1), precision=lax.Precision.HIGHEST).reshape(
        field.shape
    )


def spd_solve(matrix, right):
    lower = jnp.linalg.cholesky(matrix)
    middle = lax.linalg.triangular_solve(lower, right, left_side=True, lower=True)
    return lax.linalg.triangular_solve(lower, middle, left_side=True, lower=True, transpose_a=True)


def local(rhs, classes, supports):
    scale = stiffness(classes)
    next_plane_x = passed_along(scale[:1], "gx", -1)
    scale_x = jnp.concatenate([scale, next_plane_x], axis=0)
    next_plane_y = passed_along(scale_x[:, :1], "gy", -1)
    scale_ext = jnp.concatenate([scale_x, next_plane_y], axis=1)
    scale_ext = jnp.pad(scale_ext, ((0, 0), (0, 0), (0, 1)))
    support = supports.astype(jnp.float32)
    nx, ny, nz = support.shape
    diagonal = SPRING * support
    for a in (0, 1):
        for b in (0, 1):
            for c in (0, 1):
                diagonal = diagonal + scale_ext[a : a + nx, b : b + ny, c : c + nz] / 3.0
    coarse_step = DAMP / restrict(diagonal[None])[0]

    def fine_apply(field):
        padded = with_halo(field, (("gx", 1), ("gy", 2)), 1)
        padded = jnp.pad(padded, ((0, 0), (0, 0), (0, 0), (1, 1)))
        return hex_product(padded, scale_ext) + SPRING * support * field

    def coarse_apply(coarse):
        return restrict(fine_apply(prolong(coarse)))

    def precondition(source):
        smoothed = OMEGA * source / diagonal
        coarse_res = restrict(source - fine_apply(smoothed))
        coarse = coarse_step * coarse_res
        for sweep in range(COARSE_SWEEPS):
            coarse = coarse + coarse_step * (coarse_res - coarse_apply(coarse))
        smoothed = smoothed + prolong(coarse)
        return smoothed + OMEGA * (source - fine_apply(smoothed)) / diagonal

    first_prec = precondition(rhs)
    applied = fine_apply(first_prec)
    curvature, projection = lax.psum(
        (inner_block(first_prec, applied), inner_block(first_prec, rhs)), ("gx", "gy")
    )
    curvature = 0.5 * (curvature + curvature.T)
    step_coef = spd_solve(curvature, projection)
    solution = recombine(step_coef, first_prec)
    residual = rhs - recombine(step_coef, applied)
    next_prec = precondition(residual)
    coupling = lax.psum(inner_block(applied, next_prec), ("gx", "gy"))
    turn_coef = -spd_solve(curvature, coupling)
    new_direction = next_prec + recombine(turn_coef, first_prec)
    return (solution, residual, new_direction)


def solution(mesh):
    placed = (P(None, "gx", "gy", None), P("gx", "gy", None), P("gx", "gy", None))
    return jax.shard_map(
        local,
        mesh=mesh,
        in_specs=placed,
        out_specs=(P(None, "gx", "gy", None), P(None, "gx", "gy", None), P(None, "gx", "gy", None)),
        check_vma=False,
    )
```

profile of v0, /device:TPU:1, one launch (start us, length us, event | category | flops | bytes accessed | tf_op | source)
XLA Modules:
  0.0 458.5 jit_solution(16191875561577307046)
XLA Ops:
  0.6 0.7 fusion.311
  1.3 16.1 %collective-permute-start = (f32[1,8,128]{2,1,0:T(8,128)S(1)}, f32[1,8,128]{2,1,0:T(8,128)S(1)}, u32[]{:S(2)}, u32[]{:S(2)}) collective-permute-start(f32[1,8,128]{2,1,0:T(8,128)S(1)} %slice.759), channel_id=1, source_target_pairs={{4,0},{8,4},{12,8},{16,12},{20,16},{24,20},{28,24},{32,28},{36,32}... | collective-permute-start | bytes 12296 | tf_op jit(solution)/shard_map/ppermute | solution.py:18
  17.4 0.8 collective-permute-done
  18.2 1.4 collective-permute-start.1
  19.6 3.0 collective-permute-done.1
  22.8 0.7 copy-done
  23.6 1.9 collective-permute-start.2
  25.5 2.8 collective-permute-start.3
  28.6 2.1 collective-permute-done.3
  30.7 1.7 collective-permute-start.4
  32.4 1.3 collective-permute-start.5
  33.7 3.2 collective-permute-done.5
  39.0 3.3 collective-permute-start.6
  42.4 1.9 collective-permute-start.7
  44.5 3.1 collective-permute-done.7
  47.6 1.6 collective-permute-start.8
  49.3 1.3 collective-permute-start.9
  50.6 3.2 collective-permute-done.9
  55.9 3.3 collective-permute-start.10
  59.2 1.9 collective-permute-start.11
  61.3 3.1 collective-permute-done.11
  64.5 1.6 collective-permute-start.12
  66.1 1.3 collective-permute-start.13
  67.5 3.2 collective-permute-done.13
  72.8 3.3 collective-permute-start.14
  76.2 1.9 collective-permute-start.15
  78.1 3.3 collective-permute-done.15
  81.4 1.6 collective-permute-start.16
  83.1 1.3 collective-permute-start.17
  84.4 3.2 collective-permute-done.17
  88.7 3.3 collective-permute-start.18
  92.0 1.9 collective-permute-start.19
  94.0 3.3 collective-permute-done.19
  97.3 1.6 collective-permute-start.20
  98.9 1.3 collective-permute-start.21
  100.4 3.0 collective-permute-done.21
  104.7 145.9 %all-reduce.10 = (f32[8,8]{1,0:T(8,128)S(1)}, f32[8,8]{1,0:T(8,128)S(1)}) all-reduce(f32[8,8]{1,0:T(8,128)S(1)} %convolution_bitcast_fusion.2, f32[8,8]{1,0:T(8,128)S(1)} %convolution_bitcast_fusion.3), channel_id=1, replica_groups=mesh['gx'=256,'gy'=4] {'gx','gy'}, use_global_device_ids=true, to_apply=%region_11.13 | all-reduce | flops 128 | bytes 1024 | tf_op jit(solution)/shard_map/psum | solution.py:126
  250.8 0.7 cholesky.18
  252.2 0.6 fusion.319
  254.1 1.9 collective-permute-start.22
  256.0 2.4 collective-permute-start.23
  258.4 2.8 collective-permute-done.23
  261.2 3.6 collective-permute-start.24
  264.9 1.5 collective-permute-start.25
  266.4 3.0 collective-permute-done.25
  271.5 3.3 collective-permute-start.26
  274.9 1.9 collective-permute-start.27
  277.0 3.1 collective-permute-done.27
  280.1 1.6 collective-permute-start.28
  281.8 1.3 collective-permute-start.29
  283.1 3.2 collective-permute-done.29
  288.4 3.3 collective-permute-start.30
  291.7 1.9 collective-permute-start.31
  293.8 3.1 collective-permute-done.31
  297.0 3.0 collective-permute-start.32
  300.0 1.3 collective-permute-start.33
  301.3 3.2 collective-permute-done.33
  306.7 3.3 collective-permute-start.34
  310.0 1.9 collective-permute-start.35
  312.0 3.3 collective-permute-done.35
  315.3 1.6 collective-permute-start.36
  316.9 1.3 collective-permute-start.37
  319.7 1.7 collective-permute-done.37
  322.7 134.5 %psum.23 = f32[8,8]{1,0:T(8,128)S(1)} all-reduce(f32[8,8]{1,0:T(8,128)S(1)} %convolution_bitcast_fusion), channel_id=1, replica_groups=mesh['gx'=256,'gy'=4] {'gx','gy'}, use_global_device_ids=true, to_apply=%region_18.22 | all-reduce | flops 64 | bytes 512 | tf_op jit(solution)/shard_map/psum | solution.py:134
  (139 shorter events, 22.5 us)
Async XLA Ops:
  1.3 16.9 %collective-permute-start = (f32[1,8,128]{2,1,0:T(8,128)S(1)}, f32[1,8,128]{2,1,0:T(8,128)S(1)}, u32[]{:S(2)}, u32[]{:S(2)}) collective-permute-start(f32[1,8,128]{2,1,0:T(8,128)S(1)} %slice.759), channel_id=1, source_target_pairs={{4,0},{8,4},{12,8},{16,12},{20,16},{24,20},{28,24},{32,28},{36,32}... | collective-permute-start | bytes 12296 | tf_op jit(solution)/shard_map/ppermute | solution.py:18
  18.2 4.5 copy-start.1
  18.2 4.4 collective-permute-start.1
  22.7 0.8 copy-start
  23.6 5.0 %collective-permute-start.2 = (f32[8,1,8,128]{3,0,2,1:T(8,128)S(1)}, f32[8,1,8,128]{3,0,2,1:T(8,128)S(1)}, u32[]{:S(2)}, u32[]{:S(2)}) collective-permute-start(f32[8,1,8,128]{3,0,2,1:T(8,128)S(1)} %get-tuple-element.162), channel_id=1, source_target_pairs={{0,4},{4,8},{8,12},{12,16},{16,20},{20,24},{24,28},{28,32},{32,36}... | collective-permute-start | bytes 98312 | tf_op jit(solution)/shard_map/ppermute | solution.py:28
  25.5 5.2 %collective-permute-start.3 = (f32[8,1,8,128]{3,0,2,1:T(8,128)S(1)}, f32[8,1,8,128]{3,0,2,1:T(8,128)S(1)}, u32[]{:S(2)}, u32[]{:S(2)}) collective-permute-start(f32[8,1,8,128]{3,0,2,1:T(8,128)S(1)} %get-tuple-element.163), channel_id=1, source_target_pairs={{4,0},{8,4},{12,8},{16,12},{20,16},{24,20},{28,24},{32,28},{36,32}... | collective-permute-start | bytes 98312 | tf_op jit(solution)/shard_map/ppermute | solution.py:29
  30.7 3.0 collective-permute-start.4
  32.4 4.5 collective-permute-start.5
  39.0 5.4 %collective-permute-start.6 = (f32[8,1,8,128]{3,0,2,1:T(8,128)S(1)}, f32[8,1,8,128]{3,0,2,1:T(8,128)S(1)}, u32[]{:S(2)}, u32[]{:S(2)}) collective-permute-start(f32[8,1,8,128]{3,0,2,1:T(8,128)S(1)} %copy.53), channel_id=1, source_target_pairs={{0,4},{4,8},{8,12},{12,16},{16,20},{20,24},{24,28},{28,32},{32,36}... | collective-permute-start | bytes 98312 | tf_op jit(solution)/shard_map/ppermute | solution.py:28
  42.4 5.2 %collective-permute-start.7 = (f32[8,1,8,128]{3,0,2,1:T(8,128)S(1)}, f32[8,1,8,128]{3,0,2,1:T(8,128)S(1)}, u32[]{:S(2)}, u32[]{:S(2)}) collective-permute-start(f32[8,1,8,128]{3,0,2,1:T(8,128)S(1)} %copy.53), channel_id=1, source_target_pairs={{4,0},{8,4},{12,8},{16,12},{20,16},{24,20},{28,24},{32,28},{36,32}... | collective-permute-start | bytes 98312 | tf_op jit(solution)/shard_map/ppermute | solution.py:29
  47.6 3.0 collective-permute-start.8
  49.3 4.5 collective-permute-start.9
  55.9 5.4 %collective-permute-start.10 = (f32[8,1,8,128]{3,0,2,1:T(8,128)S(1)}, f32[8,1,8,128]{3,0,2,1:T(8,128)S(1)}, u32[]{:S(2)}, u32[]{:S(2)}) collective-permute-start(f32[8,1,8,128]{3,0,2,1:T(8,128)S(1)} %copy.57), channel_id=1, source_target_pairs={{0,4},{4,8},{8,12},{12,16},{16,20},{20,24},{24,28},{28,32},{32,36}... | collective-permute-start | bytes 98312 | tf_op jit(solution)/shard_map/ppermute | solution.py:28
  59.2 5.2 %collective-permute-start.11 = (f32[8,1,8,128]{3,0,2,1:T(8,128)S(1)}, f32[8,1,8,128]{3,0,2,1:T(8,128)S(1)}, u32[]{:S(2)}, u32[]{:S(2)}) collective-permute-start(f32[8,1,8,128]{3,0,2,1:T(8,128)S(1)} %copy.57), channel_id=1, source_target_pairs={{4,0},{8,4},{12,8},{16,12},{20,16},{24,20},{28,24},{32,28},{36,32}... | collective-permute-start | bytes 98312 | tf_op jit(solution)/shard_map/ppermute | solution.py:29
  64.5 3.0 collective-permute-start.12
  66.1 4.5 collective-permute-start.13
  72.8 5.3 %collective-permute-start.14 = (f32[8,1,8,128]{3,0,2,1:T(8,128)S(1)}, f32[8,1,8,128]{3,0,2,1:T(8,128)S(1)}, u32[]{:S(2)}, u32[]{:S(2)}) collective-permute-start(f32[8,1,8,128]{3,0,2,1:T(8,128)S(1)} %get-tuple-element.160), channel_id=1, source_target_pairs={{0,4},{4,8},{8,12},{12,16},{16,20},{20,24},{24,28},{28,32},{32,36}... | collective-permute-start | bytes 98312 | tf_op jit(solution)/shard_map/ppermute | solution.py:28
  76.2 5.2 %collective-permute-start.15 = (f32[8,1,8,128]{3,0,2,1:T(8,128)S(1)}, f32[8,1,8,128]{3,0,2,1:T(8,128)S(1)}, u32[]{:S(2)}, u32[]{:S(2)}) collective-permute-start(f32[8,1,8,128]{3,0,2,1:T(8,128)S(1)} %get-tuple-element.161), channel_id=1, source_target_pairs={{4,0},{8,4},{12,8},{16,12},{20,16},{24,20},{28,24},{32,28},{36,32}... | collective-permute-start | bytes 98312 | tf_op jit(solution)/shard_map/ppermute | solution.py:29
  81.4 2.9 collective-permute-start.16
  83.1 4.5 collective-permute-start.17
  88.7 5.3 %collective-permute-start.18 = (f32[8,1,8,128]{3,0,2,1:T(8,128)S(1)}, f32[8,1,8,128]{3,0,2,1:T(8,128)S(1)}, u32[]{:S(2)}, u32[]{:S(2)}) collective-permute-start(f32[8,1,8,128]{3,0,2,1:T(8,128)S(1)} %get-tuple-element.158), channel_id=1, source_target_pairs={{0,4},{4,8},{8,12},{12,16},{16,20},{20,24},{24,28},{28,32},{32,36}... | collective-permute-start | bytes 98312 | tf_op jit(solution)/shard_map/ppermute | solution.py:28
  92.0 5.2 %collective-permute-start.19 = (f32[8,1,8,128]{3,0,2,1:T(8,128)S(1)}, f32[8,1,8,128]{3,0,2,1:T(8,128)S(1)}, u32[]{:S(2)}, u32[]{:S(2)}) collective-permute-start(f32[8,1,8,128]{3,0,2,1:T(8,128)S(1)} %get-tuple-element.159), channel_id=1, source_target_pairs={{4,0},{8,4},{12,8},{16,12},{20,16},{24,20},{28,24},{32,28},{36,32}... | collective-permute-start | bytes 98312 | tf_op jit(solution)/shard_map/ppermute | solution.py:29
  97.3 3.1 collective-permute-start.20
  98.9 4.5 collective-permute-start.21
  254.1 4.3 collective-permute-start.22
  256.0 5.2 %collective-permute-start.23 = (f32[8,1,8,128]{3,0,2,1:T(8,128)S(1)}, f32[8,1,8,128]{3,0,2,1:T(8,128)S(1)}, u32[]{:S(2)}, u32[]{:S(2)}) collective-permute-start(f32[8,1,8,128]{3,0,2,1:T(8,128)S(1)} %get-tuple-element.157), channel_id=1, source_target_pairs={{4,0},{8,4},{12,8},{16,12},{20,16},{24,20},{28,24},{32,28},{36,32}... | collective-permute-start | bytes 98312 | tf_op jit(solution)/shard_map/ppermute | solution.py:29
  261.2 5.1 %collective-permute-start.24 = (f32[8,4,1,128]{3,0,2,1:T(8,128)S(1)}, f32[8,4,1,128]{3,0,2,1:T(8,128)S(1)}, u32[]{:S(2)}, u32[]{:S(2)}) collective-permute-start(f32[8,4,1,128]{3,0,2,1:T(8,128)S(1)} %get-tuple-element.142), channel_id=1, source_target_pairs={{0,1},{1,2},{2,3},{4,5},{5,6},{6,7},{8,9},{9,10},{10,11},{12,13},{... | collective-permute-start | bytes 49160 | tf_op jit(solution)/shard_map/ppermute | solution.py:28
  264.9 4.5 collective-permute-start.25
  271.5 5.4 %collective-permute-start.26 = (f32[8,1,8,128]{3,0,2,1:T(8,128)S(1)}, f32[8,1,8,128]{3,0,2,1:T(8,128)S(1)}, u32[]{:S(2)}, u32[]{:S(2)}) collective-permute-start(f32[8,1,8,128]{3,0,2,1:T(8,128)S(1)} %copy.72), channel_id=1, source_target_pairs={{0,4},{4,8},{8,12},{12,16},{16,20},{20,24},{24,28},{28,32},{32,36}... | collective-permute-start | bytes 98312 | tf_op jit(solution)/shard_map/ppermute | solution.py:28
  274.9 5.2 %collective-permute-start.27 = (f32[8,1,8,128]{3,0,2,1:T(8,128)S(1)}, f32[8,1,8,128]{3,0,2,1:T(8,128)S(1)}, u32[]{:S(2)}, u32[]{:S(2)}) collective-permute-start(f32[8,1,8,128]{3,0,2,1:T(8,128)S(1)} %copy.72), channel_id=1, source_target_pairs={{4,0},{8,4},{12,8},{16,12},{20,16},{24,20},{28,24},{32,28},{36,32}... | collective-permute-start | bytes 98312 | tf_op jit(solution)/shard_map/ppermute | solution.py:29
  280.1 3.0 collective-permute-start.28
  281.8 4.5 collective-permute-start.29
  288.4 5.4 %collective-permute-start.30 = (f32[8,1,8,128]{3,0,2,1:T(8,128)S(1)}, f32[8,1,8,128]{3,0,2,1:T(8,128)S(1)}, u32[]{:S(2)}, u32[]{:S(2)}) collective-permute-start(f32[8,1,8,128]{3,0,2,1:T(8,128)S(1)} %copy.76), channel_id=1, source_target_pairs={{0,4},{4,8},{8,12},{12,16},{16,20},{20,24},{24,28},{28,32},{32,36}... | collective-permute-start | bytes 98312 | tf_op jit(solution)/shard_map/ppermute | solution.py:28
  291.7 5.2 %collective-permute-start.31 = (f32[8,1,8,128]{3,0,2,1:T(8,128)S(1)}, f32[8,1,8,128]{3,0,2,1:T(8,128)S(1)}, u32[]{:S(2)}, u32[]{:S(2)}) collective-permute-start(f32[8,1,8,128]{3,0,2,1:T(8,128)S(1)} %copy.76), channel_id=1, source_target_pairs={{4,0},{8,4},{12,8},{16,12},{20,16},{24,20},{28,24},{32,28},{36,32}... | collective-permute-start | bytes 98312 | tf_op jit(solution)/shard_map/ppermute | solution.py:29
  297.0 4.3 collective-permute-start.32
  300.0 4.5 collective-permute-start.33
  306.7 5.3 %collective-permute-start.34 = (f32[8,1,8,128]{3,0,2,1:T(8,128)S(1)}, f32[8,1,8,128]{3,0,2,1:T(8,128)S(1)}, u32[]{:S(2)}, u32[]{:S(2)}) collective-permute-start(f32[8,1,8,128]{3,0,2,1:T(8,128)S(1)} %get-tuple-element.154), channel_id=1, source_target_pairs={{0,4},{4,8},{8,12},{12,16},{16,20},{20,24},{24,28},{28,32},{32,36}... | collective-permute-start | bytes 98312 | tf_op jit(solution)/shard_map/ppermute | solution.py:28
  310.0 5.2 %collective-permute-start.35 = (f32[8,1,8,128]{3,0,2,1:T(8,128)S(1)}, f32[8,1,8,128]{3,0,2,1:T(8,128)S(1)}, u32[]{:S(2)}, u32[]{:S(2)}) collective-permute-start(f32[8,1,8,128]{3,0,2,1:T(8,128)S(1)} %get-tuple-element.155), channel_id=1, source_target_pairs={{4,0},{8,4},{12,8},{16,12},{20,16},{24,20},{28,24},{32,28},{36,32}... | collective-permute-start | bytes 98312 | tf_op jit(solution)/shard_map/ppermute | solution.py:29
  315.3 4.4 collective-permute-start.36
  316.9 4.5 collective-permute-start.37
where the time goes:
time: 460 us; the launch traced here: 458 us
  blocking collectives  280 us (61%)
  starting transfers between devices  93.3 us (20%)
  waiting for transfers between devices  58 us (13%)
  other arithmetic  14.5 us (3%)
  local copies, waits for them, and re-layouts  8.8 us (2%)
    psum x1, blocking collectives, local(): lax.psum((inner_block(first_prec, applied), inner_block(first_prec, rhs))...  146 us
    psum x1, blocking collectives, local(): coupling = lax.psum(inner_block(applied, next_prec), ('gx', 'gy'))  135 us
    ppermute x18, waiting for transfers between devices, with_halo(): after = lax.ppermute(first, axis, down)  54.1 us
    ppermute x18, starting transfers between devices, with_halo(): before = lax.ppermute(last, axis, up)  45.4 us
    ppermute x18, starting transfers between devices, with_halo(): after = lax.ppermute(first, axis, down)  30.4 us
    ppermute x2, starting transfers between devices, passed_along(): return lax.ppermute(shard, axis, pairs)  17.5 us
  transfers between devices with their start and end apart: 38, of which 20 were waited for; matrix products, arithmetic and copies ran while one was open for 1% of the time, Pallas kernels for 0%

commit v1 on v0

v1 whole, which is shorter than its diff:
```python
import jax
import jax.numpy as jnp
from jax import lax
from jax.experimental import pallas as pl
from jax.experimental.pallas import tpu as pltpu
from jax.sharding import Mesh, PartitionSpec as P

SPRING = 8.0
OMEGA = 0.6
DAMP = 0.5
ROWS = 32
LANES = 128
FIELDS = 8
HIGHEST = lax.Precision.HIGHEST
PARAMS = pltpu.CompilerParams(vmem_limit_bytes=24 * 1024 * 1024)


def vmem(n):
    return [pl.BlockSpec(memory_space=pltpu.VMEM)] * n


def iota(axis, shape=(ROWS, LANES)):
    return lax.broadcasted_iota(jnp.int32, shape, axis)


def before_z(v):
    return jnp.where(iota(1) == 0, 0.0, pltpu.roll(v, 1, 1))


def after_z(v):
    return jnp.where(iota(1) == LANES - 1, 0.0, pltpu.roll(v, LANES - 1, 1))


def before_y(v):
    return jnp.where(iota(0) == 0, 0.0, pltpu.roll(v, 1, 0))


def after_y(v):
    return jnp.where(iota(0) == ROWS - 1, 0.0, pltpu.roll(v, ROWS - 1, 0))


def pair_sum(v):
    v = v + jnp.where(iota(0) % 2 == 0, pltpu.roll(v, ROWS - 1, 0), pltpu.roll(v, 1, 0))
    return v + jnp.where(iota(1) % 2 == 0, pltpu.roll(v, LANES - 1, 1), pltpu.roll(v, 1, 1))


def spread(u):
    low = before_z(u)
    out = []
    for f in (u + low, u - low):
        g = before_y(f)
        out += [f + g, f - g]
    return out


def element_plane(lower, upper, s):
    s16, s24, s48 = s * (1.0 / 16.0), s * (1.0 / 24.0), s * (1.0 / 48.0)
    ss, ds, sd, dd = [(b + a, b - a) for a, b in zip(lower, upper)]
    return (
        (None, s16 * ss[1]),
        (s16 * ds[0], s24 * ds[1]),
        (s16 * sd[0], s24 * sd[1]),
        (s24 * dd[0], s48 * dd[1]),
    )


def collect(here, following):
    n = []
    for (s0, d0), (s1, d1) in zip(here, following):
        n.append(d0 - d1 if s0 is None else (s0 + d0) + (s1 - d1))
    ss, ds, sd, dd = n
    ms = (ss + ds) + after_y(ss - ds)
    md = (sd + dd) + after_y(sd - dd)
    return (ms + md) + after_z(ms - md)


def hexes(u, s, least, most, same=lambda p: None):
    gathered, key = None, None
    lower = spread(u(least - 1))
    last, last_id = lower, same(least - 1)
    previous = None
    for e in range(least, most + 2):
        now_id = same(e)
        now = last if now_id is not None and now_id == last_id else spread(u(e))
        w = element_plane(last, now, s(e))
        if previous is not None:
            yield e - 1, collect(previous, w)
        previous, last, last_id = w, now, now_id


class Planes:
    def __init__(self, ref, first):
        self.ref, self.first = ref, first

    def __call__(self, p):
        return self.ref[p - self.first]

    def put(self, p, v):
        self.ref[p - self.first] = v


def from_blocks(refs, field):
    def get(p):
        ref, q = refs[p // 4 + 2], p % 4
        tiles = [ref[x * 2 + q // 2, field, q % 2] for x in range(4)]
        return jnp.concatenate(tiles, axis=0)

    return get


def setup(present, stiff, support, dv, steps):
    sums = None
    diagonal = {}
    for p in range(-7, 12):
        t = stiff(p)
        t = t + after_z(t)
        t = t + after_y(t)
        if sums is not None:
            d = SPRING * support(p - 1) + (sums + t) * (1.0 / 3.0)
            ok = present[(p - 1) // 4 + 2] != 0
            dv.put(p - 1, jnp.where(ok, OMEGA / d, 0.0))
            if (p - 1) % 2 and p - 1 > -7:
                steps.put((p - 1) // 2, jnp.where(ok, DAMP / pair_sum(kept + d), 0.0))
            kept = d
        sums = t


def precondition(source, stiff, support, dv, steps, z, res, c, c1, least, most, emit):
    for p in range(-7, 11):
        z.put(p, dv(p) * source(p))

    def rest(u, lo, hi, same=lambda p: None):
        for p, h in hexes(u, stiff, lo, hi, same):
            yield p, h + SPRING * support(p) * u(p)

    kept = None
    for p, a in rest(z, -6, 9):
        v = source(p) - a
        if p % 2:
            i = p // 2
            r = pair_sum(kept + v)
            res.put(i, r)
            c.put(i, steps(i) * r)
        kept = v

    def sweep(old, new, lo, hi):
        held = None
        for p, a in rest(lambda q: old(q // 2), 2 * lo, 2 * hi + 1, lambda q: q // 2):
            if p % 2:
                i = p // 2
                new.put(i, old(i) + steps(i) * (res(i) - pair_sum(held + a)))
            held = a

    sweep(c, c1, -2, 3)
    sweep(c1, c, -1, 2)
    for p in range(least - 1, most + 2):
        z.put(p, z(p) + c(p // 2))
    for p, a in rest(z, least, most):
        emit(p, z(p) + dv(p) * (source(p) - a))


def store_block(ref, field, q, v):
    for x in range(4):
        tile = v[8 * x : 8 * x + 8]
        if field is None:
            ref[x * 2 + q // 2, q % 2] = tile
        else:
            ref[x * 2 + q // 2, field, q % 2] = tile


def scratch():
    plane = lambda n: pltpu.VMEM((n, ROWS, LANES), jnp.float32)
    return [plane(18), plane(8), plane(18), plane(8), plane(8), plane(8), plane(6)]


def wrap_scratch(dv, steps, z, res, c, c1, out):
    return Planes(dv, -7), Planes(steps, -3), Planes(z, -7), Planes(res, -3), Planes(c, -3), Planes(c1, -3), Planes(out, -1)


def pack_kernel(rhs, classes, supports, out):
    density = (classes[...].astype(jnp.float32) + 1.0) / 4.0
    stiff = 0.001 + density * density * density
    support = supports[...].astype(jnp.float32)
    for j in range(FIELDS):
        out[j, 0] = rhs[j]
        out[j, 1] = stiff
        out[j, 2] = support


def first_kernel(present, m2, m1, own, p1, p2, first, applied, *work):
    refs = (m2, m1, own, p1, p2)
    source, stiff, support = (from_blocks(refs, f) for f in range(3))
    dv, steps, z, res, c, c1, out = wrap_scratch(*work)
    setup(present, stiff, support, dv, steps)

    def emit(p, v):
        out.put(p, v)
        if 0 <= p < 4:
            store_block(first, None, p, v)

    precondition(source, stiff, support, dv, steps, z, res, c, c1, -1, 4, emit)
    for p, h in hexes(out, stiff, 0, 3):
        store_block(applied, None, p, h + SPRING * support(p) * out(p))


def second_kernel(present, m2, m1, own, p1, p2, a_m2, a_m1, a_own, a_p1, a_p2, first, packed, *work):
    refs = (m2, m1, own, p1, p2)
    moved = (a_m2, a_m1, a_own, a_p1, a_p2)
    stiff, support = (from_blocks(refs, f) for f in (1, 2))

    def source(p):
        ref, q = moved[p // 4 + 2], p % 4
        return jnp.concatenate([ref[x * 2 + q // 2, q % 2] for x in range(4)], axis=0)

    dv, steps, z, res, c, c1, _ = wrap_scratch(*work)
    setup(present, stiff, support, dv, steps)
    for p in range(8):
        packed[p, 0] = first[p]
        packed[p, 1] = a_own[p]
    emit = lambda p, v: store_block(packed, 2, p, v)
    precondition(source, stiff, support, dv, steps, z, res, c, c1, 0, 3, emit)


def rows_of(ref, field, fields):
    return jnp.concatenate(
        [ref[pl.ds(field * 16 + t, FIELDS, stride=fields * 16), :] for t in range(16)], axis=1
    )


def gram_kernel(parts, rhs, out):
    f, a, n = (rows_of(parts, k, 3) for k in range(3))
    r = rows_of(rhs, 0, 1)
    left = jnp.concatenate([f, a], axis=0)
    right = jnp.concatenate([a, r, n, f, jnp.zeros((LANES - 32, 2048), jnp.float32)], axis=0)
    g = lax.dot_general(left, right, (((1,), (1,)), ((), ())), precision=HIGHEST, preferred_element_type=jnp.float32)
    tile = jnp.where(iota(1, (8, LANES)) < 16, g[:8], g[8:])
    for k in range(out.shape[0]):
        out[k] = tile


def final_kernel(sums, parts, rhs, sol, resid, direction):
    w = sums[0]
    for k in range(1, sums.shape[0]):
        w = w + sums[k]
    shape = (8, LANES)
    lane, row = iota(1, shape), iota(0, shape)
    w = jnp.where(lane < 8, 0.5 * (w + pltpu.roll(w, LANES - 24, 1)), w)
    for k in range(8):
        pivot = w[k : k + 1, :] / w[k : k + 1, k : k + 1]
        w = jnp.where(row == k, pivot, w - w[:, k : k + 1] * pivot)
    coef = jnp.where((lane >= 8) & (lane < 16), w, 0.0)
    turn = -pltpu.roll(w, LANES - 16, 1)
    for k in range(8):
        turn = turn + w[:, 16 + k : 17 + k] * coef[k : k + 1, :]
    turn = jnp.where((lane >= 8) & (lane < 16), turn, 0.0)
    weights = jnp.concatenate(
        [pltpu.roll(coef, LANES - 8, 1) + pltpu.roll(turn, 8, 1), -coef, -pltpu.roll(coef, 8, 1)], axis=0
    )
    f, a, n = (rows_of(parts, k, 3) for k in range(3))
    fields = jnp.concatenate([f, a, n], axis=0)
    new = lax.dot_general(weights, fields, (((0,), (0,)), ((), ())), precision=HIGHEST, preferred_element_type=jnp.float32)
    r = rows_of(rhs, 0, 1)
    for ref, v in ((sol, new[:8]), (resid, r + new[8:16]), (direction, f + new[16:24])):
        for t in range(16):
            ref[pl.ds(t, FIELDS, stride=16), :] = v[:, LANES * t : LANES * t + LANES]


def f32(*shape):
    return jax.ShapeDtypeStruct(shape, jnp.float32)


def shared_sum(tile, axis):
    return lax.all_to_all(tile, axis, 0, 0)


def local(rhs, classes, supports):
    sizes = {a: lax.axis_size(a) for a in ("z", "y", "c", "x")}
    chips = sizes["z"] * sizes["y"]
    chip = lax.axis_index("z") * sizes["y"] + lax.axis_index("y")
    place = chip + jnp.arange(-2, 3, dtype=jnp.int32)
    present = ((place >= 0) & (place < chips)).astype(jnp.int32)
    smem = [pl.BlockSpec(memory_space=pltpu.SMEM)]

    packed = pl.pallas_call(
        pack_kernel, out_shape=f32(8, 3, 2, 8, LANES), in_specs=vmem(3), out_specs=vmem(1)[0], compiler_params=PARAMS
    )(rhs, classes, supports)
    own = lax.all_to_all(packed, ("x", "c"), 0, 0)

    def around(v):
        def moved(by):
            pairs = [(i, i + by) for i in range(chips) if 0 <= i + by < chips]
            return lax.ppermute(v, ("z", "y"), pairs)

        m1, p1, m2, p2 = moved(1), moved(-1), moved(2), moved(-2)
        return m2, m1, v, p1, p2

    grids = around(own)
    first, applied = pl.pallas_call(
        first_kernel,
        out_shape=(f32(8, 2, 8, LANES), f32(8, 2, 8, LANES)),
        in_specs=smem + vmem(5),
        out_specs=tuple(vmem(2)),
        scratch_shapes=scratch(),
        compiler_params=PARAMS,
    )(present, *grids)
    results = pl.pallas_call(
        second_kernel,
        out_shape=f32(8, 3, 2, 8, LANES),
        in_specs=smem + vmem(11),
        out_specs=vmem(1)[0],
        scratch_shapes=scratch(),
        compiler_params=PARAMS,
    )(present, *grids, *around(applied), first)
    parts = lax.all_to_all(results, ("x", "c"), 0, 0).reshape(8 * 48, LANES)
    rows = rhs.reshape(8 * 16, LANES)

    tile = pl.pallas_call(
        gram_kernel, out_shape=f32(sizes["x"], 8, LANES), in_specs=vmem(2), out_specs=vmem(1)[0], compiler_params=PARAMS
    )(parts, rows)
    tile = shared_sum(tile, "x").sum(0)
    tile = jnp.broadcast_to(tile, (sizes["y"] * sizes["c"], 8, LANES))
    tile = shared_sum(tile, ("y", "c")).sum(0)
    tile = jnp.broadcast_to(tile, (sizes["z"], 8, LANES))
    tile = shared_sum(tile, "z")
    outs = pl.pallas_call(
        final_kernel,
        out_shape=(f32(128, LANES),) * 3,
        in_specs=vmem(3),
        out_specs=tuple(vmem(3)),
        compiler_params=PARAMS,
    )(tile, parts, rows)
    return tuple(v.reshape(8, 2, 8, LANES) for v in outs)


def solution(mesh):
    gx, gy = mesh.shape["gx"], mesh.shape["gy"]
    y = min(8, gx // 2)
    fine = Mesh(mesh.devices.reshape(gx // (2 * y), y, 2, gy), ("z", "y", "c", "x"))
    grid = P(("z", "y", "c"), "x", None)
    fields = P(None, ("z", "y", "c"), "x", None)
    return jax.shard_map(
        local, mesh=fine, in_specs=(fields, grid, grid), out_specs=(fields,) * 3, check_vma=False
    )
```

time: 460 us -> 130 us (0.28)
  blocking collectives: 280 us -> 85.2 us
  starting transfers between devices: 93.3 us -> 28.6 us
  waiting for transfers between devices: 58 us -> 3.89 us
  other arithmetic: 14.5 us -> 0.03 us
  Pallas kernels: 0 us -> 9.04 us
  local copies, waits for them, and re-layouts: 8.8 us -> 2.25 us
    psum x2 -> x0, blocking collectives: 280 us -> none  [the longest x1 146 us: local(): lax.psum((inner_block(first_prec, applied), inner_block(first_prec, rhs))...]
    all_to_all x0 -> x5, blocking collectives: none -> 85.2 us  [the longest x3 51.7 us: shared_sum(): return lax.all_to_all(tile, axis, 0, 0)]
    ppermute x38 -> x8, starting transfers between devices: 93.3 us -> 28.6 us  [moved(): return lax.ppermute(v, ('z', 'y'), pairs)]
    ppermute x38 -> x8, waiting for transfers between devices: 58 us -> 3.89 us  [moved(): return lax.ppermute(v, ('z', 'y'), pairs)]
    pallas_call x0 -> x5, Pallas kernels: none -> 9.04 us  [the longest x1 3.14 us: local(): pl.pallas_call(first_kernel, out_shape=(f32(8, 2, 8, LANES), f32(8, 2, 8,...]
    reduce_sum x13 -> x2, other arithmetic: 5 us -> 0.02 us  [the longest x1 0.02 us: local(): tile = shared_sum(tile, ('y', 'c')).sum(0)]
  transfers between devices with their start and end apart: 38 -> 8, of which waited for: 20 -> 3; matrix products, arithmetic and copies ran while one was open for 1% -> 0% of each run, Pallas kernels for 0% -> 0%
where the time goes in v1:
time: 130 us
  blocking collectives  85.2 us (66%)
  starting transfers between devices  28.6 us (22%)
  Pallas kernels  9.04 us (7%)
  waiting for transfers between devices  3.89 us (3%)
  local copies, waits for them, and re-layouts  2.25 us (2%)
    all_to_all x3, blocking collectives, shared_sum(): return lax.all_to_all(tile, axis, 0, 0)  51.7 us
    ppermute x8, starting transfers between devices, moved(): return lax.ppermute(v, ('z', 'y'), pairs)  28.6 us
    all_to_all x1, blocking collectives, local(): own = lax.all_to_all(packed, ('x', 'c'), 0, 0)  22.4 us
    all_to_all x1, blocking collectives, local(): parts = lax.all_to_all(results, ('x', 'c'), 0, 0).reshape(8 * 48, LANES)  11.1 us
    ppermute x8, waiting for transfers between devices, moved(): return lax.ppermute(v, ('z', 'y'), pairs)  3.89 us
    pallas_call x1, Pallas kernels, local(): pl.pallas_call(first_kernel, out_shape=(f32(8, 2, 8, LANES), f32(8, 2, 8,...  3.14 us
    pallas_call x1, Pallas kernels, local(): pl.pallas_call(second_kernel, out_shape=f32(8, 3, 2, 8, LANES), in_specs=...  3 us
  transfers between devices with their start and end apart: 8, of which 3 were waited for; matrix products, arithmetic and copies ran while one was open for 0% of the time, Pallas kernels for 0%

profile of v1, /device:TPU:1, one launch (start us, length us, event | category | flops | bytes accessed | tf_op | source)
XLA Modules:
  0.0 129.8 jit_solution(9401429326392875031)
XLA Ops:
  0.6 0.0 copy-start
  0.6 0.8 copy-done
  1.5 0.0 copy-start.2
  1.5 0.7 copy-done.2
  2.2 0.0 copy-start.3
  2.2 0.7 copy-done.3
  2.9 22.4 %all_to_all.25.own = f32[8,3,2,8,128]{4,3,2,1,0:T(8,128)S(1)} all-to-all(f32[8,3,2,8,128]{4,3,2,1,0:T(8,128)S(1)} %shard_map.58), channel_id=1, replica_groups=mesh['z'=16,'y'=8,'c'=2,'x'=4] {'x','c'}, dimensions={0} | all-to-all | bytes 393216 | tf_op jit(solution)/shard_map/all_to_all | solution.py:287
  25.3 1.3 collective-permute-start.3
  26.6 1.3 collective-permute-start.2
  27.9 4.0 %collective-permute-start.1 = (f32[8,3,2,8,128]{4,3,2,1,0:T(8,128)S(1)}, f32[8,3,2,8,128]{4,3,2,1,0:T(8,128)S(1)}, u32[]{:S(2)}, u32[]{:S(2)}) collective-permute-start(f32[8,3,2,8,128]{4,3,2,1,0:T(8,128)S(1)} %all_to_all.25.own), channel_id=1, source_target_pairs={{0,8},{8,16},{16,24},{24,32},{32,40},{40,48},{48,56},{56,64},{64,7... | collective-permute-start | bytes 589832 | tf_op jit(solution)/shard_map/ppermute | solution.py:292
  31.9 4.9 %collective-permute-start = (f32[8,3,2,8,128]{4,3,2,1,0:T(8,128)S(1)}, f32[8,3,2,8,128]{4,3,2,1,0:T(8,128)S(1)}, u32[]{:S(2)}, u32[]{:S(2)}) collective-permute-start(f32[8,3,2,8,128]{4,3,2,1,0:T(8,128)S(1)} %all_to_all.25.own), channel_id=1, source_target_pairs={{0,16},{8,24},{16,32},{24,40},{32,48},{40,56},{48,64},{56,72},{64,... | collective-permute-start | bytes 589832 | tf_op jit(solution)/shard_map/ppermute | solution.py:292
  36.8 0.0 collective-permute-done.3.p2
  36.8 2.3 %collective-permute-done.2.p1 = f32[8,3,2,8,128]{4,3,2,1,0:T(8,128)S(1)} collective-permute-done((f32[8,3,2,8,128]{4,3,2,1,0:T(8,128)S(1)}, f32[8,3,2,8,128]{4,3,2,1,0:T(8,128)S(1)}, u32[]{:S(2)}, u32[]{:S(2)}) %collective-permute-start.2) | collective-permute-done | bytes 196640 | tf_op jit(solution)/shard_map/ppermute | solution.py:292
  39.1 0.0 collective-permute-done.1.m1
  39.1 0.3 collective-permute-done.m2
  39.4 3.1 %shard_map.59 = (f32[8,2,8,128]{3,2,1,0:T(8,128)S(1)}, f32[8,2,8,128]{3,2,1,0:T(8,128)S(1)}) custom-call(s32[5]{0:T(128)S(1)} %and_convert_fusion.present, f32[8,3,2,8,128]{4,3,2,1,0:T(8,128)S(1)} %collective-permute-done.m2, f32[8,3,2,8,128]{4,3,2,1,0:T(8,128)S(1)} %collective-permute-done.1.m1, f32[8,3,2,8,128]{4,3,2,1,0:T(8,128)S(1)} %all_to_all.25.own, ...), custom_call_target="tpu_custom_call" | custom-call | tf_op jit(solution)/shard_map/pallas_call | solution.py:298
  42.6 1.3 collective-permute-start.7
  43.9 1.3 collective-permute-start.6
  45.2 8.9 %collective-permute-start.5 = (f32[8,2,8,128]{3,2,1,0:T(8,128)S(1)}, f32[8,2,8,128]{3,2,1,0:T(8,128)S(1)}, u32[]{:S(2)}, u32[]{:S(2)}) collective-permute-start(f32[8,2,8,128]{3,2,1,0:T(8,128)S(1)} %get-tuple-element.8.a_own), channel_id=1, source_target_pairs={{0,8},{8,16},{16,24},{24,32},{32,40},{40,48},{48,56},{56,64},{64,7... | collective-permute-start | bytes 196616 | tf_op jit(solution)/shard_map/ppermute | solution.py:292
  54.1 5.6 %collective-permute-start.4 = (f32[8,2,8,128]{3,2,1,0:T(8,128)S(1)}, f32[8,2,8,128]{3,2,1,0:T(8,128)S(1)}, u32[]{:S(2)}, u32[]{:S(2)}) collective-permute-start(f32[8,2,8,128]{3,2,1,0:T(8,128)S(1)} %get-tuple-element.8.a_own), channel_id=1, source_target_pairs={{0,16},{8,24},{16,32},{24,40},{32,48},{40,56},{48,64},{56,72},{64,... | collective-permute-start | bytes 196616 | tf_op jit(solution)/shard_map/ppermute | solution.py:292
  59.8 0.0 collective-permute-done.7.a_p2
  59.8 0.0 collective-permute-done.6.a_p1
  59.8 0.0 collective-permute-done.5.a_m1
  59.8 1.3 collective-permute-done.4.a_m2
  61.1 3.0 %shard_map.60 = f32[8,3,2,8,128]{4,3,2,1,0:T(8,128)S(1)} custom-call(s32[5]{0:T(128)S(1)} %and_convert_fusion.present, f32[8,3,2,8,128]{4,3,2,1,0:T(8,128)S(1)} %collective-permute-done.m2, f32[8,3,2,8,128]{4,3,2,1,0:T(8,128)S(1)} %collective-permute-done.1.m1, f32[8,3,2,8,128]{4,3,2,1,0:T(8,128)S(1)} %all_to_all.25.own, ...), custom_call_target="tpu_custom_call" | custom-call | tf_op jit(solution)/shard_map/pallas_call | solution.py:306
  64.1 0.0 copy-start.1
  64.1 11.1 %all_to_all.26 = f32[8,3,2,8,128]{4,3,2,1,0:T(8,128)S(1)} all-to-all(f32[8,3,2,8,128]{4,3,2,1,0:T(8,128)S(1)} %shard_map.60), channel_id=1, replica_groups=mesh['z'=16,'y'=8,'c'=2,'x'=4] {'x','c'}, dimensions={0} | all-to-all | bytes 393216 | tf_op jit(solution)/shard_map/all_to_all | solution.py:314
  75.2 0.0 copy-done.1
  75.2 0.3 shard_map.61
  75.5 6.6 %all_to_all.27 = f32[4,8,128]{2,1,0:T(8,128)S(1)} all-to-all(f32[4,8,128]{2,1,0:T(8,128)S(1)} %shard_map.61), channel_id=1, replica_groups=mesh['z'=16,'y'=8,'c'=2,'x'=4] {'x'}, dimensions={0} | all-to-all | bytes 32768 | tf_op jit(solution)/shard_map/all_to_all | solution.py:273
  82.1 20.2 %all_to_all.28 = f32[16,8,128]{2,1,0:T(8,128)S(1)} all-to-all(f32[16,8,128]{2,1,0:T(8,128)S(1)} %broadcast_in_dim.6), channel_id=1, replica_groups=mesh['z'=16,'y'=8,'c'=2,'x'=4] {'y','c'}, dimensions={0} | all-to-all | bytes 131072 | tf_op jit(solution)/shard_map/all_to_all | solution.py:273
  102.3 24.9 %all_to_all.29.sums = f32[16,8,128]{2,1,0:T(8,128)S(1)} all-to-all(f32[16,8,128]{2,1,0:T(8,128)S(1)} %broadcast_in_dim.7), channel_id=1, replica_groups=mesh['z'=16,'y'=8,'c'=2,'x'=4] {'z'}, dimensions={0} | all-to-all | bytes 131072 | tf_op jit(solution)/shard_map/all_to_all | solution.py:273
  127.2 2.5 %shard_map.62 = (f32[128,128]{1,0:T(8,128)}, f32[128,128]{1,0:T(8,128)}, f32[128,128]{1,0:T(8,128)}) custom-call(f32[16,8,128]{2,1,0:T(8,128)S(1)} %all_to_all.29.sums, f32[384,128]{1,0:T(8,128)S(1)} %bitcast.6, f32[128,128]{1,0:T(8,128)S(1)} %bitcast.8), custom_call_target="tpu_custom_call" | custom-call | tf_op jit(solution)/shard_map/pallas_call | solution.py:325
  (6 shorter events, 0.1 us)
Async XLA Ops:
  0.6 0.8 copy-start
  1.5 0.7 copy-start.2
  2.2 0.7 copy-start.3
  25.3 11.5 %collective-permute-start.3 = (f32[8,3,2,8,128]{4,3,2,1,0:T(8,128)S(1)}, f32[8,3,2,8,128]{4,3,2,1,0:T(8,128)S(1)}, u32[]{:S(2)}, u32[]{:S(2)}) collective-permute-start(f32[8,3,2,8,128]{4,3,2,1,0:T(8,128)S(1)} %all_to_all.25.own), channel_id=1, source_target_pairs={{16,0},{24,8},{32,16},{40,24},{48,32},{56,40},{64,48},{72,56},{80,... | collective-permute-start | bytes 589832 | tf_op jit(solution)/shard_map/ppermute | solution.py:292
  26.6 12.5 %collective-permute-start.2 = (f32[8,3,2,8,128]{4,3,2,1,0:T(8,128)S(1)}, f32[8,3,2,8,128]{4,3,2,1,0:T(8,128)S(1)}, u32[]{:S(2)}, u32[]{:S(2)}) collective-permute-start(f32[8,3,2,8,128]{4,3,2,1,0:T(8,128)S(1)} %all_to_all.25.own), channel_id=1, source_target_pairs={{8,0},{16,8},{24,16},{32,24},{40,32},{48,40},{56,48},{64,56},{72,6... | collective-permute-start | bytes 589832 | tf_op jit(solution)/shard_map/ppermute | solution.py:292
  27.9 11.2 %collective-permute-start.1 = (f32[8,3,2,8,128]{4,3,2,1,0:T(8,128)S(1)}, f32[8,3,2,8,128]{4,3,2,1,0:T(8,128)S(1)}, u32[]{:S(2)}, u32[]{:S(2)}) collective-permute-start(f32[8,3,2,8,128]{4,3,2,1,0:T(8,128)S(1)} %all_to_all.25.own), channel_id=1, source_target_pairs={{0,8},{8,16},{16,24},{24,32},{32,40},{40,48},{48,56},{56,64},{64,7... | collective-permute-start | bytes 589832 | tf_op jit(solution)/shard_map/ppermute | solution.py:292
  31.9 7.5 %collective-permute-start = (f32[8,3,2,8,128]{4,3,2,1,0:T(8,128)S(1)}, f32[8,3,2,8,128]{4,3,2,1,0:T(8,128)S(1)}, u32[]{:S(2)}, u32[]{:S(2)}) collective-permute-start(f32[8,3,2,8,128]{4,3,2,1,0:T(8,128)S(1)} %all_to_all.25.own), channel_id=1, source_target_pairs={{0,16},{8,24},{16,32},{24,40},{32,48},{40,56},{48,64},{56,72},{64,... | collective-permute-start | bytes 589832 | tf_op jit(solution)/shard_map/ppermute | solution.py:292
  42.6 17.2 %collective-permute-start.7 = (f32[8,2,8,128]{3,2,1,0:T(8,128)S(1)}, f32[8,2,8,128]{3,2,1,0:T(8,128)S(1)}, u32[]{:S(2)}, u32[]{:S(2)}) collective-permute-start(f32[8,2,8,128]{3,2,1,0:T(8,128)S(1)} %get-tuple-element.8.a_own), channel_id=1, source_target_pairs={{16,0},{24,8},{32,16},{40,24},{48,32},{56,40},{64,48},{72,56},{80,... | collective-permute-start | bytes 196616 | tf_op jit(solution)/shard_map/ppermute | solution.py:292
  43.9 15.9 %collective-permute-start.6 = (f32[8,2,8,128]{3,2,1,0:T(8,128)S(1)}, f32[8,2,8,128]{3,2,1,0:T(8,128)S(1)}, u32[]{:S(2)}, u32[]{:S(2)}) collective-permute-start(f32[8,2,8,128]{3,2,1,0:T(8,128)S(1)} %get-tuple-element.8.a_own), channel_id=1, source_target_pairs={{8,0},{16,8},{24,16},{32,24},{40,32},{48,40},{56,48},{64,56},{72,6... | collective-permute-start | bytes 196616 | tf_op jit(solution)/shard_map/ppermute | solution.py:292
  45.2 14.6 %collective-permute-start.5 = (f32[8,2,8,128]{3,2,1,0:T(8,128)S(1)}, f32[8,2,8,128]{3,2,1,0:T(8,128)S(1)}, u32[]{:S(2)}, u32[]{:S(2)}) collective-permute-start(f32[8,2,8,128]{3,2,1,0:T(8,128)S(1)} %get-tuple-element.8.a_own), channel_id=1, source_target_pairs={{0,8},{8,16},{16,24},{24,32},{32,40},{40,48},{48,56},{56,64},{64,7... | collective-permute-start | bytes 196616 | tf_op jit(solution)/shard_map/ppermute | solution.py:292
  54.1 7.0 %collective-permute-start.4 = (f32[8,2,8,128]{3,2,1,0:T(8,128)S(1)}, f32[8,2,8,128]{3,2,1,0:T(8,128)S(1)}, u32[]{:S(2)}, u32[]{:S(2)}) collective-permute-start(f32[8,2,8,128]{3,2,1,0:T(8,128)S(1)} %get-tuple-element.8.a_own), channel_id=1, source_target_pairs={{0,16},{8,24},{16,32},{24,40},{32,48},{40,56},{48,64},{56,72},{64,... | collective-permute-start | bytes 196616 | tf_op jit(solution)/shard_map/ppermute | solution.py:292
  64.1 11.1 %copy-start.1 = (f32[8,2,8,128]{3,2,1,0:T(8,128)S(1)}, f32[8,2,8,128]{3,2,1,0:T(8,128)}, u32[]{:S(2)}) copy-start(f32[8,2,8,128]{3,2,1,0:T(8,128)} %rhs.1) | copy-start | bytes 196612

commit v2 on v1

v2 whole, which is shorter than its diff:
```python
import jax
import jax.numpy as jnp
from jax import lax
from jax.experimental import pallas as pl
from jax.experimental.pallas import tpu as pltpu
from jax.sharding import Mesh, PartitionSpec as P

SPRING = 8.0
OMEGA = 0.6
DAMP = 0.5
LANES = 128
FIELDS = 8
TILE = (4, 8, LANES)
HIGHEST = lax.Precision.HIGHEST
PARAMS = pltpu.CompilerParams(vmem_limit_bytes=24 * 1024 * 1024)


def vmem(n):
    return [pl.BlockSpec(memory_space=pltpu.VMEM)] * n


def smem():
    return [pl.BlockSpec(memory_space=pltpu.SMEM)]


def iota(axis, shape=TILE):
    return lax.broadcasted_iota(jnp.int32, shape, axis)


def before_z(v):
    return jnp.where(iota(2) == 0, 0.0, pltpu.roll(v, 1, 2))


def after_z(v):
    return jnp.where(iota(2) == LANES - 1, 0.0, pltpu.roll(v, LANES - 1, 2))


def before_y(v):
    r = pltpu.roll(v, 1, 1)
    return jnp.where(iota(1) == 0, jnp.concatenate([jnp.zeros_like(r[:1]), r[:3]], axis=0), r)


def after_y(v):
    r = pltpu.roll(v, 7, 1)
    return jnp.where(iota(1) == 7, jnp.concatenate([r[1:], jnp.zeros_like(r[:1])], axis=0), r)


def pair_sum(v):
    v = v + jnp.where(iota(1) % 2 == 0, pltpu.roll(v, 7, 1), pltpu.roll(v, 1, 1))
    return v + jnp.where(iota(2) % 2 == 0, pltpu.roll(v, LANES - 1, 2), pltpu.roll(v, 1, 2))


def spread(u):
    low = before_z(u)
    out = []
    for f in (u + low, u - low):
        g = before_y(f)
        out += [f + g, f - g]
    return out


def element_plane(lower, upper, s16):
    s24, s48 = s16 * (2.0 / 3.0), s16 * (1.0 / 3.0)
    ss, ds, sd, dd = [(b + a, b - a) for a, b in zip(lower, upper)]
    w = ((s16 * ds[0], s24 * ds[1]), (s16 * sd[0], s24 * sd[1]), (s24 * dd[0], s48 * dd[1]))
    v = s16 * ss[1]
    return [-v] + [a - b for a, b in w], [v] + [a + b for a, b in w]


def gather(n):
    ss, ds, sd, dd = n
    ms = (ss + ds) + after_y(ss - ds)
    md = (sd + dd) + after_y(sd - dd)
    return (ms + md) + after_z(ms - md)


def apply_fine(u, s16, sp8, least, most):
    last, above = spread(u(least - 1)), None
    for e in range(least, most + 2):
        now = spread(u(e))
        to_lower, to_upper = element_plane(last, now, s16(e))
        if above is not None:
            yield e - 1, gather([a + b for a, b in zip(above, to_lower)]) + sp8(e - 1) * u(e - 1)
        last, above = now, to_upper


def apply_coarse(c, s16, sp8, least, most):
    last, above = spread(c(least - 1)), None
    for i in range(least, most + 2):
        now = spread(c(i))
        to_lower, to_upper = element_plane(last, now, s16(2 * i))
        if above is not None:
            inner = s16(2 * i - 1) * 4.0
            part = [inner * last[1], inner * last[2], (inner * (2.0 / 3.0)) * last[3]]
            n = [a + b for a, b in zip(above, to_lower)]
            n = [n[0]] + [a + b for a, b in zip(n[1:], part)]
            yield i - 1, pair_sum(gather(n) + (sp8(2 * i - 2) + sp8(2 * i - 1)) * c(i - 1))
        last, above = now, to_upper


class Planes:
    def __init__(self, ref, first, offset=None):
        self.ref, self.first, self.offset = ref, first, offset

    def at(self, p):
        return p - self.first if self.offset is None else p - self.first + self.offset

    def __call__(self, p):
        return self.ref[self.at(p)]

    def put(self, p, v):
        self.ref[self.at(p)] = v


def precondition(source, s16, sp8, dv, steps, work, least, most, emit):
    z, res, c, c1 = work
    lo, hi = (least - 1) // 2, (most + 1) // 2
    for p in range(2 * lo - 5, 2 * hi + 7):
        z.put(p, dv(p) * source(p))
    kept = None
    for p, a in apply_fine(z, s16, sp8, 2 * lo - 4, 2 * hi + 5):
        v = source(p) - a
        if p % 2:
            i = p // 2
            r = pair_sum(kept + v)
            res.put(i, r)
            c.put(i, steps(i) * r)
        kept = v
    for old, new, first, last in ((c, c1, lo - 1, hi + 1), (c1, c, lo, hi)):
        for i, a in apply_coarse(old, s16, sp8, first, last):
            new.put(i, old(i) + steps(i) * (res(i) - a))
    for p in range(least - 1, most + 2):
        z.put(p, z(p) + c(p // 2))
    for p, a in apply_fine(z, s16, sp8, least, most):
        emit(p, z(p) + dv(p) * (source(p) - a))


def work_shapes():
    plane = lambda n: pltpu.VMEM((n, *TILE), jnp.float32)
    return [plane(24), plane(12), plane(12), plane(12)]


def work_of(z, res, c, c1):
    return Planes(z, -8), Planes(res, -4), Planes(c, -4), Planes(c1, -4)


def pack_kernel(rhs, classes, supports, out, r, k, s, sems):
    copies = [pltpu.make_async_copy(a, b, sems.at[i]) for i, (a, b) in enumerate(((classes, k), (supports, s), (rhs, r)))]
    for copy in copies:
        copy.start()
    copies[0].wait()
    density = (k[...].astype(jnp.float32) + 1.0) / 4.0
    stiff = 0.001 + density * density * density
    for j in range(16):
        out[j, 1] = stiff
    copies[1].wait()
    support = s[...].astype(jnp.float32)
    for j in range(16):
        out[j, 2] = support
    copies[2].wait()
    for x in range(4):
        for c in range(2):
            v = r[x * 2 + c]
            for h in range(2):
                out[(x * 2 + h) * 2 + c, 0] = v


def first_kernel(where, own, swap, far, first, applied, s16_out, sp8_out, dv_out, steps_out, out, source_ref, *work):
    upper_chip = where[0] != 0

    def block(ref, field, q):
        h, c = q // 4, (q // 2) % 2
        return jnp.stack([ref[(x * 2 + h) * 2 + c, field, q % 2] for x in range(4)])

    def plane(field, p):
        q = p % 8
        if 0 <= p < 8:
            return block(own, field, q)
        a, b = block(swap, field, q), block(far, field, q)
        return jnp.where(upper_chip, b, a) if p < 0 else jnp.where(upper_chip, a, b)

    source, s16, sp8, dv = (Planes(r, -8) for r in (source_ref, s16_out, sp8_out, dv_out))
    steps, fields = Planes(steps_out, -4), Planes(out, -1)
    for p in range(-7, 15):
        source.put(p, plane(0, p))
        sp8.put(p, SPRING * plane(2, p))
    sums = kept = None
    for p in range(-7, 16):
        t = plane(1, p)
        s16.put(p, t * (1.0 / 16.0))
        t = t + after_z(t)
        t = t + after_y(t)
        if sums is not None:
            n = p - 1
            d = sp8(n) + (sums + t) * (1.0 / 3.0)
            ok = where[1 + (n + 8) // 8] != 0
            dv.put(n, jnp.where(ok, OMEGA / d, 0.0))
            if n % 2 and n > -7:
                steps.put(n // 2, jnp.where(ok, DAMP / pair_sum(kept + d), 0.0))
            kept = d
        sums = t

    def emit(p, v):
        fields.put(p, v)
        if 0 <= p < 8:
            first[p] = v

    precondition(source, s16, sp8, dv, steps, work_of(*work), -1, 8, emit)
    for p, v in apply_fine(fields, s16, sp8, 0, 7):
        applied[p] = v


def second_kernel(where, first, applied, below, above, s16_ref, sp8_ref, dv_ref, steps_ref, packed, source_ref, *work):
    shift = where[0] * 4
    for q in range(8):
        source_ref[q] = below[q]
        source_ref[8 + q] = applied[q]
        source_ref[16 + q] = above[q]
    source, s16, sp8, dv = (Planes(r, -8, shift) for r in (source_ref, s16_ref, sp8_ref, dv_ref))
    steps = Planes(steps_ref, -4, where[0] * 2)

    def put(field, p, v):
        for x in range(4):
            packed[x * 2 + p // 2, field, p % 2] = v[x]

    for p in range(4):
        put(0, p, first[shift + p])
        put(1, p, applied[shift + p])
    precondition(source, s16, sp8, dv, steps, work_of(*work), 0, 3, lambda p, v: put(2, p, v))


def rows_of(ref, field, fields):
    return jnp.concatenate(
        [ref[pl.ds(field * 16 + t, FIELDS, stride=fields * 16), :] for t in range(16)], axis=1
    )


def gram_kernel(parts, rhs, out):
    f, a, n = (rows_of(parts, k, 3) for k in range(3))
    r = rows_of(rhs, 0, 1)
    left = jnp.concatenate([f, a], axis=0)
    right = jnp.concatenate([a, r, n, f, jnp.zeros((LANES - 32, 2048), jnp.float32)], axis=0)
    g = lax.dot_general(left, right, (((1,), (1,)), ((), ())), precision=HIGHEST, preferred_element_type=jnp.float32)
    tile = jnp.where(iota(1, (8, LANES)) < 16, g[:8], g[8:])
    for k in range(out.shape[0]):
        out[k] = tile


def final_kernel(sums, parts, rhs, sol, resid, direction):
    w = sums[0]
    for k in range(1, sums.shape[0]):
        w = w + sums[k]
    shape = (8, LANES)
    lane, row = iota(1, shape), iota(0, shape)
    w = jnp.where(lane < 8, 0.5 * (w + pltpu.roll(w, LANES - 24, 1)), w)
    for k in range(8):
        pivot = w[k : k + 1, :] / w[k : k + 1, k : k + 1]
        w = jnp.where(row == k, pivot, w - w[:, k : k + 1] * pivot)
    coef = jnp.where((lane >= 8) & (lane < 16), w, 0.0)
    turn = -pltpu.roll(w, LANES - 16, 1)
    for k in range(8):
        turn = turn + w[:, 16 + k : 17 + k] * coef[k : k + 1, :]
    turn = jnp.where((lane >= 8) & (lane < 16), turn, 0.0)
    weights = jnp.concatenate(
        [pltpu.roll(coef, LANES - 8, 1) + pltpu.roll(turn, 8, 1), -coef, -pltpu.roll(coef, 8, 1)], axis=0
    )[:, :24]
    f, a, n = (rows_of(parts, k, 3) for k in range(3))
    fields = jnp.concatenate([f, a, n], axis=0)
    new = lax.dot_general(weights, fields, (((0,), (0,)), ((), ())), precision=HIGHEST, preferred_element_type=jnp.float32)
    r = rows_of(rhs, 0, 1)
    for ref, v in ((sol, new[:8]), (resid, r + new[8:16]), (direction, f + new[16:24])):
        for t in range(16):
            ref[pl.ds(t, FIELDS, stride=16), :] = v[:, LANES * t : LANES * t + LANES]


def f32(*shape):
    return jax.ShapeDtypeStruct(shape, jnp.float32)


def local(rhs, classes, supports):
    sizes = {a: lax.axis_size(a) for a in ("z", "p", "h", "c", "x")}
    chips = sizes["z"] * sizes["p"] * 2
    upper_chip = lax.axis_index("h")
    pair = lax.axis_index("z") * sizes["p"] + lax.axis_index("p") + jnp.arange(-1, 2, dtype=jnp.int32)
    present = ((pair >= 0) & (pair < chips // 2)).astype(jnp.int32)
    where = jnp.concatenate([upper_chip[None].astype(jnp.int32), present])
    chip = ("z", "p", "h")

    packed = pl.pallas_call(
        pack_kernel,
        out_shape=f32(16, 3, 2, 8, LANES),
        in_specs=[pl.BlockSpec(memory_space=pltpu.HBM)] * 3,
        out_specs=vmem(1)[0],
        scratch_shapes=[
            pltpu.VMEM((8, 2, 8, LANES), jnp.float32),
            pltpu.VMEM((2, 8, LANES), jnp.int32),
            pltpu.VMEM((2, 8, LANES), jnp.int32),
            pltpu.SemaphoreType.DMA((3,)),
        ],
        compiler_params=PARAMS,
    )(rhs, classes, supports)
    own = lax.all_to_all(packed, ("x", "h", "c"), 0, 0)

    def moved(v, sources):
        return lax.ppermute(v, chip, [(s, i) for i, s in enumerate(sources) if 0 <= s < chips])

    far = moved(own, [i + 2 if i % 2 == 0 else i - 2 for i in range(chips)])
    swap = moved(own, [i - 1 if i % 2 == 0 else i + 1 for i in range(chips)])
    first, applied, *coefs = pl.pallas_call(
        first_kernel,
        out_shape=[f32(8, *TILE)] * 2 + [f32(24, *TILE)] * 3 + [f32(12, *TILE)],
        in_specs=smem() + vmem(3),
        out_specs=vmem(6),
        scratch_shapes=[pltpu.VMEM((10, *TILE), jnp.float32), pltpu.VMEM((24, *TILE), jnp.float32)] + work_shapes(),
        compiler_params=PARAMS,
    )(where, own, swap, far)
    below = moved(applied, [i - 2 for i in range(chips)])
    above = moved(applied, [i + 2 for i in range(chips)])
    results = pl.pallas_call(
        second_kernel,
        out_shape=f32(8, 3, 2, 8, LANES),
        in_specs=smem() + vmem(8),
        out_specs=vmem(1)[0],
        scratch_shapes=[pltpu.VMEM((24, *TILE), jnp.float32)] + work_shapes(),
        compiler_params=PARAMS,
    )(where, first, applied, below, above, *coefs)
    parts = lax.all_to_all(results, ("x", "c"), 0, 0).reshape(8 * 48, LANES)
    rows = rhs.reshape(8 * 16, LANES)

    tile = pl.pallas_call(
        gram_kernel, out_shape=f32(sizes["x"], 8, LANES), in_specs=vmem(2), out_specs=vmem(1)[0], compiler_params=PARAMS
    )(parts, rows)
    tile = lax.all_to_all(tile, "x", 0, 0).sum(0)
    tile = jnp.broadcast_to(tile, (sizes["p"] * 4, 8, LANES))
    tile = lax.all_to_all(tile, ("p", "h", "c"), 0, 0).sum(0)
    tile = jnp.broadcast_to(tile, (sizes["z"], 8, LANES))
    tile = lax.all_to_all(tile, "z", 0, 0)
    outs = pl.pallas_call(
        final_kernel,
        out_shape=[f32(128, LANES)] * 3,
        in_specs=vmem(3),
        out_specs=vmem(3),
        compiler_params=PARAMS,
    )(tile, parts, rows)
    return tuple(v.reshape(8, 2, 8, LANES) for v in outs)


def solution(mesh):
    gx, gy = mesh.shape["gx"], mesh.shape["gy"]
    y = min(8, gx // 2)
    fine = Mesh(mesh.devices.reshape(gx // (2 * y), y // 2, 2, 2, gy), ("z", "p", "h", "c", "x"))
    across = ("z", "p", "h", "c")
    grid = P(across, "x", None)
    fields = P(None, across, "x", None)
    return jax.shard_map(
        local, mesh=fine, in_specs=(fields, grid, grid), out_specs=(fields,) * 3, check_vma=False
    )
```

time: 130 us -> 127 us (0.977)
  starting transfers between devices: 28.6 us -> 14.9 us
  waiting for transfers between devices: 3.89 us -> 12.1 us
  blocking collectives: 85.2 us -> 87.5 us
    ppermute x8 -> x4, starting transfers between devices: 28.6 us -> 14.9 us  [moved(): lax.ppermute(v, chip, [(s, i) for i, s in enumerate(sources) if 0 <= s <...]
    ppermute x8 -> x4, waiting for transfers between devices: 3.89 us -> 12.1 us  [moved(): lax.ppermute(v, chip, [(s, i) for i, s in enumerate(sources) if 0 <= s <...]
    all_to_all x4, blocking collectives: 74.1 us -> 77.1 us  [the longest x1 25.1 us: local(): own = lax.all_to_all(packed, ('x', 'h', 'c'), 0, 0)]
  transfers between devices with their start and end apart: 8 -> 4, of which waited for: 3 -> 3; matrix products, arithmetic and copies ran while one was open for 0% -> 0% of each run, Pallas kernels for 0% -> 0%
where the time goes in v2:
time: 127 us
  blocking collectives  87.5 us (69%)
  starting transfers between devices  14.9 us (12%)
  waiting for transfers between devices  12.1 us (10%)
  Pallas kernels  9.17 us (7%)
  local copies, waits for them, and re-layouts  2.25 us (2%)
    all_to_all x1, blocking collectives, local(): own = lax.all_to_all(packed, ('x', 'h', 'c'), 0, 0)  25.1 us
    all_to_all x1, blocking collectives, local(): tile = lax.all_to_all(tile, 'z', 0, 0)  24.1 us
    all_to_all x1, blocking collectives, local(): tile = lax.all_to_all(tile, ('p', 'h', 'c'), 0, 0).sum(0)  21.3 us
    ppermute x4, starting transfers between devices, moved(): lax.ppermute(v, chip, [(s, i) for i, s in enumerate(sources) if 0 <= s <...  14.9 us
    ppermute x4, waiting for transfers between devices, moved(): lax.ppermute(v, chip, [(s, i) for i, s in enumerate(sources) if 0 <= s <...  12.1 us
    all_to_all x1, blocking collectives, local(): parts = lax.all_to_all(results, ('x', 'c'), 0, 0).reshape(8 * 48, LANES)  10.4 us
    all_to_all x1, blocking collectives, local(): tile = lax.all_to_all(tile, 'x', 0, 0).sum(0)  6.56 us
    pallas_call x1, Pallas kernels, local(): pl.pallas_call(first_kernel, out_shape=[f32(8, *TILE)] * 2 + [f32(24, *TI...  4.56 us
  transfers between devices with their start and end apart: 4, of which 3 were waited for; matrix products, arithmetic and copies ran while one was open for 0% of the time, Pallas kernels for 0%

profile of v2, /device:TPU:1, one launch (start us, length us, event | category | flops | bytes accessed | tf_op | source)
XLA Modules:
  0.0 126.7 jit_solution(2304301517948672458)
XLA Ops:
  0.6 0.0 copy-start
  0.6 0.8 copy-done
  1.5 0.0 copy-start.2
  1.5 0.7 copy-done.2
  2.2 0.0 copy-start.3
  2.2 0.7 copy-done.3
  2.9 0.1 shard_map.58
  3.0 25.1 %all_to_all.25.own = f32[16,3,2,8,128]{4,3,2,1,0:T(8,128)S(1)} all-to-all(f32[16,3,2,8,128]{4,3,2,1,0:T(8,128)S(1)} %shard_map.58), channel_id=1, replica_groups=mesh['z'=16,'p'=4,'h'=2,'c'=2,'x'=4] {'x','h','c'}, dimensions={0} | all-to-all | bytes 786432 | tf_op jit(solution)/shard_map/all_to_all | solution.py:302
  28.1 1.3 %collective-permute-start.1 = (f32[16,3,2,8,128]{4,3,2,1,0:T(8,128)S(1)}, f32[16,3,2,8,128]{4,3,2,1,0:T(8,128)S(1)}, u32[]{:S(2)}, u32[]{:S(2)}) collective-permute-start(f32[16,3,2,8,128]{4,3,2,1,0:T(8,128)S(1)} %all_to_all.25.own), channel_id=1, source_target_pairs={{16,0},{32,16},{8,24},{48,32},{24,40},{64,48},{40,56},{80,64},{56,... | collective-permute-start | bytes 1179656 | tf_op jit(solution)/shard_map/ppermute | solution.py:305
  29.4 0.7 collective-permute-start
  30.1 0.1 pad_add_fusion.where
  30.1 10.1 %collective-permute-done.1.far = f32[16,3,2,8,128]{4,3,2,1,0:T(8,128)S(1)} collective-permute-done((f32[16,3,2,8,128]{4,3,2,1,0:T(8,128)S(1)}, f32[16,3,2,8,128]{4,3,2,1,0:T(8,128)S(1)}, u32[]{:S(2)}, u32[]{:S(2)}) %collective-permute-start.1) | collective-permute-done | bytes 393248 | tf_op jit(solution)/shard_map/ppermute | solution.py:305
  40.3 0.0 collective-permute-done.swap
  40.3 4.6 %shard_map.59 = (f32[8,4,8,128]{3,2,1,0:T(8,128)S(1)}, f32[8,4,8,128]{3,2,1,0:T(8,128)S(1)}, f32[24,4,8,128]{3,2,1,0:T(8,128)S(1)}, f32[24,4,8,128]{3,2,1,0:T(8,...) custom-call(s32[4]{0:T(128)S(1)} %pad_add_fusion.where, ...), custom_call_target="tpu_custom_call" | custom-call | tf_op jit(solution)/shard_map/pallas_call | solution.py:309
  44.9 1.3 %collective-permute-start.3 = (f32[8,4,8,128]{3,2,1,0:T(8,128)S(1)}, f32[8,4,8,128]{3,2,1,0:T(8,128)S(1)}, u32[]{:S(2)}, u32[]{:S(2)}) collective-permute-start(f32[8,4,8,128]{3,2,1,0:T(8,128)S(1)} %get-tuple-element.13.applied), channel_id=1, source_target_pairs={{16,0},{24,8},{32,16},{40,24},{48,32},{56,40},{64,48},{72,56},{80,... | collective-permute-start | bytes 393224 | tf_op jit(solution)/shard_map/ppermute | solution.py:305
  46.1 11.6 %collective-permute-start.2 = (f32[8,4,8,128]{3,2,1,0:T(8,128)S(1)}, f32[8,4,8,128]{3,2,1,0:T(8,128)S(1)}, u32[]{:S(2)}, u32[]{:S(2)}) collective-permute-start(f32[8,4,8,128]{3,2,1,0:T(8,128)S(1)} %get-tuple-element.13.applied), channel_id=1, source_target_pairs={{0,16},{8,24},{16,32},{24,40},{32,48},{40,56},{48,64},{56,72},{64,... | collective-permute-start | bytes 393224 | tf_op jit(solution)/shard_map/ppermute | solution.py:305
  57.8 1.1 collective-permute-done.3.above
  58.9 0.8 collective-permute-done.2.below
  59.7 2.2 %shard_map.60 = f32[8,3,2,8,128]{4,3,2,1,0:T(8,128)S(1)} custom-call(s32[4]{0:T(128)S(1)} %pad_add_fusion.where, f32[8,4,8,128]{3,2,1,0:T(8,128)S(1)} %get-tuple-element.12.first, f32[8,4,8,128]{3,2,1,0:T(8,128)S(1)} %get-tuple-element.13.applied, f32[8,4,8,128]{3,2,1,0:T(8,128)S(1)} %collective-permute-done.2.below, ...), custom_call_target="tpu_custom_call" | custom-call | tf_op jit(solution)/shard_map/pallas_call | solution.py:319
  61.9 0.0 copy-start.1
  61.9 10.4 %all_to_all.26 = f32[8,3,2,8,128]{4,3,2,1,0:T(8,128)S(1)} all-to-all(f32[8,3,2,8,128]{4,3,2,1,0:T(8,128)S(1)} %shard_map.60), channel_id=1, replica_groups=mesh['z'=16,'p'=4,'h'=2,'c'=2,'x'=4] {'x','c'}, dimensions={0} | all-to-all | bytes 393216 | tf_op jit(solution)/shard_map/all_to_all | solution.py:327
  72.4 0.0 copy-done.1
  72.4 0.3 shard_map.61
  72.7 6.6 %all_to_all.27 = f32[4,8,128]{2,1,0:T(8,128)S(1)} all-to-all(f32[4,8,128]{2,1,0:T(8,128)S(1)} %shard_map.61), channel_id=1, replica_groups=mesh['z'=16,'p'=4,'h'=2,'c'=2,'x'=4] {'x'}, dimensions={0} | all-to-all | bytes 32768 | tf_op jit(solution)/shard_map/all_to_all | solution.py:333
  79.3 21.3 %all_to_all.28 = f32[16,8,128]{2,1,0:T(8,128)S(1)} all-to-all(f32[16,8,128]{2,1,0:T(8,128)S(1)} %broadcast_in_dim.10), channel_id=1, replica_groups=mesh['z'=16,'p'=4,'h'=2,'c'=2,'x'=4] {'p','h','c'}, dimensions={0} | all-to-all | bytes 131072 | tf_op jit(solution)/shard_map/all_to_all | solution.py:335
  100.7 24.1 %all_to_all.29.sums = f32[16,8,128]{2,1,0:T(8,128)S(1)} all-to-all(f32[16,8,128]{2,1,0:T(8,128)S(1)} %broadcast_in_dim.11), channel_id=1, replica_groups=mesh['z'=16,'p'=4,'h'=2,'c'=2,'x'=4] {'z'}, dimensions={0} | all-to-all | bytes 131072 | tf_op jit(solution)/shard_map/all_to_all | solution.py:337
  124.8 1.9 %shard_map.62 = (f32[128,128]{1,0:T(8,128)}, f32[128,128]{1,0:T(8,128)}, f32[128,128]{1,0:T(8,128)}) custom-call(f32[16,8,128]{2,1,0:T(8,128)S(1)} %all_to_all.29.sums, f32[384,128]{1,0:T(8,128)S(1)} %bitcast.7, f32[128,128]{1,0:T(8,128)S(1)} %bitcast.9), custom_call_target="tpu_custom_call" | custom-call | tf_op jit(solution)/shard_map/pallas_call | solution.py:338
  (5 shorter events, 0.0 us)
Async XLA Ops:
  0.6 0.8 copy-start
  1.5 0.7 copy-start.2
  2.2 0.7 copy-start.3
  28.1 12.2 %collective-permute-start.1 = (f32[16,3,2,8,128]{4,3,2,1,0:T(8,128)S(1)}, f32[16,3,2,8,128]{4,3,2,1,0:T(8,128)S(1)}, u32[]{:S(2)}, u32[]{:S(2)}) collective-permute-start(f32[16,3,2,8,128]{4,3,2,1,0:T(8,128)S(1)} %all_to_all.25.own), channel_id=1, source_target_pairs={{16,0},{32,16},{8,24},{48,32},{24,40},{64,48},{40,56},{80,64},{56,... | collective-permute-start | bytes 1179656 | tf_op jit(solution)/shard_map/ppermute | solution.py:305
  29.4 10.9 %collective-permute-start = (f32[16,3,2,8,128]{4,3,2,1,0:T(8,128)S(1)}, f32[16,3,2,8,128]{4,3,2,1,0:T(8,128)S(1)}, u32[]{:S(2)}, u32[]{:S(2)}) collective-permute-start(f32[16,3,2,8,128]{4,3,2,1,0:T(8,128)S(1)} %all_to_all.25.own), channel_id=1, source_target_pairs={{16,8},{8,16},{32,24},{24,32},{48,40},{40,48},{64,56},{56,64},{80,... | collective-permute-start | bytes 1179656 | tf_op jit(solution)/shard_map/ppermute | solution.py:305
  44.9 14.0 %collective-permute-start.3 = (f32[8,4,8,128]{3,2,1,0:T(8,128)S(1)}, f32[8,4,8,128]{3,2,1,0:T(8,128)S(1)}, u32[]{:S(2)}, u32[]{:S(2)}) collective-permute-start(f32[8,4,8,128]{3,2,1,0:T(8,128)S(1)} %get-tuple-element.13.applied), channel_id=1, source_target_pairs={{16,0},{24,8},{32,16},{40,24},{48,32},{56,40},{64,48},{72,56},{80,... | collective-permute-start | bytes 393224 | tf_op jit(solution)/shard_map/ppermute | solution.py:305
  46.1 13.5 %collective-permute-start.2 = (f32[8,4,8,128]{3,2,1,0:T(8,128)S(1)}, f32[8,4,8,128]{3,2,1,0:T(8,128)S(1)}, u32[]{:S(2)}, u32[]{:S(2)}) collective-permute-start(f32[8,4,8,128]{3,2,1,0:T(8,128)S(1)} %get-tuple-element.13.applied), channel_id=1, source_target_pairs={{0,16},{8,24},{16,32},{24,40},{32,48},{40,56},{48,64},{56,72},{64,... | collective-permute-start | bytes 393224 | tf_op jit(solution)/shard_map/ppermute | solution.py:305
  61.9 10.5 %copy-start.1 = (f32[8,2,8,128]{3,2,1,0:T(8,128)S(1)}, f32[8,2,8,128]{3,2,1,0:T(8,128)}, u32[]{:S(2)}) copy-start(f32[8,2,8,128]{3,2,1,0:T(8,128)} %rhs.1) | copy-start | bytes 196612

commit v3 on v2

--- a/solution.py
+++ b/solution.py
@@ -13,6 +13,7 @@
 TILE = (4, 8, LANES)
 HIGHEST = lax.Precision.HIGHEST
 PARAMS = pltpu.CompilerParams(vmem_limit_bytes=24 * 1024 * 1024)
+WIDE = pltpu.CompilerParams(vmem_limit_bytes=62 * 1024 * 1024)
 
 
 def vmem(n):
@@ -241,15 +242,20 @@
     left = jnp.concatenate([f, a], axis=0)
     right = jnp.concatenate([a, r, n, f, jnp.zeros((LANES - 32, 2048), jnp.float32)], axis=0)
     g = lax.dot_general(left, right, (((1,), (1,)), ((), ())), precision=HIGHEST, preferred_element_type=jnp.float32)
-    tile = jnp.where(iota(1, (8, LANES)) < 16, g[:8], g[8:])
+    lane = iota(1, (8, LANES))
+    tile = jnp.where(lane < 16, g[:8], jnp.where(lane < 32, g[8:], 0.0))
+    turned = [tile] + [pltpu.roll(tile, 32 * m, 1) for m in range(1, 4)]
+    short = jnp.concatenate([sum(turned[m][k + m : k + m + 1] for m in range(4)) for k in (0, 4)], axis=0)
     for k in range(out.shape[0]):
-        out[k] = tile
+        out[k] = short
 
 
 def final_kernel(sums, parts, rhs, sol, resid, direction):
     w = sums[0]
     for k in range(1, sums.shape[0]):
         w = w + sums[k]
+    turned = [w] + [pltpu.roll(w, LANES - 32 * m, 1) for m in range(1, 4)]
+    w = jnp.concatenate([turned[m][k : k + 1] for k in range(2) for m in range(4)], axis=0)
     shape = (8, LANES)
     lane, row = iota(1, shape), iota(0, shape)
     w = jnp.where(lane < 8, 0.5 * (w + pltpu.roll(w, LANES - 24, 1)), w)
@@ -297,7 +303,7 @@
             pltpu.VMEM((2, 8, LANES), jnp.int32),
             pltpu.SemaphoreType.DMA((3,)),
         ],
-        compiler_params=PARAMS,
+        compiler_params=WIDE,
     )(rhs, classes, supports)
     own = lax.all_to_all(packed, ("x", "h", "c"), 0, 0)
 
@@ -328,12 +334,10 @@
     rows = rhs.reshape(8 * 16, LANES)
 
     tile = pl.pallas_call(
-        gram_kernel, out_shape=f32(sizes["x"], 8, LANES), in_specs=vmem(2), out_specs=vmem(1)[0], compiler_params=PARAMS
+        gram_kernel, out_shape=f32(sizes["p"] * 4 * sizes["x"], 2, LANES), in_specs=vmem(2), out_specs=vmem(1)[0], compiler_params=PARAMS
     )(parts, rows)
-    tile = lax.all_to_all(tile, "x", 0, 0).sum(0)
-    tile = jnp.broadcast_to(tile, (sizes["p"] * 4, 8, LANES))
-    tile = lax.all_to_all(tile, ("p", "h", "c"), 0, 0).sum(0)
-    tile = jnp.broadcast_to(tile, (sizes["z"], 8, LANES))
+    tile = lax.all_to_all(tile, ("x", "p", "h", "c"), 0, 0).sum(0)
+    tile = jnp.broadcast_to(tile, (sizes["z"], 2, LANES))
     tile = lax.all_to_all(tile, "z", 0, 0)
     outs = pl.pallas_call(
         final_kernel,

time: 127 us -> 122 us (0.961)
  blocking collectives: 87.5 us -> 82.9 us
  local copies, waits for them, and re-layouts: 2.25 us -> 0.02 us
  Pallas kernels: 9.17 us -> 10.9 us
    all_to_all x2 -> x1, blocking collectives: 27.9 us -> 23.4 us  [local(): tile = lax.all_to_all(tile, ('x', 'p', 'h', 'c'), 0, 0).sum(0)]
    unnamed x8 -> x2, local copies, waits for them, and re-layouts: 2.23 us -> 0.01 us
    pallas_call x1, Pallas kernels: 0.14 us -> 1.65 us  [local(): pl.pallas_call(pack_kernel, out_shape=f32(16, 3, 2, 8, LANES), in_specs=[...]
where the time goes in v3:
time: 122 us
  blocking collectives  82.9 us (68%)
  starting transfers between devices  14.9 us (12%)
  waiting for transfers between devices  12.1 us (10%)
  Pallas kernels  10.9 us (9%)
    all_to_all x1, blocking collectives, local(): own = lax.all_to_all(packed, ('x', 'h', 'c'), 0, 0)  26 us
    all_to_all x1, blocking collectives, local(): tile = lax.all_to_all(tile, ('x', 'p', 'h', 'c'), 0, 0).sum(0)  23.4 us
    all_to_all x1, blocking collectives, local(): tile = lax.all_to_all(tile, 'z', 0, 0)  23.2 us
    ppermute x4, starting transfers between devices, moved(): lax.ppermute(v, chip, [(s, i) for i, s in enumerate(sources) if 0 <= s <...  14.9 us
    ppermute x4, waiting for transfers between devices, moved(): lax.ppermute(v, chip, [(s, i) for i, s in enumerate(sources) if 0 <= s <...  12.1 us
    all_to_all x1, blocking collectives, local(): parts = lax.all_to_all(results, ('x', 'c'), 0, 0).reshape(8 * 48, LANES)  10.4 us
    pallas_call x1, Pallas kernels, local(): pl.pallas_call(first_kernel, out_shape=[f32(8, *TILE)] * 2 + [f32(24, *TI...  4.56 us
  transfers between devices with their start and end apart: 4, of which 3 were waited for; matrix products, arithmetic and copies ran while one was open for 0% of the time, Pallas kernels for 0%

profile of v3, /device:TPU:1, one launch (start us, length us, event | category | flops | bytes accessed | tf_op | source)
XLA Modules:
  0.0 121.6 jit_solution(762146814264081135)
XLA Ops:
  0.6 1.7 %shard_map.58 = f32[16,3,2,8,128]{4,3,2,1,0:T(8,128)} custom-call(f32[8,2,8,128]{3,2,1,0:T(8,128)} %rhs.1, s32[2,8,128]{2,1,0:T(8,128)} %classes.1, s32[2,8,128]{2,1,0:T(8,128)} %supports.1), custom_call_target="tpu_custom_call" | custom-call | tf_op jit(solution)/shard_map/pallas_call | solution.py:295
  2.3 26.0 %all_to_all.20.own = f32[16,3,2,8,128]{4,3,2,1,0:T(8,128)S(1)} all-to-all(f32[16,3,2,8,128]{4,3,2,1,0:T(8,128)} %shard_map.58), channel_id=1, replica_groups=mesh['z'=16,'p'=4,'h'=2,'c'=2,'x'=4] {'x','h','c'}, dimensions={0} | all-to-all | bytes 786432 | tf_op jit(solution)/shard_map/all_to_all | solution.py:308
  28.3 1.3 %collective-permute-start.1 = (f32[16,3,2,8,128]{4,3,2,1,0:T(8,128)S(1)}, f32[16,3,2,8,128]{4,3,2,1,0:T(8,128)S(1)}, u32[]{:S(2)}, u32[]{:S(2)}) collective-permute-start(f32[16,3,2,8,128]{4,3,2,1,0:T(8,128)S(1)} %all_to_all.20.own), channel_id=1, source_target_pairs={{16,0},{32,16},{8,24},{48,32},{24,40},{64,48},{40,56},{80,64},{56,... | collective-permute-start | bytes 1179656 | tf_op jit(solution)/shard_map/ppermute | solution.py:311
  29.5 0.7 collective-permute-start
  30.3 0.1 pad_add_fusion.where
  30.3 10.1 %collective-permute-done.1.far = f32[16,3,2,8,128]{4,3,2,1,0:T(8,128)S(1)} collective-permute-done((f32[16,3,2,8,128]{4,3,2,1,0:T(8,128)S(1)}, f32[16,3,2,8,128]{4,3,2,1,0:T(8,128)S(1)}, u32[]{:S(2)}, u32[]{:S(2)}) %collective-permute-start.1) | collective-permute-done | bytes 393248 | tf_op jit(solution)/shard_map/ppermute | solution.py:311
  40.5 0.0 collective-permute-done.swap
  40.5 4.6 %shard_map.59 = (f32[8,4,8,128]{3,2,1,0:T(8,128)S(1)}, f32[8,4,8,128]{3,2,1,0:T(8,128)S(1)}, f32[24,4,8,128]{3,2,1,0:T(8,128)S(1)}, f32[24,4,8,128]{3,2,1,0:T(8,...) custom-call(s32[4]{0:T(128)S(1)} %pad_add_fusion.where, ...), custom_call_target="tpu_custom_call" | custom-call | tf_op jit(solution)/shard_map/pallas_call | solution.py:315
  45.0 1.3 %collective-permute-start.3 = (f32[8,4,8,128]{3,2,1,0:T(8,128)S(1)}, f32[8,4,8,128]{3,2,1,0:T(8,128)S(1)}, u32[]{:S(2)}, u32[]{:S(2)}) collective-permute-start(f32[8,4,8,128]{3,2,1,0:T(8,128)S(1)} %get-tuple-element.13.applied), channel_id=1, source_target_pairs={{16,0},{24,8},{32,16},{40,24},{48,32},{56,40},{64,48},{72,56},{80,... | collective-permute-start | bytes 393224 | tf_op jit(solution)/shard_map/ppermute | solution.py:311
  46.3 11.6 %collective-permute-start.2 = (f32[8,4,8,128]{3,2,1,0:T(8,128)S(1)}, f32[8,4,8,128]{3,2,1,0:T(8,128)S(1)}, u32[]{:S(2)}, u32[]{:S(2)}) collective-permute-start(f32[8,4,8,128]{3,2,1,0:T(8,128)S(1)} %get-tuple-element.13.applied), channel_id=1, source_target_pairs={{0,16},{8,24},{16,32},{24,40},{32,48},{40,56},{48,64},{56,72},{64,... | collective-permute-start | bytes 393224 | tf_op jit(solution)/shard_map/ppermute | solution.py:311
  57.9 1.0 collective-permute-done.3.above
  59.0 0.9 collective-permute-done.2.below
  59.9 2.2 %shard_map.60 = f32[8,3,2,8,128]{4,3,2,1,0:T(8,128)S(1)} custom-call(s32[4]{0:T(128)S(1)} %pad_add_fusion.where, f32[8,4,8,128]{3,2,1,0:T(8,128)S(1)} %get-tuple-element.12.first, f32[8,4,8,128]{3,2,1,0:T(8,128)S(1)} %get-tuple-element.13.applied, f32[8,4,8,128]{3,2,1,0:T(8,128)S(1)} %collective-permute-done.2.below, ...), custom_call_target="tpu_custom_call" | custom-call | tf_op jit(solution)/shard_map/pallas_call | solution.py:325
  62.1 0.0 copy-start
  62.1 10.4 %all_to_all.21 = f32[8,3,2,8,128]{4,3,2,1,0:T(8,128)S(1)} all-to-all(f32[8,3,2,8,128]{4,3,2,1,0:T(8,128)S(1)} %shard_map.60), channel_id=1, replica_groups=mesh['z'=16,'p'=4,'h'=2,'c'=2,'x'=4] {'x','c'}, dimensions={0} | all-to-all | bytes 393216 | tf_op jit(solution)/shard_map/all_to_all | solution.py:333
  72.5 0.0 copy-done
  72.5 0.4 shard_map.61
  73.0 23.4 %all_to_all.22 = f32[64,2,128]{2,1,0:T(2,128)S(1)} all-to-all(f32[64,2,128]{2,1,0:T(2,128)S(1)} %shard_map.61), channel_id=1, replica_groups=mesh['z'=16,'p'=4,'h'=2,'c'=2,'x'=4] {'x','p','h','c'}, dimensions={0} | all-to-all | bytes 131072 | tf_op jit(solution)/shard_map/all_to_all | solution.py:339
  96.3 0.1 reduce_sum.9
  96.4 23.2 %all_to_all.23.sums = f32[16,2,128]{2,1,0:T(2,128)S(1)} all-to-all(f32[16,2,128]{2,1,0:T(2,128)S(1)} %broadcast_in_dim.7), channel_id=1, replica_groups=mesh['z'=16,'p'=4,'h'=2,'c'=2,'x'=4] {'z'}, dimensions={0} | all-to-all | bytes 32768 | tf_op jit(solution)/shard_map/all_to_all | solution.py:341
  119.6 2.0 %shard_map.62 = (f32[128,128]{1,0:T(8,128)}, f32[128,128]{1,0:T(8,128)}, f32[128,128]{1,0:T(8,128)}) custom-call(f32[16,2,128]{2,1,0:T(2,128)S(1)} %all_to_all.23.sums, f32[384,128]{1,0:T(8,128)S(1)} %bitcast.7, f32[128,128]{1,0:T(8,128)S(1)} %bitcast.9), custom_call_target="tpu_custom_call" | custom-call | tf_op jit(solution)/shard_map/pallas_call | solution.py:342
  (2 shorter events, 0.0 us)
Async XLA Ops:
  28.3 12.2 %collective-permute-start.1 = (f32[16,3,2,8,128]{4,3,2,1,0:T(8,128)S(1)}, f32[16,3,2,8,128]{4,3,2,1,0:T(8,128)S(1)}, u32[]{:S(2)}, u32[]{:S(2)}) collective-permute-start(f32[16,3,2,8,128]{4,3,2,1,0:T(8,128)S(1)} %all_to_all.20.own), channel_id=1, source_target_pairs={{16,0},{32,16},{8,24},{48,32},{24,40},{64,48},{40,56},{80,64},{56,... | collective-permute-start | bytes 1179656 | tf_op jit(solution)/shard_map/ppermute | solution.py:311
  29.5 10.9 %collective-permute-start = (f32[16,3,2,8,128]{4,3,2,1,0:T(8,128)S(1)}, f32[16,3,2,8,128]{4,3,2,1,0:T(8,128)S(1)}, u32[]{:S(2)}, u32[]{:S(2)}) collective-permute-start(f32[16,3,2,8,128]{4,3,2,1,0:T(8,128)S(1)} %all_to_all.20.own), channel_id=1, source_target_pairs={{16,8},{8,16},{32,24},{24,32},{48,40},{40,48},{64,56},{56,64},{80,... | collective-permute-start | bytes 1179656 | tf_op jit(solution)/shard_map/ppermute | solution.py:311
  45.0 13.9 %collective-permute-start.3 = (f32[8,4,8,128]{3,2,1,0:T(8,128)S(1)}, f32[8,4,8,128]{3,2,1,0:T(8,128)S(1)}, u32[]{:S(2)}, u32[]{:S(2)}) collective-permute-start(f32[8,4,8,128]{3,2,1,0:T(8,128)S(1)} %get-tuple-element.13.applied), channel_id=1, source_target_pairs={{16,0},{24,8},{32,16},{40,24},{48,32},{56,40},{64,48},{72,56},{80,... | collective-permute-start | bytes 393224 | tf_op jit(solution)/shard_map/ppermute | solution.py:311
  46.3 13.5 %collective-permute-start.2 = (f32[8,4,8,128]{3,2,1,0:T(8,128)S(1)}, f32[8,4,8,128]{3,2,1,0:T(8,128)S(1)}, u32[]{:S(2)}, u32[]{:S(2)}) collective-permute-start(f32[8,4,8,128]{3,2,1,0:T(8,128)S(1)} %get-tuple-element.13.applied), channel_id=1, source_target_pairs={{0,16},{8,24},{16,32},{24,40},{32,48},{40,56},{48,64},{56,72},{64,... | collective-permute-start | bytes 393224 | tf_op jit(solution)/shard_map/ppermute | solution.py:311
  62.1 10.4 %copy-start = (f32[8,2,8,128]{3,2,1,0:T(8,128)S(1)}, f32[8,2,8,128]{3,2,1,0:T(8,128)}, u32[]{:S(2)}) copy-start(f32[8,2,8,128]{3,2,1,0:T(8,128)} %rhs.1) | copy-start | bytes 196612

commit v4 on v3

--- a/solution.py
+++ b/solution.py
@@ -152,42 +152,58 @@
     copies[0].wait()
     density = (k[...].astype(jnp.float32) + 1.0) / 4.0
     stiff = 0.001 + density * density * density
-    for j in range(16):
-        out[j, 1] = stiff
+    for j in range(0, 16, 2):
+        out[j, 0] = stiff
     copies[1].wait()
     support = s[...].astype(jnp.float32)
-    for j in range(16):
-        out[j, 2] = support
+    for j in range(1, 16, 2):
+        out[j, 0] = support
     copies[2].wait()
     for x in range(4):
         for c in range(2):
             v = r[x * 2 + c]
             for h in range(2):
-                out[(x * 2 + h) * 2 + c, 0] = v
-
-
-def first_kernel(where, own, swap, far, first, applied, s16_out, sp8_out, dv_out, steps_out, out, source_ref, *work):
-    upper_chip = where[0] != 0
+                out[(x * 2 + h) * 2 + c, 1] = v
+
+
+def grids_kernel(*refs):
+    *blocks, out = refs
+    for i, ref in enumerate(blocks):
+        for j in range(16):
+            out[i, j] = ref[j, 0]
+
+
+def first_kernel(
+    where, own, swap, far, own_other, halo_other, first, applied, s16_out, sp8_out, dv_out, steps_out, out, source_ref, *work
+):
+    upper_chip, upper_core = where[0] != 0, where[4] != 0
 
     def block(ref, field, q):
         h, c = q // 4, (q // 2) % 2
-        return jnp.stack([ref[(x * 2 + h) * 2 + c, field, q % 2] for x in range(4)])
-
-    def plane(field, p):
+        return jnp.stack([ref[(x * 2 + h) * 2 + c, *field, q % 2] for x in range(4)])
+
+    def plane(field, p, other=None):
         q = p % 8
         if 0 <= p < 8:
-            return block(own, field, q)
-        a, b = block(swap, field, q), block(far, field, q)
+            return block(own if other is None else own_other.at[0], field, q)
+        if other is None:
+            a, b = block(swap, field, q), block(far, field, q)
+        else:
+            a, b = block(halo_other.at[0], field, q), block(halo_other.at[1], field, q)
         return jnp.where(upper_chip, b, a) if p < 0 else jnp.where(upper_chip, a, b)
+
+    def grids(p):
+        a, b = plane((0,), p), plane((), p, True)
+        return jnp.where(upper_core, b, a), jnp.where(upper_core, a, b)
 
     source, s16, sp8, dv = (Planes(r, -8) for r in (source_ref, s16_out, sp8_out, dv_out))
     steps, fields = Planes(steps_out, -4), Planes(out, -1)
     for p in range(-7, 15):
-        source.put(p, plane(0, p))
-        sp8.put(p, SPRING * plane(2, p))
+        source.put(p, plane((1,), p))
     sums = kept = None
     for p in range(-7, 16):
-        t = plane(1, p)
+        t, support = grids(p)
+        sp8.put(p, SPRING * support)
         s16.put(p, t * (1.0 / 16.0))
         t = t + after_z(t)
         t = t + after_y(t)
@@ -289,12 +305,13 @@
     upper_chip = lax.axis_index("h")
     pair = lax.axis_index("z") * sizes["p"] + lax.axis_index("p") + jnp.arange(-1, 2, dtype=jnp.int32)
     present = ((pair >= 0) & (pair < chips // 2)).astype(jnp.int32)
-    where = jnp.concatenate([upper_chip[None].astype(jnp.int32), present])
+    core = lax.axis_index("c")
+    where = jnp.concatenate([upper_chip[None].astype(jnp.int32), present, core[None].astype(jnp.int32)])
     chip = ("z", "p", "h")
 
     packed = pl.pallas_call(
         pack_kernel,
-        out_shape=f32(16, 3, 2, 8, LANES),
+        out_shape=f32(16, 2, 2, 8, LANES),
         in_specs=[pl.BlockSpec(memory_space=pltpu.HBM)] * 3,
         out_specs=vmem(1)[0],
         scratch_shapes=[
@@ -312,14 +329,27 @@
 
     far = moved(own, [i + 2 if i % 2 == 0 else i - 2 for i in range(chips)])
     swap = moved(own, [i - 1 if i % 2 == 0 else i + 1 for i in range(chips)])
+
+    def partner(*blocks):
+        n = len(blocks)
+        grids = pl.pallas_call(
+            grids_kernel,
+            out_shape=f32(n, 16, 2, 8, LANES),
+            in_specs=vmem(n),
+            out_specs=vmem(1)[0],
+            compiler_params=PARAMS,
+        )(*blocks)
+        return lax.ppermute(grids, "c", [(0, 1), (1, 0)])
+
+    own_other, halo_other = partner(own), partner(swap, far)
     first, applied, *coefs = pl.pallas_call(
         first_kernel,
         out_shape=[f32(8, *TILE)] * 2 + [f32(24, *TILE)] * 3 + [f32(12, *TILE)],
-        in_specs=smem() + vmem(3),
+        in_specs=smem() + vmem(5),
         out_specs=vmem(6),
         scratch_shapes=[pltpu.VMEM((10, *TILE), jnp.float32), pltpu.VMEM((24, *TILE), jnp.float32)] + work_shapes(),
         compiler_params=PARAMS,
-    )(where, own, swap, far)
+    )(where, own, swap, far, own_other, halo_other)
     below = moved(applied, [i - 2 for i in range(chips)])
     above = moved(applied, [i + 2 for i in range(chips)])
     results = pl.pallas_call(

time: 122 us -> 121 us (level)
  blocking collectives: 82.9 us -> 81.1 us
  starting transfers between devices: 14.9 us -> 16.4 us
    ppermute x0 -> x2, starting transfers between devices: none -> 7.27 us  [partner(): return lax.ppermute(grids, 'c', [(0, 1), (1, 0)])]
    ppermute x4, starting transfers between devices: 14.9 us -> 9.15 us  [moved(): lax.ppermute(v, chip, [(s, i) for i, s in enumerate(sources) if 0 <= s <...]
    ppermute x4, waiting for transfers between devices: 12.1 us -> 10.3 us  [moved(): lax.ppermute(v, chip, [(s, i) for i, s in enumerate(sources) if 0 <= s <...]
    all_to_all x1, blocking collectives: 26 us -> 24.7 us  [local(): own = lax.all_to_all(packed, ('x', 'h', 'c'), 0, 0)]
    ppermute x0 -> x2, waiting for transfers between devices: none -> 1.22 us  [partner(): return lax.ppermute(grids, 'c', [(0, 1), (1, 0)])]
  transfers between devices with their start and end apart: 4 -> 6, of which waited for: 3 -> 4; matrix products, arithmetic and copies ran while one was open for 0% -> 0% of each run, Pallas kernels for 0% -> 0%
where the time goes in v4:
time: 121 us
  blocking collectives  81.1 us (67%)
  starting transfers between devices  16.4 us (14%)
  waiting for transfers between devices  11.6 us (10%)
  Pallas kernels  10.8 us (9%)
    all_to_all x1, blocking collectives, local(): own = lax.all_to_all(packed, ('x', 'h', 'c'), 0, 0)  24.7 us
    all_to_all x1, blocking collectives, local(): tile = lax.all_to_all(tile, ('x', 'p', 'h', 'c'), 0, 0).sum(0)  23.7 us
    all_to_all x1, blocking collectives, local(): tile = lax.all_to_all(tile, 'z', 0, 0)  23.3 us
    ppermute x4, waiting for transfers between devices, moved(): lax.ppermute(v, chip, [(s, i) for i, s in enumerate(sources) if 0 <= s <...  10.3 us
    all_to_all x1, blocking collectives, local(): parts = lax.all_to_all(results, ('x', 'c'), 0, 0).reshape(8 * 48, LANES)  9.48 us
    ppermute x4, starting transfers between devices, moved(): lax.ppermute(v, chip, [(s, i) for i, s in enumerate(sources) if 0 <= s <...  9.15 us
    ppermute x2, starting transfers between devices, partner(): return lax.ppermute(grids, 'c', [(0, 1), (1, 0)])  7.27 us
    pallas_call x1, Pallas kernels, local(): pl.pallas_call(first_kernel, out_shape=[f32(8, *TILE)] * 2 + [f32(24, *TI...  4.54 us
  transfers between devices with their start and end apart: 6, of which 4 were waited for; matrix products, arithmetic and copies ran while one was open for 0% of the time, Pallas kernels for 0%

profile of v4, /device:TPU:1, one launch (start us, length us, event | category | flops | bytes accessed | tf_op | source)
XLA Modules:
  0.0 120.9 jit_solution(11436898473333144446)
XLA Ops:
  0.6 1.6 %shard_map.58 = f32[16,2,2,8,128]{4,3,2,1,0:T(8,128)} custom-call(f32[8,2,8,128]{3,2,1,0:T(8,128)} %rhs.1, s32[2,8,128]{2,1,0:T(8,128)} %classes.1, s32[2,8,128]{2,1,0:T(8,128)} %supports.1), custom_call_target="tpu_custom_call" | custom-call | tf_op jit(solution)/shard_map/pallas_call | solution.py:312
  2.2 24.7 %all_to_all.20.refs_0_.own = f32[16,2,2,8,128]{4,3,2,1,0:T(8,128)S(1)} all-to-all(f32[16,2,2,8,128]{4,3,2,1,0:T(8,128)} %shard_map.58), channel_id=1, replica_groups=mesh['z'=16,'p'=4,'h'=2,'c'=2,'x'=4] {'x','h','c'}, dimensions={0} | all-to-all | bytes 524288 | tf_op jit(solution)/shard_map/all_to_all | solution.py:325
  26.9 1.3 %collective-permute-start.1 = (f32[16,2,2,8,128]{4,3,2,1,0:T(8,128)S(1)}, f32[16,2,2,8,128]{4,3,2,1,0:T(8,128)S(1)}, u32[]{:S(2)}, u32[]{:S(2)}) collective-permute-start(f32[16,2,2,8,128]{4,3,2,1,0:T(8,128)S(1)} %all_to_all.20.refs_0_.own), channel_id=1, source_target_pairs={{16,0},{32,16},{8,24},{48,32},{24,40},{64,48},{40,56},{80,64},{56,... | collective-permute-start | bytes 786440 | tf_op jit(solution)/shard_map/ppermute | solution.py:328
  28.2 0.7 collective-permute-start
  28.9 7.6 %collective-permute-done.1.refs_1_.far = f32[16,2,2,8,128]{4,3,2,1,0:T(8,128)S(1)} collective-permute-done((f32[16,2,2,8,128]{4,3,2,1,0:T(8,128)S(1)}, f32[16,2,2,8,128]{4,3,2,1,0:T(8,128)S(1)}, u32[]{:S(2)}, u32[]{:S(2)}) %collective-permute-start.1) | collective-permute-done | bytes 262176 | tf_op jit(solution)/shard_map/ppermute | solution.py:328
  36.5 0.0 collective-permute-done.refs_0_.swap
  36.6 5.3 %collective-permute-start.3 = (f32[2,16,2,8,128]{4,3,2,1,0:T(8,128)S(1)}, f32[2,16,2,8,128]{4,3,2,1,0:T(8,128)S(1)}, u32[]{:S(2)}, u32[]{:S(2)}) collective-permute-start(f32[2,16,2,8,128]{4,3,2,1,0:T(8,128)S(1)} %shard_map.60), channel_id=1, source_target_pairs={{0,4},{4,0},{1,5},{5,1},{2,6},{6,2},{3,7},{7,3},{8,12},{12,8},{9,1... | collective-permute-start | bytes 786440 | tf_op jit(solution)/shard_map/ppermute | solution.py:342
  41.9 1.9 %collective-permute-start.2 = (f32[1,16,2,8,128]{4,3,2,1,0:T(8,128)S(1)}, f32[1,16,2,8,128]{4,3,2,1,0:T(8,128)S(1)}, u32[]{:S(2)}, u32[]{:S(2)}) collective-permute-start(f32[1,16,2,8,128]{4,3,2,1,0:T(8,128)S(1)} %shard_map.59), channel_id=1, source_target_pairs={{0,4},{4,0},{1,5},{5,1},{2,6},{6,2},{3,7},{7,3},{8,12},{12,8},{9,1... | collective-permute-start | bytes 393224 | tf_op jit(solution)/shard_map/ppermute | solution.py:342
  43.9 0.1 pad_add_fusion.where
  44.0 1.2 %collective-permute-done.2.own_other = f32[1,16,2,8,128]{4,3,2,1,0:T(8,128)S(1)} collective-permute-done((f32[1,16,2,8,128]{4,3,2,1,0:T(8,128)S(1)}, f32[1,16,2,8,128]{4,3,2,1,0:T(8,128)S(1)}, u32[]{:S(2)}, u32[]{:S(2)}) %collective-permute-start.2) | collective-permute-done | bytes 131104 | tf_op jit(solution)/shard_map/ppermute | solution.py:342
  45.2 0.0 collective-permute-done.3.halo_other
  45.2 4.5 %shard_map.61 = (f32[8,4,8,128]{3,2,1,0:T(8,128)S(1)}, f32[8,4,8,128]{3,2,1,0:T(8,128)S(1)}, f32[24,4,8,128]{3,2,1,0:T(8,128)S(1)}, f32[24,4,8,128]{3,2,1,0:T(8,...) custom-call(s32[5]{0:T(128)S(1)} %pad_add_fusion.where, ...), custom_call_target="tpu_custom_call" | custom-call | tf_op jit(solution)/shard_map/pallas_call | solution.py:345
  49.7 1.3 %collective-permute-start.5 = (f32[8,4,8,128]{3,2,1,0:T(8,128)S(1)}, f32[8,4,8,128]{3,2,1,0:T(8,128)S(1)}, u32[]{:S(2)}, u32[]{:S(2)}) collective-permute-start(f32[8,4,8,128]{3,2,1,0:T(8,128)S(1)} %get-tuple-element.13.applied), channel_id=1, source_target_pairs={{16,0},{24,8},{32,16},{40,24},{48,32},{56,40},{64,48},{72,56},{80,... | collective-permute-start | bytes 393224 | tf_op jit(solution)/shard_map/ppermute | solution.py:328
  51.0 5.9 %collective-permute-start.4 = (f32[8,4,8,128]{3,2,1,0:T(8,128)S(1)}, f32[8,4,8,128]{3,2,1,0:T(8,128)S(1)}, u32[]{:S(2)}, u32[]{:S(2)}) collective-permute-start(f32[8,4,8,128]{3,2,1,0:T(8,128)S(1)} %get-tuple-element.13.applied), channel_id=1, source_target_pairs={{0,16},{8,24},{16,32},{24,40},{32,48},{40,56},{48,64},{56,72},{64,... | collective-permute-start | bytes 393224 | tf_op jit(solution)/shard_map/ppermute | solution.py:328
  56.9 1.8 %collective-permute-done.5.above = f32[8,4,8,128]{3,2,1,0:T(8,128)S(1)} collective-permute-done((f32[8,4,8,128]{3,2,1,0:T(8,128)S(1)}, f32[8,4,8,128]{3,2,1,0:T(8,128)S(1)}, u32[]{:S(2)}, u32[]{:S(2)}) %collective-permute-start.5) | collective-permute-done | bytes 131104 | tf_op jit(solution)/shard_map/ppermute | solution.py:328
  58.7 0.9 collective-permute-done.4.below
  59.6 2.2 %shard_map.62 = f32[8,3,2,8,128]{4,3,2,1,0:T(8,128)S(1)} custom-call(s32[5]{0:T(128)S(1)} %pad_add_fusion.where, f32[8,4,8,128]{3,2,1,0:T(8,128)S(1)} %get-tuple-element.12.first, f32[8,4,8,128]{3,2,1,0:T(8,128)S(1)} %get-tuple-element.13.applied, f32[8,4,8,128]{3,2,1,0:T(8,128)S(1)} %collective-permute-done.4.below, ...), custom_call_target="tpu_custom_call" | custom-call | tf_op jit(solution)/shard_map/pallas_call | solution.py:355
  61.9 0.0 copy-start
  61.9 9.5 %all_to_all.21 = f32[8,3,2,8,128]{4,3,2,1,0:T(8,128)S(1)} all-to-all(f32[8,3,2,8,128]{4,3,2,1,0:T(8,128)S(1)} %shard_map.62), channel_id=1, replica_groups=mesh['z'=16,'p'=4,'h'=2,'c'=2,'x'=4] {'x','c'}, dimensions={0} | all-to-all | bytes 393216 | tf_op jit(solution)/shard_map/all_to_all | solution.py:363
  71.4 0.0 copy-done
  71.4 0.4 shard_map.63
  71.8 23.7 %all_to_all.22 = f32[64,2,128]{2,1,0:T(2,128)S(1)} all-to-all(f32[64,2,128]{2,1,0:T(2,128)S(1)} %shard_map.63), channel_id=1, replica_groups=mesh['z'=16,'p'=4,'h'=2,'c'=2,'x'=4] {'x','p','h','c'}, dimensions={0} | all-to-all | bytes 131072 | tf_op jit(solution)/shard_map/all_to_all | solution.py:369
  95.5 0.1 reduce_sum.9
  95.6 23.3 %all_to_all.23.sums = f32[16,2,128]{2,1,0:T(2,128)S(1)} all-to-all(f32[16,2,128]{2,1,0:T(2,128)S(1)} %broadcast_in_dim.11), channel_id=1, replica_groups=mesh['z'=16,'p'=4,'h'=2,'c'=2,'x'=4] {'z'}, dimensions={0} | all-to-all | bytes 32768 | tf_op jit(solution)/shard_map/all_to_all | solution.py:371
  118.9 2.0 %shard_map.64 = (f32[128,128]{1,0:T(8,128)}, f32[128,128]{1,0:T(8,128)}, f32[128,128]{1,0:T(8,128)}) custom-call(f32[16,2,128]{2,1,0:T(2,128)S(1)} %all_to_all.23.sums, f32[384,128]{1,0:T(8,128)S(1)} %bitcast.8, f32[128,128]{1,0:T(8,128)S(1)} %bitcast.10), custom_call_target="tpu_custom_call" | custom-call | tf_op jit(solution)/shard_map/pallas_call | solution.py:372
  (4 shorter events, 0.0 us)
Async XLA Ops:
  26.9 9.6 %collective-permute-start.1 = (f32[16,2,2,8,128]{4,3,2,1,0:T(8,128)S(1)}, f32[16,2,2,8,128]{4,3,2,1,0:T(8,128)S(1)}, u32[]{:S(2)}, u32[]{:S(2)}) collective-permute-start(f32[16,2,2,8,128]{4,3,2,1,0:T(8,128)S(1)} %all_to_all.20.refs_0_.own), channel_id=1, source_target_pairs={{16,0},{32,16},{8,24},{48,32},{24,40},{64,48},{40,56},{80,64},{56,... | collective-permute-start | bytes 786440 | tf_op jit(solution)/shard_map/ppermute | solution.py:328
  28.2 8.3 %collective-permute-start = (f32[16,2,2,8,128]{4,3,2,1,0:T(8,128)S(1)}, f32[16,2,2,8,128]{4,3,2,1,0:T(8,128)S(1)}, u32[]{:S(2)}, u32[]{:S(2)}) collective-permute-start(f32[16,2,2,8,128]{4,3,2,1,0:T(8,128)S(1)} %all_to_all.20.refs_0_.own), channel_id=1, source_target_pairs={{16,8},{8,16},{32,24},{24,32},{48,40},{40,48},{64,56},{56,64},{80,... | collective-permute-start | bytes 786440 | tf_op jit(solution)/shard_map/ppermute | solution.py:328
  36.6 8.6 %collective-permute-start.3 = (f32[2,16,2,8,128]{4,3,2,1,0:T(8,128)S(1)}, f32[2,16,2,8,128]{4,3,2,1,0:T(8,128)S(1)}, u32[]{:S(2)}, u32[]{:S(2)}) collective-permute-start(f32[2,16,2,8,128]{4,3,2,1,0:T(8,128)S(1)} %shard_map.60), channel_id=1, source_target_pairs={{0,4},{4,0},{1,5},{5,1},{2,6},{6,2},{3,7},{7,3},{8,12},{12,8},{9,1... | collective-permute-start | bytes 786440 | tf_op jit(solution)/shard_map/ppermute | solution.py:342
  41.9 3.2 %collective-permute-start.2 = (f32[1,16,2,8,128]{4,3,2,1,0:T(8,128)S(1)}, f32[1,16,2,8,128]{4,3,2,1,0:T(8,128)S(1)}, u32[]{:S(2)}, u32[]{:S(2)}) collective-permute-start(f32[1,16,2,8,128]{4,3,2,1,0:T(8,128)S(1)} %shard_map.59), channel_id=1, source_target_pairs={{0,4},{4,0},{1,5},{5,1},{2,6},{6,2},{3,7},{7,3},{8,12},{12,8},{9,1... | collective-permute-start | bytes 393224 | tf_op jit(solution)/shard_map/ppermute | solution.py:342
  49.7 9.0 %collective-permute-start.5 = (f32[8,4,8,128]{3,2,1,0:T(8,128)S(1)}, f32[8,4,8,128]{3,2,1,0:T(8,128)S(1)}, u32[]{:S(2)}, u32[]{:S(2)}) collective-permute-start(f32[8,4,8,128]{3,2,1,0:T(8,128)S(1)} %get-tuple-element.13.applied), channel_id=1, source_target_pairs={{16,0},{24,8},{32,16},{40,24},{48,32},{56,40},{64,48},{72,56},{80,... | collective-permute-start | bytes 393224 | tf_op jit(solution)/shard_map/ppermute | solution.py:328
  51.0 8.6 %collective-permute-start.4 = (f32[8,4,8,128]{3,2,1,0:T(8,128)S(1)}, f32[8,4,8,128]{3,2,1,0:T(8,128)S(1)}, u32[]{:S(2)}, u32[]{:S(2)}) collective-permute-start(f32[8,4,8,128]{3,2,1,0:T(8,128)S(1)} %get-tuple-element.13.applied), channel_id=1, source_target_pairs={{0,16},{8,24},{16,32},{24,40},{32,48},{40,56},{48,64},{56,72},{64,... | collective-permute-start | bytes 393224 | tf_op jit(solution)/shard_map/ppermute | solution.py:328
  61.9 9.5 %copy-start = (f32[8,2,8,128]{3,2,1,0:T(8,128)S(1)}, f32[8,2,8,128]{3,2,1,0:T(8,128)}, u32[]{:S(2)}) copy-start(f32[8,2,8,128]{3,2,1,0:T(8,128)} %rhs.1) | copy-start | bytes 196612

commit v5 on v4

--- a/solution.py
+++ b/solution.py
@@ -47,8 +47,16 @@
 
 
 def pair_sum(v):
-    v = v + jnp.where(iota(1) % 2 == 0, pltpu.roll(v, 7, 1), pltpu.roll(v, 1, 1))
-    return v + jnp.where(iota(2) % 2 == 0, pltpu.roll(v, LANES - 1, 2), pltpu.roll(v, 1, 2))
+    v = (v + jnp.where(iota(1) % 2 == 0, pltpu.roll(v, 7, 1), pltpu.roll(v, 1, 1))).reshape(32, LANES)
+    square = (LANES, LANES)
+    ones = (iota(0, square) // 2 == iota(1, square) // 2).astype(jnp.bfloat16)
+    high = v.astype(jnp.bfloat16)
+    rest = v - high.astype(jnp.float32)
+    middle = rest.astype(jnp.bfloat16)
+    low = (rest - middle.astype(jnp.float32)).astype(jnp.bfloat16)
+    pieces = jnp.concatenate([high, middle, low], axis=1)
+    ones = jnp.concatenate([ones] * 3, axis=0)
+    return jnp.dot(pieces, ones, preferred_element_type=jnp.float32).reshape(TILE)
 
 
 def spread(u):
@@ -85,18 +93,31 @@
         last, above = now, to_upper
 
 
-def apply_coarse(c, s16, sp8, least, most):
-    last, above = spread(c(least - 1)), None
+def restricted(even, odd, s16, least, most):
+    last, above = (even if odd is None else odd)(least - 1), None
     for i in range(least, most + 2):
-        now = spread(c(i))
+        now = even(i)
         to_lower, to_upper = element_plane(last, now, s16(2 * i))
         if above is not None:
-            inner = s16(2 * i - 1) * 4.0
-            part = [inner * last[1], inner * last[2], (inner * (2.0 / 3.0)) * last[3]]
             n = [a + b for a, b in zip(above, to_lower)]
-            n = [n[0]] + [a + b for a, b in zip(n[1:], part)]
-            yield i - 1, pair_sum(gather(n) + (sp8(2 * i - 2) + sp8(2 * i - 1)) * c(i - 1))
-        last, above = now, to_upper
+            yield i - 1, gather([n[0]] + [a + b for a, b in zip(n[1:], inside)])
+        if i <= most:
+            last = now if odd is None else odd(i)
+            inner = s16(2 * i + 1) * (4.0 if odd is None else 2.0)
+            both = now if odd is None else [a + b for a, b in zip(now, last)]
+            inside = [inner * both[1], inner * both[2], (inner * (2.0 / 3.0)) * both[3]]
+        above = to_upper
+
+
+def apply_coarse(c, s16, sp8, least, most):
+    for i, h in restricted(lambda i: spread(c(i)), None, s16, least, most):
+        yield i, pair_sum(h + (sp8(2 * i) + sp8(2 * i + 1)) * c(i))
+
+
+def coarse_residual(source, u, s16, sp8, least, most):
+    for i, h in restricted(lambda i: spread(u(2 * i)), lambda i: spread(u(2 * i + 1)), s16, least, most):
+        a, b = 2 * i, 2 * i + 1
+        yield i, pair_sum((source(a) - sp8(a) * u(a)) + (source(b) - sp8(b) * u(b)) - h)
 
 
 class Planes:
@@ -118,15 +139,9 @@
     lo, hi = (least - 1) // 2, (most + 1) // 2
     for p in range(2 * lo - 5, 2 * hi + 7):
         z.put(p, dv(p) * source(p))
-    kept = None
-    for p, a in apply_fine(z, s16, sp8, 2 * lo - 4, 2 * hi + 5):
-        v = source(p) - a
-        if p % 2:
-            i = p // 2
-            r = pair_sum(kept + v)
-            res.put(i, r)
-            c.put(i, steps(i) * r)
-        kept = v
+    for i, r in coarse_residual(source, z, s16, sp8, lo - 2, hi + 2):
+        res.put(i, r)
+        c.put(i, steps(i) * r)
     for old, new, first, last in ((c, c1, lo - 1, hi + 1), (c1, c, lo, hi)):
         for i, a in apply_coarse(old, s16, sp8, first, last):
             new.put(i, old(i) + steps(i) * (res(i) - a))
@@ -174,7 +189,7 @@
 
 
 def first_kernel(
-    where, own, swap, far, own_other, halo_other, first, applied, s16_out, sp8_out, dv_out, steps_out, out, source_ref, *work
+    where, own, swap, far, other, first, applied, s16_out, sp8_out, dv_out, steps_out, out, source_ref, *work
 ):
     upper_chip, upper_core = where[0] != 0, where[4] != 0
 
@@ -182,18 +197,16 @@
         h, c = q // 4, (q // 2) % 2
         return jnp.stack([ref[(x * 2 + h) * 2 + c, *field, q % 2] for x in range(4)])
 
-    def plane(field, p, other=None):
+    def plane(field, p, grid=None):
         q = p % 8
         if 0 <= p < 8:
-            return block(own if other is None else own_other.at[0], field, q)
-        if other is None:
-            a, b = block(swap, field, q), block(far, field, q)
-        else:
-            a, b = block(halo_other.at[0], field, q), block(halo_other.at[1], field, q)
+            return block(own if grid is None else grid.at[0], field, q)
+        a, b = (swap, far) if grid is None else (grid.at[1], grid.at[2])
+        a, b = block(a, field, q), block(b, field, q)
         return jnp.where(upper_chip, b, a) if p < 0 else jnp.where(upper_chip, a, b)
 
     def grids(p):
-        a, b = plane((0,), p), plane((), p, True)
+        a, b = plane((0,), p), plane((), p, other)
         return jnp.where(upper_core, b, a), jnp.where(upper_core, a, b)
 
     source, s16, sp8, dv = (Planes(r, -8) for r in (source_ref, s16_out, sp8_out, dv_out))
@@ -275,9 +288,13 @@
     shape = (8, LANES)
     lane, row = iota(1, shape), iota(0, shape)
     w = jnp.where(lane < 8, 0.5 * (w + pltpu.roll(w, LANES - 24, 1)), w)
+    scale = jnp.ones(shape, jnp.float32)
     for k in range(8):
-        pivot = w[k : k + 1, :] / w[k : k + 1, k : k + 1]
-        w = jnp.where(row == k, pivot, w - w[:, k : k + 1] * pivot)
+        column = jnp.broadcast_to(w[:, k : k + 1], shape)
+        inverse = 1.0 / jnp.broadcast_to(column[k : k + 1, :], shape)
+        scale = jnp.where(row == k, inverse, scale)
+        w = w - jnp.where(row == k, 0.0, column * inverse) * w[k : k + 1, :]
+    w = w * scale
     coef = jnp.where((lane >= 8) & (lane < 16), w, 0.0)
     turn = -pltpu.roll(w, LANES - 16, 1)
     for k in range(8):
@@ -341,15 +358,15 @@
         )(*blocks)
         return lax.ppermute(grids, "c", [(0, 1), (1, 0)])
 
-    own_other, halo_other = partner(own), partner(swap, far)
+    other = partner(own, swap, far)
     first, applied, *coefs = pl.pallas_call(
         first_kernel,
         out_shape=[f32(8, *TILE)] * 2 + [f32(24, *TILE)] * 3 + [f32(12, *TILE)],
-        in_specs=smem() + vmem(5),
+        in_specs=smem() + vmem(4),
         out_specs=vmem(6),
         scratch_shapes=[pltpu.VMEM((10, *TILE), jnp.float32), pltpu.VMEM((24, *TILE), jnp.float32)] + work_shapes(),
         compiler_params=PARAMS,
-    )(where, own, swap, far, own_other, halo_other)
+    )(where, own, swap, far, other)
     below = moved(applied, [i - 2 for i in range(chips)])
     above = moved(applied, [i + 2 for i in range(chips)])
     results = pl.pallas_call(

time: 121 us -> 118 us (0.975)
  starting transfers between devices: 16.4 us -> 14.5 us
    ppermute x2 -> x1, starting transfers between devices: 7.27 us -> 5.35 us  [partner(): return lax.ppermute(grids, 'c', [(0, 1), (1, 0)])]
    pallas_call x1, Pallas kernels: 4.54 us -> 3.13 us  [local(): pl.pallas_call(first_kernel, out_shape=[f32(8, *TILE)] * 2 + [f32(24, *TI...]
  transfers between devices with their start and end apart: 6 -> 5, of which waited for: 4 -> 4; matrix products, arithmetic and copies ran while one was open for 0% -> 0% of each run, Pallas kernels for 0% -> 0%
where the time goes in v5:
time: 118 us
  blocking collectives  81.4 us (69%)
  starting transfers between devices  14.5 us (12%)
  waiting for transfers between devices  11.3 us (10%)
  Pallas kernels  9.61 us (8%)
    all_to_all x1, blocking collectives, local(): own = lax.all_to_all(packed, ('x', 'h', 'c'), 0, 0)  24.7 us
    all_to_all x1, blocking collectives, local(): tile = lax.all_to_all(tile, ('x', 'p', 'h', 'c'), 0, 0).sum(0)  23.7 us
    all_to_all x1, blocking collectives, local(): tile = lax.all_to_all(tile, 'z', 0, 0)  23.3 us
    ppermute x4, waiting for transfers between devices, moved(): lax.ppermute(v, chip, [(s, i) for i, s in enumerate(sources) if 0 <= s <...  10.1 us
    all_to_all x1, blocking collectives, local(): parts = lax.all_to_all(results, ('x', 'c'), 0, 0).reshape(8 * 48, LANES)  9.72 us
    ppermute x4, starting transfers between devices, moved(): lax.ppermute(v, chip, [(s, i) for i, s in enumerate(sources) if 0 <= s <...  9.15 us
    ppermute x1, starting transfers between devices, partner(): return lax.ppermute(grids, 'c', [(0, 1), (1, 0)])  5.35 us
    pallas_call x1, Pallas kernels, local(): pl.pallas_call(first_kernel, out_shape=[f32(8, *TILE)] * 2 + [f32(24, *TI...  3.13 us
  transfers between devices with their start and end apart: 5, of which 4 were waited for; matrix products, arithmetic and copies ran while one was open for 0% of the time, Pallas kernels for 0%

profile of v5, /device:TPU:1, one launch (start us, length us, event | category | flops | bytes accessed | tf_op | source)
XLA Modules:
  0.0 117.7 jit_solution(8557162056216028834)
XLA Ops:
  0.6 1.6 %shard_map.58 = f32[16,2,2,8,128]{4,3,2,1,0:T(8,128)} custom-call(f32[8,2,8,128]{3,2,1,0:T(8,128)} %rhs.1, s32[2,8,128]{2,1,0:T(8,128)} %classes.1, s32[2,8,128]{2,1,0:T(8,128)} %supports.1), custom_call_target="tpu_custom_call" | custom-call | tf_op jit(solution)/shard_map/pallas_call | solution.py:329
  2.2 24.7 %all_to_all.20.refs_0_.own = f32[16,2,2,8,128]{4,3,2,1,0:T(8,128)S(1)} all-to-all(f32[16,2,2,8,128]{4,3,2,1,0:T(8,128)} %shard_map.58), channel_id=1, replica_groups=mesh['z'=16,'p'=4,'h'=2,'c'=2,'x'=4] {'x','h','c'}, dimensions={0} | all-to-all | bytes 524288 | tf_op jit(solution)/shard_map/all_to_all | solution.py:342
  26.9 1.3 %collective-permute-start.1 = (f32[16,2,2,8,128]{4,3,2,1,0:T(8,128)S(1)}, f32[16,2,2,8,128]{4,3,2,1,0:T(8,128)S(1)}, u32[]{:S(2)}, u32[]{:S(2)}) collective-permute-start(f32[16,2,2,8,128]{4,3,2,1,0:T(8,128)S(1)} %all_to_all.20.refs_0_.own), channel_id=1, source_target_pairs={{16,0},{32,16},{8,24},{48,32},{24,40},{64,48},{40,56},{80,64},{56,... | collective-permute-start | bytes 786440 | tf_op jit(solution)/shard_map/ppermute | solution.py:345
  28.2 0.7 collective-permute-start
  28.9 7.6 %collective-permute-done.1.refs_2_.far = f32[16,2,2,8,128]{4,3,2,1,0:T(8,128)S(1)} collective-permute-done((f32[16,2,2,8,128]{4,3,2,1,0:T(8,128)S(1)}, f32[16,2,2,8,128]{4,3,2,1,0:T(8,128)S(1)}, u32[]{:S(2)}, u32[]{:S(2)}) %collective-permute-start.1) | collective-permute-done | bytes 262176 | tf_op jit(solution)/shard_map/ppermute | solution.py:345
  36.5 0.0 collective-permute-done.refs_1_.swap
  36.6 5.3 %collective-permute-start.2 = (f32[3,16,2,8,128]{4,3,2,1,0:T(8,128)S(1)}, f32[3,16,2,8,128]{4,3,2,1,0:T(8,128)S(1)}, u32[]{:S(2)}, u32[]{:S(2)}) collective-permute-start(f32[3,16,2,8,128]{4,3,2,1,0:T(8,128)S(1)} %shard_map.59), channel_id=1, source_target_pairs={{0,4},{4,0},{1,5},{5,1},{2,6},{6,2},{3,7},{7,3},{8,12},{12,8},{9,1... | collective-permute-start | bytes 1179656 | tf_op jit(solution)/shard_map/ppermute | solution.py:359
  41.9 0.1 pad_add_fusion.where
  42.0 1.2 %collective-permute-done.2.other = f32[3,16,2,8,128]{4,3,2,1,0:T(8,128)S(1)} collective-permute-done((f32[3,16,2,8,128]{4,3,2,1,0:T(8,128)S(1)}, f32[3,16,2,8,128]{4,3,2,1,0:T(8,128)S(1)}, u32[]{:S(2)}, u32[]{:S(2)}) %collective-permute-start.2) | collective-permute-done | bytes 393248 | tf_op jit(solution)/shard_map/ppermute | solution.py:359
  43.2 3.1 %shard_map.60 = (f32[8,4,8,128]{3,2,1,0:T(8,128)S(1)}, f32[8,4,8,128]{3,2,1,0:T(8,128)S(1)}, f32[24,4,8,128]{3,2,1,0:T(8,128)S(1)}, f32[24,4,8,128]{3,2,1,0:T(8,...) custom-call(s32[5]{0:T(128)S(1)} %pad_add_fusion.where, ...), custom_call_target="tpu_custom_call" | custom-call | tf_op jit(solution)/shard_map/pallas_call | solution.py:362
  46.4 1.3 %collective-permute-start.4 = (f32[8,4,8,128]{3,2,1,0:T(8,128)S(1)}, f32[8,4,8,128]{3,2,1,0:T(8,128)S(1)}, u32[]{:S(2)}, u32[]{:S(2)}) collective-permute-start(f32[8,4,8,128]{3,2,1,0:T(8,128)S(1)} %get-tuple-element.13.applied), channel_id=1, source_target_pairs={{16,0},{24,8},{32,16},{40,24},{48,32},{56,40},{64,48},{72,56},{80,... | collective-permute-start | bytes 393224 | tf_op jit(solution)/shard_map/ppermute | solution.py:345
  47.7 5.9 %collective-permute-start.3 = (f32[8,4,8,128]{3,2,1,0:T(8,128)S(1)}, f32[8,4,8,128]{3,2,1,0:T(8,128)S(1)}, u32[]{:S(2)}, u32[]{:S(2)}) collective-permute-start(f32[8,4,8,128]{3,2,1,0:T(8,128)S(1)} %get-tuple-element.13.applied), channel_id=1, source_target_pairs={{0,16},{8,24},{16,32},{24,40},{32,48},{40,56},{48,64},{56,72},{64,... | collective-permute-start | bytes 393224 | tf_op jit(solution)/shard_map/ppermute | solution.py:345
  53.6 1.6 %collective-permute-done.4.above = f32[8,4,8,128]{3,2,1,0:T(8,128)S(1)} collective-permute-done((f32[8,4,8,128]{3,2,1,0:T(8,128)S(1)}, f32[8,4,8,128]{3,2,1,0:T(8,128)S(1)}, u32[]{:S(2)}, u32[]{:S(2)}) %collective-permute-start.4) | collective-permute-done | bytes 131104 | tf_op jit(solution)/shard_map/ppermute | solution.py:345
  55.2 0.9 collective-permute-done.3.below
  56.1 2.2 %shard_map.61 = f32[8,3,2,8,128]{4,3,2,1,0:T(8,128)S(1)} custom-call(s32[5]{0:T(128)S(1)} %pad_add_fusion.where, f32[8,4,8,128]{3,2,1,0:T(8,128)S(1)} %get-tuple-element.12.first, f32[8,4,8,128]{3,2,1,0:T(8,128)S(1)} %get-tuple-element.13.applied, f32[8,4,8,128]{3,2,1,0:T(8,128)S(1)} %collective-permute-done.3.below, ...), custom_call_target="tpu_custom_call" | custom-call | tf_op jit(solution)/shard_map/pallas_call | solution.py:372
  58.3 0.0 copy-start
  58.3 9.7 %all_to_all.21 = f32[8,3,2,8,128]{4,3,2,1,0:T(8,128)S(1)} all-to-all(f32[8,3,2,8,128]{4,3,2,1,0:T(8,128)S(1)} %shard_map.61), channel_id=1, replica_groups=mesh['z'=16,'p'=4,'h'=2,'c'=2,'x'=4] {'x','c'}, dimensions={0} | all-to-all | bytes 393216 | tf_op jit(solution)/shard_map/all_to_all | solution.py:380
  68.0 0.0 copy-done
  68.0 0.4 shard_map.62
  68.4 23.7 %all_to_all.22 = f32[64,2,128]{2,1,0:T(2,128)S(1)} all-to-all(f32[64,2,128]{2,1,0:T(2,128)S(1)} %shard_map.62), channel_id=1, replica_groups=mesh['z'=16,'p'=4,'h'=2,'c'=2,'x'=4] {'x','p','h','c'}, dimensions={0} | all-to-all | bytes 131072 | tf_op jit(solution)/shard_map/all_to_all | solution.py:386
  92.1 0.1 reduce_sum.9
  92.2 23.3 %all_to_all.23.sums = f32[16,2,128]{2,1,0:T(2,128)S(1)} all-to-all(f32[16,2,128]{2,1,0:T(2,128)S(1)} %broadcast_in_dim.11), channel_id=1, replica_groups=mesh['z'=16,'p'=4,'h'=2,'c'=2,'x'=4] {'z'}, dimensions={0} | all-to-all | bytes 32768 | tf_op jit(solution)/shard_map/all_to_all | solution.py:388
  115.5 2.2 %shard_map.63 = (f32[128,128]{1,0:T(8,128)}, f32[128,128]{1,0:T(8,128)}, f32[128,128]{1,0:T(8,128)}) custom-call(f32[16,2,128]{2,1,0:T(2,128)S(1)} %all_to_all.23.sums, f32[384,128]{1,0:T(8,128)S(1)} %bitcast.8, f32[128,128]{1,0:T(8,128)S(1)} %bitcast.10), custom_call_target="tpu_custom_call" | custom-call | tf_op jit(solution)/shard_map/pallas_call | solution.py:389
  (3 shorter events, 0.0 us)
Async XLA Ops:
  26.9 9.6 %collective-permute-start.1 = (f32[16,2,2,8,128]{4,3,2,1,0:T(8,128)S(1)}, f32[16,2,2,8,128]{4,3,2,1,0:T(8,128)S(1)}, u32[]{:S(2)}, u32[]{:S(2)}) collective-permute-start(f32[16,2,2,8,128]{4,3,2,1,0:T(8,128)S(1)} %all_to_all.20.refs_0_.own), channel_id=1, source_target_pairs={{16,0},{32,16},{8,24},{48,32},{24,40},{64,48},{40,56},{80,64},{56,... | collective-permute-start | bytes 786440 | tf_op jit(solution)/shard_map/ppermute | solution.py:345
  28.2 8.3 %collective-permute-start = (f32[16,2,2,8,128]{4,3,2,1,0:T(8,128)S(1)}, f32[16,2,2,8,128]{4,3,2,1,0:T(8,128)S(1)}, u32[]{:S(2)}, u32[]{:S(2)}) collective-permute-start(f32[16,2,2,8,128]{4,3,2,1,0:T(8,128)S(1)} %all_to_all.20.refs_0_.own), channel_id=1, source_target_pairs={{16,8},{8,16},{32,24},{24,32},{48,40},{40,48},{64,56},{56,64},{80,... | collective-permute-start | bytes 786440 | tf_op jit(solution)/shard_map/ppermute | solution.py:345
  36.6 6.7 %collective-permute-start.2 = (f32[3,16,2,8,128]{4,3,2,1,0:T(8,128)S(1)}, f32[3,16,2,8,128]{4,3,2,1,0:T(8,128)S(1)}, u32[]{:S(2)}, u32[]{:S(2)}) collective-permute-start(f32[3,16,2,8,128]{4,3,2,1,0:T(8,128)S(1)} %shard_map.59), channel_id=1, source_target_pairs={{0,4},{4,0},{1,5},{5,1},{2,6},{6,2},{3,7},{7,3},{8,12},{12,8},{9,1... | collective-permute-start | bytes 1179656 | tf_op jit(solution)/shard_map/ppermute | solution.py:359
  46.4 8.8 %collective-permute-start.4 = (f32[8,4,8,128]{3,2,1,0:T(8,128)S(1)}, f32[8,4,8,128]{3,2,1,0:T(8,128)S(1)}, u32[]{:S(2)}, u32[]{:S(2)}) collective-permute-start(f32[8,4,8,128]{3,2,1,0:T(8,128)S(1)} %get-tuple-element.13.applied), channel_id=1, source_target_pairs={{16,0},{24,8},{32,16},{40,24},{48,32},{56,40},{64,48},{72,56},{80,... | collective-permute-start | bytes 393224 | tf_op jit(solution)/shard_map/ppermute | solution.py:345
  47.7 8.4 %collective-permute-start.3 = (f32[8,4,8,128]{3,2,1,0:T(8,128)S(1)}, f32[8,4,8,128]{3,2,1,0:T(8,128)S(1)}, u32[]{:S(2)}, u32[]{:S(2)}) collective-permute-start(f32[8,4,8,128]{3,2,1,0:T(8,128)S(1)} %get-tuple-element.13.applied), channel_id=1, source_target_pairs={{0,16},{8,24},{16,32},{24,40},{32,48},{40,56},{48,64},{56,72},{64,... | collective-permute-start | bytes 393224 | tf_op jit(solution)/shard_map/ppermute | solution.py:345
  58.3 9.7 %copy-start = (f32[8,2,8,128]{3,2,1,0:T(8,128)S(1)}, f32[8,2,8,128]{3,2,1,0:T(8,128)}, u32[]{:S(2)}) copy-start(f32[8,2,8,128]{3,2,1,0:T(8,128)} %rhs.1) | copy-start | bytes 196612

commit v6 on v5

--- a/solution.py
+++ b/solution.py
@@ -288,12 +288,15 @@
     shape = (8, LANES)
     lane, row = iota(1, shape), iota(0, shape)
     w = jnp.where(lane < 8, 0.5 * (w + pltpu.roll(w, LANES - 24, 1)), w)
+    columns = [jnp.broadcast_to(w[:, k : k + 1], shape) for k in range(8)]
     scale = jnp.ones(shape, jnp.float32)
     for k in range(8):
-        column = jnp.broadcast_to(w[:, k : k + 1], shape)
-        inverse = 1.0 / jnp.broadcast_to(column[k : k + 1, :], shape)
+        inverse = 1.0 / columns[k][k : k + 1, :]
         scale = jnp.where(row == k, inverse, scale)
-        w = w - jnp.where(row == k, 0.0, column * inverse) * w[k : k + 1, :]
+        factor = jnp.where(row == k, 0.0, columns[k] * inverse)
+        for j in range(k + 1, 8):
+            columns[j] = columns[j] - factor * columns[j][k : k + 1, :]
+        w = w - factor * w[k : k + 1, :]
     w = w * scale
     coef = jnp.where((lane >= 8) & (lane < 16), w, 0.0)
     turn = -pltpu.roll(w, LANES - 16, 1)

time: 118 us -> 118 us (level)
  no operation moved by 1% of the time
where the time goes in v6:
time: 118 us; the launch traced here: 117 us
  blocking collectives  81.4 us (69%)
  starting transfers between devices  14.5 us (12%)
  waiting for transfers between devices  11.3 us (10%)
  Pallas kernels  8.94 us (8%)
    all_to_all x1, blocking collectives, local(): own = lax.all_to_all(packed, ('x', 'h', 'c'), 0, 0)  24.7 us
    all_to_all x1, blocking collectives, local(): tile = lax.all_to_all(tile, ('x', 'p', 'h', 'c'), 0, 0).sum(0)  23.7 us
    all_to_all x1, blocking collectives, local(): tile = lax.all_to_all(tile, 'z', 0, 0)  23.3 us
    ppermute x4, waiting for transfers between devices, moved(): lax.ppermute(v, chip, [(s, i) for i, s in enumerate(sources) if 0 <= s <...  10.1 us
    all_to_all x1, blocking collectives, local(): parts = lax.all_to_all(results, ('x', 'c'), 0, 0).reshape(8 * 48, LANES)  9.72 us
    ppermute x4, starting transfers between devices, moved(): lax.ppermute(v, chip, [(s, i) for i, s in enumerate(sources) if 0 <= s <...  9.15 us
    ppermute x1, starting transfers between devices, partner(): return lax.ppermute(grids, 'c', [(0, 1), (1, 0)])  5.35 us
    pallas_call x1, Pallas kernels, local(): pl.pallas_call(first_kernel, out_shape=[f32(8, *TILE)] * 2 + [f32(24, *TI...  3.13 us
  transfers between devices with their start and end apart: 5, of which 4 were waited for; matrix products, arithmetic and copies ran while one was open for 0% of the time, Pallas kernels for 0%

profile of v6, /device:TPU:1, one launch (start us, length us, event | category | flops | bytes accessed | tf_op | source)
XLA Modules:
  0.0 117.0 jit_solution(16831069219530288989)
XLA Ops:
  0.6 1.6 %shard_map.58 = f32[16,2,2,8,128]{4,3,2,1,0:T(8,128)} custom-call(f32[8,2,8,128]{3,2,1,0:T(8,128)} %rhs.1, s32[2,8,128]{2,1,0:T(8,128)} %classes.1, s32[2,8,128]{2,1,0:T(8,128)} %supports.1), custom_call_target="tpu_custom_call" | custom-call | tf_op jit(solution)/shard_map/pallas_call | solution.py:332
  2.2 24.7 %all_to_all.20.refs_0_.own = f32[16,2,2,8,128]{4,3,2,1,0:T(8,128)S(1)} all-to-all(f32[16,2,2,8,128]{4,3,2,1,0:T(8,128)} %shard_map.58), channel_id=1, replica_groups=mesh['z'=16,'p'=4,'h'=2,'c'=2,'x'=4] {'x','h','c'}, dimensions={0} | all-to-all | bytes 524288 | tf_op jit(solution)/shard_map/all_to_all | solution.py:345
  26.9 1.3 %collective-permute-start.1 = (f32[16,2,2,8,128]{4,3,2,1,0:T(8,128)S(1)}, f32[16,2,2,8,128]{4,3,2,1,0:T(8,128)S(1)}, u32[]{:S(2)}, u32[]{:S(2)}) collective-permute-start(f32[16,2,2,8,128]{4,3,2,1,0:T(8,128)S(1)} %all_to_all.20.refs_0_.own), channel_id=1, source_target_pairs={{16,0},{32,16},{8,24},{48,32},{24,40},{64,48},{40,56},{80,64},{56,... | collective-permute-start | bytes 786440 | tf_op jit(solution)/shard_map/ppermute | solution.py:348
  28.2 0.7 collective-permute-start
  28.9 7.6 %collective-permute-done.1.refs_2_.far = f32[16,2,2,8,128]{4,3,2,1,0:T(8,128)S(1)} collective-permute-done((f32[16,2,2,8,128]{4,3,2,1,0:T(8,128)S(1)}, f32[16,2,2,8,128]{4,3,2,1,0:T(8,128)S(1)}, u32[]{:S(2)}, u32[]{:S(2)}) %collective-permute-start.1) | collective-permute-done | bytes 262176 | tf_op jit(solution)/shard_map/ppermute | solution.py:348
  36.5 0.0 collective-permute-done.refs_1_.swap
  36.6 5.3 %collective-permute-start.2 = (f32[3,16,2,8,128]{4,3,2,1,0:T(8,128)S(1)}, f32[3,16,2,8,128]{4,3,2,1,0:T(8,128)S(1)}, u32[]{:S(2)}, u32[]{:S(2)}) collective-permute-start(f32[3,16,2,8,128]{4,3,2,1,0:T(8,128)S(1)} %shard_map.59), channel_id=1, source_target_pairs={{0,4},{4,0},{1,5},{5,1},{2,6},{6,2},{3,7},{7,3},{8,12},{12,8},{9,1... | collective-permute-start | bytes 1179656 | tf_op jit(solution)/shard_map/ppermute | solution.py:362
  41.9 0.1 pad_add_fusion.where
  42.0 1.2 %collective-permute-done.2.other = f32[3,16,2,8,128]{4,3,2,1,0:T(8,128)S(1)} collective-permute-done((f32[3,16,2,8,128]{4,3,2,1,0:T(8,128)S(1)}, f32[3,16,2,8,128]{4,3,2,1,0:T(8,128)S(1)}, u32[]{:S(2)}, u32[]{:S(2)}) %collective-permute-start.2) | collective-permute-done | bytes 393248 | tf_op jit(solution)/shard_map/ppermute | solution.py:362
  43.2 3.1 %shard_map.60 = (f32[8,4,8,128]{3,2,1,0:T(8,128)S(1)}, f32[8,4,8,128]{3,2,1,0:T(8,128)S(1)}, f32[24,4,8,128]{3,2,1,0:T(8,128)S(1)}, f32[24,4,8,128]{3,2,1,0:T(8,...) custom-call(s32[5]{0:T(128)S(1)} %pad_add_fusion.where, ...), custom_call_target="tpu_custom_call" | custom-call | tf_op jit(solution)/shard_map/pallas_call | solution.py:365
  46.4 1.3 %collective-permute-start.4 = (f32[8,4,8,128]{3,2,1,0:T(8,128)S(1)}, f32[8,4,8,128]{3,2,1,0:T(8,128)S(1)}, u32[]{:S(2)}, u32[]{:S(2)}) collective-permute-start(f32[8,4,8,128]{3,2,1,0:T(8,128)S(1)} %get-tuple-element.13.applied), channel_id=1, source_target_pairs={{16,0},{24,8},{32,16},{40,24},{48,32},{56,40},{64,48},{72,56},{80,... | collective-permute-start | bytes 393224 | tf_op jit(solution)/shard_map/ppermute | solution.py:348
  47.7 5.9 %collective-permute-start.3 = (f32[8,4,8,128]{3,2,1,0:T(8,128)S(1)}, f32[8,4,8,128]{3,2,1,0:T(8,128)S(1)}, u32[]{:S(2)}, u32[]{:S(2)}) collective-permute-start(f32[8,4,8,128]{3,2,1,0:T(8,128)S(1)} %get-tuple-element.13.applied), channel_id=1, source_target_pairs={{0,16},{8,24},{16,32},{24,40},{32,48},{40,56},{48,64},{56,72},{64,... | collective-permute-start | bytes 393224 | tf_op jit(solution)/shard_map/ppermute | solution.py:348
  53.6 1.6 %collective-permute-done.4.above = f32[8,4,8,128]{3,2,1,0:T(8,128)S(1)} collective-permute-done((f32[8,4,8,128]{3,2,1,0:T(8,128)S(1)}, f32[8,4,8,128]{3,2,1,0:T(8,128)S(1)}, u32[]{:S(2)}, u32[]{:S(2)}) %collective-permute-start.4) | collective-permute-done | bytes 131104 | tf_op jit(solution)/shard_map/ppermute | solution.py:348
  55.2 0.9 collective-permute-done.3.below
  56.1 2.2 %shard_map.61 = f32[8,3,2,8,128]{4,3,2,1,0:T(8,128)S(1)} custom-call(s32[5]{0:T(128)S(1)} %pad_add_fusion.where, f32[8,4,8,128]{3,2,1,0:T(8,128)S(1)} %get-tuple-element.12.first, f32[8,4,8,128]{3,2,1,0:T(8,128)S(1)} %get-tuple-element.13.applied, f32[8,4,8,128]{3,2,1,0:T(8,128)S(1)} %collective-permute-done.3.below, ...), custom_call_target="tpu_custom_call" | custom-call | tf_op jit(solution)/shard_map/pallas_call | solution.py:375
  58.3 0.0 copy-start
  58.3 9.7 %all_to_all.21 = f32[8,3,2,8,128]{4,3,2,1,0:T(8,128)S(1)} all-to-all(f32[8,3,2,8,128]{4,3,2,1,0:T(8,128)S(1)} %shard_map.61), channel_id=1, replica_groups=mesh['z'=16,'p'=4,'h'=2,'c'=2,'x'=4] {'x','c'}, dimensions={0} | all-to-all | bytes 393216 | tf_op jit(solution)/shard_map/all_to_all | solution.py:383
  68.0 0.0 copy-done
  68.0 0.4 shard_map.62
  68.4 23.7 %all_to_all.22 = f32[64,2,128]{2,1,0:T(2,128)S(1)} all-to-all(f32[64,2,128]{2,1,0:T(2,128)S(1)} %shard_map.62), channel_id=1, replica_groups=mesh['z'=16,'p'=4,'h'=2,'c'=2,'x'=4] {'x','p','h','c'}, dimensions={0} | all-to-all | bytes 131072 | tf_op jit(solution)/shard_map/all_to_all | solution.py:389
  92.1 0.1 reduce_sum.9
  92.2 23.3 %all_to_all.23.sums = f32[16,2,128]{2,1,0:T(2,128)S(1)} all-to-all(f32[16,2,128]{2,1,0:T(2,128)S(1)} %broadcast_in_dim.11), channel_id=1, replica_groups=mesh['z'=16,'p'=4,'h'=2,'c'=2,'x'=4] {'z'}, dimensions={0} | all-to-all | bytes 32768 | tf_op jit(solution)/shard_map/all_to_all | solution.py:391
  115.5 1.6 %shard_map.63 = (f32[128,128]{1,0:T(8,128)}, f32[128,128]{1,0:T(8,128)}, f32[128,128]{1,0:T(8,128)}) custom-call(f32[16,2,128]{2,1,0:T(2,128)S(1)} %all_to_all.23.sums, f32[384,128]{1,0:T(8,128)S(1)} %bitcast.8, f32[128,128]{1,0:T(8,128)S(1)} %bitcast.10), custom_call_target="tpu_custom_call" | custom-call | tf_op jit(solution)/shard_map/pallas_call | solution.py:392
  (3 shorter events, 0.0 us)
Async XLA Ops:
  26.9 9.6 %collective-permute-start.1 = (f32[16,2,2,8,128]{4,3,2,1,0:T(8,128)S(1)}, f32[16,2,2,8,128]{4,3,2,1,0:T(8,128)S(1)}, u32[]{:S(2)}, u32[]{:S(2)}) collective-permute-start(f32[16,2,2,8,128]{4,3,2,1,0:T(8,128)S(1)} %all_to_all.20.refs_0_.own), channel_id=1, source_target_pairs={{16,0},{32,16},{8,24},{48,32},{24,40},{64,48},{40,56},{80,64},{56,... | collective-permute-start | bytes 786440 | tf_op jit(solution)/shard_map/ppermute | solution.py:348
  28.2 8.3 %collective-permute-start = (f32[16,2,2,8,128]{4,3,2,1,0:T(8,128)S(1)}, f32[16,2,2,8,128]{4,3,2,1,0:T(8,128)S(1)}, u32[]{:S(2)}, u32[]{:S(2)}) collective-permute-start(f32[16,2,2,8,128]{4,3,2,1,0:T(8,128)S(1)} %all_to_all.20.refs_0_.own), channel_id=1, source_target_pairs={{16,8},{8,16},{32,24},{24,32},{48,40},{40,48},{64,56},{56,64},{80,... | collective-permute-start | bytes 786440 | tf_op jit(solution)/shard_map/ppermute | solution.py:348
  36.6 6.7 %collective-permute-start.2 = (f32[3,16,2,8,128]{4,3,2,1,0:T(8,128)S(1)}, f32[3,16,2,8,128]{4,3,2,1,0:T(8,128)S(1)}, u32[]{:S(2)}, u32[]{:S(2)}) collective-permute-start(f32[3,16,2,8,128]{4,3,2,1,0:T(8,128)S(1)} %shard_map.59), channel_id=1, source_target_pairs={{0,4},{4,0},{1,5},{5,1},{2,6},{6,2},{3,7},{7,3},{8,12},{12,8},{9,1... | collective-permute-start | bytes 1179656 | tf_op jit(solution)/shard_map/ppermute | solution.py:362
  46.4 8.8 %collective-permute-start.4 = (f32[8,4,8,128]{3,2,1,0:T(8,128)S(1)}, f32[8,4,8,128]{3,2,1,0:T(8,128)S(1)}, u32[]{:S(2)}, u32[]{:S(2)}) collective-permute-start(f32[8,4,8,128]{3,2,1,0:T(8,128)S(1)} %get-tuple-element.13.applied), channel_id=1, source_target_pairs={{16,0},{24,8},{32,16},{40,24},{48,32},{56,40},{64,48},{72,56},{80,... | collective-permute-start | bytes 393224 | tf_op jit(solution)/shard_map/ppermute | solution.py:348
  47.7 8.4 %collective-permute-start.3 = (f32[8,4,8,128]{3,2,1,0:T(8,128)S(1)}, f32[8,4,8,128]{3,2,1,0:T(8,128)S(1)}, u32[]{:S(2)}, u32[]{:S(2)}) collective-permute-start(f32[8,4,8,128]{3,2,1,0:T(8,128)S(1)} %get-tuple-element.13.applied), channel_id=1, source_target_pairs={{0,16},{8,24},{16,32},{24,40},{32,48},{40,56},{48,64},{56,72},{64,... | collective-permute-start | bytes 393224 | tf_op jit(solution)/shard_map/ppermute | solution.py:348
  58.3 9.7 %copy-start = (f32[8,2,8,128]{3,2,1,0:T(8,128)S(1)}, f32[8,2,8,128]{3,2,1,0:T(8,128)}, u32[]{:S(2)}) copy-start(f32[8,2,8,128]{3,2,1,0:T(8,128)} %rhs.1) | copy-start | bytes 196612

commit v7 on v6

--- a/solution.py
+++ b/solution.py
@@ -189,34 +189,29 @@
 
 
 def first_kernel(
-    where, own, swap, far, other, first, applied, s16_out, sp8_out, dv_out, steps_out, out, source_ref, *work
+    where, own, swap, far, grids, first, applied, s16_out, sp8_out, dv_out, steps_out, out, source_ref, *work
 ):
-    upper_chip, upper_core = where[0] != 0, where[4] != 0
-
-    def block(ref, field, q):
+    upper_chip = where[0] != 0
+
+    def plane(refs, p):
+        q = p % 8
         h, c = q // 4, (q // 2) % 2
-        return jnp.stack([ref[(x * 2 + h) * 2 + c, *field, q % 2] for x in range(4)])
-
-    def plane(field, p, grid=None):
-        q = p % 8
+        block = lambda ref: jnp.stack([ref[(x * 2 + h) * 2 + c, q % 2] for x in range(4)])
         if 0 <= p < 8:
-            return block(own if grid is None else grid.at[0], field, q)
-        a, b = (swap, far) if grid is None else (grid.at[1], grid.at[2])
-        a, b = block(a, field, q), block(b, field, q)
+            return block(refs[0])
+        a, b = block(refs[1]), block(refs[2])
         return jnp.where(upper_chip, b, a) if p < 0 else jnp.where(upper_chip, a, b)
 
-    def grids(p):
-        a, b = plane((0,), p), plane((), p, other)
-        return jnp.where(upper_core, b, a), jnp.where(upper_core, a, b)
-
+    fields = [ref.at[:, 1] for ref in (own, swap, far)]
+    stiffs, supports = ([grids.at[core, i] for i in range(3)] for core in range(2))
     source, s16, sp8, dv = (Planes(r, -8) for r in (source_ref, s16_out, sp8_out, dv_out))
-    steps, fields = Planes(steps_out, -4), Planes(out, -1)
+    steps, new = Planes(steps_out, -4), Planes(out, -1)
     for p in range(-7, 15):
-        source.put(p, plane((1,), p))
+        source.put(p, plane(fields, p))
     sums = kept = None
     for p in range(-7, 16):
-        t, support = grids(p)
-        sp8.put(p, SPRING * support)
+        t = plane(stiffs, p)
+        sp8.put(p, SPRING * plane(supports, p))
         s16.put(p, t * (1.0 / 16.0))
         t = t + after_z(t)
         t = t + after_y(t)
@@ -231,12 +226,12 @@
         sums = t
 
     def emit(p, v):
-        fields.put(p, v)
+        new.put(p, v)
         if 0 <= p < 8:
             first[p] = v
 
     precondition(source, s16, sp8, dv, steps, work_of(*work), -1, 8, emit)
-    for p, v in apply_fine(fields, s16, sp8, 0, 7):
+    for p, v in apply_fine(new, s16, sp8, 0, 7):
         applied[p] = v
 
 
@@ -325,8 +320,7 @@
     upper_chip = lax.axis_index("h")
     pair = lax.axis_index("z") * sizes["p"] + lax.axis_index("p") + jnp.arange(-1, 2, dtype=jnp.int32)
     present = ((pair >= 0) & (pair < chips // 2)).astype(jnp.int32)
-    core = lax.axis_index("c")
-    where = jnp.concatenate([upper_chip[None].astype(jnp.int32), present, core[None].astype(jnp.int32)])
+    where = jnp.concatenate([upper_chip[None].astype(jnp.int32), present])
     chip = ("z", "p", "h")
 
     packed = pl.pallas_call(
@@ -350,7 +344,7 @@
     far = moved(own, [i + 2 if i % 2 == 0 else i - 2 for i in range(chips)])
     swap = moved(own, [i - 1 if i % 2 == 0 else i + 1 for i in range(chips)])
 
-    def partner(*blocks):
+    def both_cores(*blocks):
         n = len(blocks)
         grids = pl.pallas_call(
             grids_kernel,
@@ -359,9 +353,9 @@
             out_specs=vmem(1)[0],
             compiler_params=PARAMS,
         )(*blocks)
-        return lax.ppermute(grids, "c", [(0, 1), (1, 0)])
-
-    other = partner(own, swap, far)
+        return lax.all_gather(grids, "c")
+
+    grids = both_cores(own, swap, far)
     first, applied, *coefs = pl.pallas_call(
         first_kernel,
         out_shape=[f32(8, *TILE)] * 2 + [f32(24, *TILE)] * 3 + [f32(12, *TILE)],
@@ -369,7 +363,7 @@
         out_specs=vmem(6),
         scratch_shapes=[pltpu.VMEM((10, *TILE), jnp.float32), pltpu.VMEM((24, *TILE), jnp.float32)] + work_shapes(),
         compiler_params=PARAMS,
-    )(where, own, swap, far, other)
+    )(where, own, swap, far, grids)
     below = moved(applied, [i - 2 for i in range(chips)])
     above = moved(applied, [i + 2 for i in range(chips)])
     results = pl.pallas_call(

time: 118 us -> 116 us (0.983)
  blocking collectives: 81.4 us -> 86.8 us
  starting transfers between devices: 14.5 us -> 9.15 us
  waiting for transfers between devices: 11.3 us -> 10 us
    all_gather x0 -> x1, blocking collectives: none -> 5.44 us  [both_cores(): return lax.all_gather(grids, 'c')]
    ppermute x1 -> x0, starting transfers between devices: 5.35 us -> none  [partner(): return lax.ppermute(grids, 'c', [(0, 1), (1, 0)])]
    ppermute x1 -> x0, waiting for transfers between devices: 1.23 us -> none  [partner(): return lax.ppermute(grids, 'c', [(0, 1), (1, 0)])]
  transfers between devices with their start and end apart: 5 -> 4, of which waited for: 4 -> 3; matrix products, arithmetic and copies ran while one was open for 0% -> 0% of each run, Pallas kernels for 0% -> 0%
where the time goes in v7:
time: 116 us
  blocking collectives  86.8 us (75%)
  waiting for transfers between devices  10 us (9%)
  starting transfers between devices  9.15 us (8%)
  Pallas kernels  8.92 us (8%)
    all_to_all x1, blocking collectives, local(): own = lax.all_to_all(packed, ('x', 'h', 'c'), 0, 0)  24.7 us
    all_to_all x1, blocking collectives, local(): tile = lax.all_to_all(tile, ('x', 'p', 'h', 'c'), 0, 0).sum(0)  23.7 us
    all_to_all x1, blocking collectives, local(): tile = lax.all_to_all(tile, 'z', 0, 0)  23.3 us
    ppermute x4, waiting for transfers between devices, moved(): lax.ppermute(v, chip, [(s, i) for i, s in enumerate(sources) if 0 <= s <...  10 us
    all_to_all x1, blocking collectives, local(): parts = lax.all_to_all(results, ('x', 'c'), 0, 0).reshape(8 * 48, LANES)  9.72 us
    ppermute x4, starting transfers between devices, moved(): lax.ppermute(v, chip, [(s, i) for i, s in enumerate(sources) if 0 <= s <...  9.15 us
    all_gather x1, blocking collectives, both_cores(): return lax.all_gather(grids, 'c')  5.44 us
    pallas_call x1, Pallas kernels, local(): pl.pallas_call(first_kernel, out_shape=[f32(8, *TILE)] * 2 + [f32(24, *TI...  3.13 us
  transfers between devices with their start and end apart: 4, of which 3 were waited for; matrix products, arithmetic and copies ran while one was open for 0% of the time, Pallas kernels for 0%

profile of v7, /device:TPU:1, one launch (start us, length us, event | category | flops | bytes accessed | tf_op | source)
XLA Modules:
  0.0 115.8 jit_solution(13383801522549145756)
XLA Ops:
  0.6 1.6 %shard_map.58 = f32[16,2,2,8,128]{4,3,2,1,0:T(8,128)} custom-call(f32[8,2,8,128]{3,2,1,0:T(8,128)} %rhs.1, s32[2,8,128]{2,1,0:T(8,128)} %classes.1, s32[2,8,128]{2,1,0:T(8,128)} %supports.1), custom_call_target="tpu_custom_call" | custom-call | tf_op jit(solution)/shard_map/pallas_call | solution.py:326
  2.2 24.7 %all_to_all.20.refs_0_.own = f32[16,2,2,8,128]{4,3,2,1,0:T(8,128)S(1)} all-to-all(f32[16,2,2,8,128]{4,3,2,1,0:T(8,128)} %shard_map.58), channel_id=1, replica_groups=mesh['z'=16,'p'=4,'h'=2,'c'=2,'x'=4] {'x','h','c'}, dimensions={0} | all-to-all | bytes 524288 | tf_op jit(solution)/shard_map/all_to_all | solution.py:339
  26.9 1.3 %collective-permute-start.1 = (f32[16,2,2,8,128]{4,3,2,1,0:T(8,128)S(1)}, f32[16,2,2,8,128]{4,3,2,1,0:T(8,128)S(1)}, u32[]{:S(2)}, u32[]{:S(2)}) collective-permute-start(f32[16,2,2,8,128]{4,3,2,1,0:T(8,128)S(1)} %all_to_all.20.refs_0_.own), channel_id=1, source_target_pairs={{16,0},{32,16},{8,24},{48,32},{24,40},{64,48},{40,56},{80,64},{56,... | collective-permute-start | bytes 786440 | tf_op jit(solution)/shard_map/ppermute | solution.py:342
  28.2 0.7 collective-permute-start
  28.9 0.1 pad_add_fusion.where
  29.0 7.5 %collective-permute-done.1.refs_2_.far = f32[16,2,2,8,128]{4,3,2,1,0:T(8,128)S(1)} collective-permute-done((f32[16,2,2,8,128]{4,3,2,1,0:T(8,128)S(1)}, f32[16,2,2,8,128]{4,3,2,1,0:T(8,128)S(1)}, u32[]{:S(2)}, u32[]{:S(2)}) %collective-permute-start.1) | collective-permute-done | bytes 262176 | tf_op jit(solution)/shard_map/ppermute | solution.py:342
  36.5 0.0 collective-permute-done.refs_1_.swap
  36.5 5.4 %all-gather = f32[6,16,2,8,128]{4,3,2,1,0:T(8,128)S(1)} all-gather(f32[3,16,2,8,128]{4,3,2,1,0:T(8,128)S(1)} %shard_map.59), channel_id=2, replica_groups=mesh['z'=16,'p'=4,'h'=2,'c'=2,'x'=4] {'c'}, dimensions={0}, use_global_device_ids=true | all-gather | bytes 1179648 | tf_op jit(solution)/shard_map/all_gather | solution.py:356
  42.0 3.1 %shard_map.60 = (f32[8,4,8,128]{3,2,1,0:T(8,128)S(1)}, f32[8,4,8,128]{3,2,1,0:T(8,128)S(1)}, f32[24,4,8,128]{3,2,1,0:T(8,128)S(1)}, f32[24,4,8,128]{3,2,1,0:T(8,...) custom-call(s32[4]{0:T(128)S(1)} %pad_add_fusion.where, ...), custom_call_target="tpu_custom_call" | custom-call | tf_op jit(solution)/shard_map/pallas_call | solution.py:359
  45.1 1.3 %collective-permute-start.3 = (f32[8,4,8,128]{3,2,1,0:T(8,128)S(1)}, f32[8,4,8,128]{3,2,1,0:T(8,128)S(1)}, u32[]{:S(2)}, u32[]{:S(2)}) collective-permute-start(f32[8,4,8,128]{3,2,1,0:T(8,128)S(1)} %get-tuple-element.13.applied), channel_id=1, source_target_pairs={{16,0},{24,8},{32,16},{40,24},{48,32},{56,40},{64,48},{72,56},{80,... | collective-permute-start | bytes 393224 | tf_op jit(solution)/shard_map/ppermute | solution.py:342
  46.4 5.9 %collective-permute-start.2 = (f32[8,4,8,128]{3,2,1,0:T(8,128)S(1)}, f32[8,4,8,128]{3,2,1,0:T(8,128)S(1)}, u32[]{:S(2)}, u32[]{:S(2)}) collective-permute-start(f32[8,4,8,128]{3,2,1,0:T(8,128)S(1)} %get-tuple-element.13.applied), channel_id=1, source_target_pairs={{0,16},{8,24},{16,32},{24,40},{32,48},{40,56},{48,64},{56,72},{64,... | collective-permute-start | bytes 393224 | tf_op jit(solution)/shard_map/ppermute | solution.py:342
  52.3 1.6 %collective-permute-done.3.above = f32[8,4,8,128]{3,2,1,0:T(8,128)S(1)} collective-permute-done((f32[8,4,8,128]{3,2,1,0:T(8,128)S(1)}, f32[8,4,8,128]{3,2,1,0:T(8,128)S(1)}, u32[]{:S(2)}, u32[]{:S(2)}) %collective-permute-start.3) | collective-permute-done | bytes 131104 | tf_op jit(solution)/shard_map/ppermute | solution.py:342
  53.9 0.9 collective-permute-done.2.below
  54.8 2.2 %shard_map.61 = f32[8,3,2,8,128]{4,3,2,1,0:T(8,128)S(1)} custom-call(s32[4]{0:T(128)S(1)} %pad_add_fusion.where, f32[8,4,8,128]{3,2,1,0:T(8,128)S(1)} %get-tuple-element.12.first, f32[8,4,8,128]{3,2,1,0:T(8,128)S(1)} %get-tuple-element.13.applied, f32[8,4,8,128]{3,2,1,0:T(8,128)S(1)} %collective-permute-done.2.below, ...), custom_call_target="tpu_custom_call" | custom-call | tf_op jit(solution)/shard_map/pallas_call | solution.py:369
  57.0 0.0 copy-start
  57.0 9.7 %all_to_all.21 = f32[8,3,2,8,128]{4,3,2,1,0:T(8,128)S(1)} all-to-all(f32[8,3,2,8,128]{4,3,2,1,0:T(8,128)S(1)} %shard_map.61), channel_id=1, replica_groups=mesh['z'=16,'p'=4,'h'=2,'c'=2,'x'=4] {'x','c'}, dimensions={0} | all-to-all | bytes 393216 | tf_op jit(solution)/shard_map/all_to_all | solution.py:377
  66.7 0.0 copy-done
  66.7 0.4 shard_map.62
  67.2 23.7 %all_to_all.22 = f32[64,2,128]{2,1,0:T(2,128)S(1)} all-to-all(f32[64,2,128]{2,1,0:T(2,128)S(1)} %shard_map.62), channel_id=1, replica_groups=mesh['z'=16,'p'=4,'h'=2,'c'=2,'x'=4] {'x','p','h','c'}, dimensions={0} | all-to-all | bytes 131072 | tf_op jit(solution)/shard_map/all_to_all | solution.py:383
  90.9 0.1 reduce_sum.9
  90.9 23.3 %all_to_all.23.sums = f32[16,2,128]{2,1,0:T(2,128)S(1)} all-to-all(f32[16,2,128]{2,1,0:T(2,128)S(1)} %broadcast_in_dim.7), channel_id=1, replica_groups=mesh['z'=16,'p'=4,'h'=2,'c'=2,'x'=4] {'z'}, dimensions={0} | all-to-all | bytes 32768 | tf_op jit(solution)/shard_map/all_to_all | solution.py:385
  114.2 1.5 %shard_map.63 = (f32[128,128]{1,0:T(8,128)}, f32[128,128]{1,0:T(8,128)}, f32[128,128]{1,0:T(8,128)}) custom-call(f32[16,2,128]{2,1,0:T(2,128)S(1)} %all_to_all.23.sums, f32[384,128]{1,0:T(8,128)S(1)} %bitcast.9, f32[128,128]{1,0:T(8,128)S(1)} %bitcast.11), custom_call_target="tpu_custom_call" | custom-call | tf_op jit(solution)/shard_map/pallas_call | solution.py:386
  (3 shorter events, 0.0 us)
Async XLA Ops:
  26.9 9.6 %collective-permute-start.1 = (f32[16,2,2,8,128]{4,3,2,1,0:T(8,128)S(1)}, f32[16,2,2,8,128]{4,3,2,1,0:T(8,128)S(1)}, u32[]{:S(2)}, u32[]{:S(2)}) collective-permute-start(f32[16,2,2,8,128]{4,3,2,1,0:T(8,128)S(1)} %all_to_all.20.refs_0_.own), channel_id=1, source_target_pairs={{16,0},{32,16},{8,24},{48,32},{24,40},{64,48},{40,56},{80,64},{56,... | collective-permute-start | bytes 786440 | tf_op jit(solution)/shard_map/ppermute | solution.py:342
  28.2 8.3 %collective-permute-start = (f32[16,2,2,8,128]{4,3,2,1,0:T(8,128)S(1)}, f32[16,2,2,8,128]{4,3,2,1,0:T(8,128)S(1)}, u32[]{:S(2)}, u32[]{:S(2)}) collective-permute-start(f32[16,2,2,8,128]{4,3,2,1,0:T(8,128)S(1)} %all_to_all.20.refs_0_.own), channel_id=1, source_target_pairs={{16,8},{8,16},{32,24},{24,32},{48,40},{40,48},{64,56},{56,64},{80,... | collective-permute-start | bytes 786440 | tf_op jit(solution)/shard_map/ppermute | solution.py:342
  45.1 8.8 %collective-permute-start.3 = (f32[8,4,8,128]{3,2,1,0:T(8,128)S(1)}, f32[8,4,8,128]{3,2,1,0:T(8,128)S(1)}, u32[]{:S(2)}, u32[]{:S(2)}) collective-permute-start(f32[8,4,8,128]{3,2,1,0:T(8,128)S(1)} %get-tuple-element.13.applied), channel_id=1, source_target_pairs={{16,0},{24,8},{32,16},{40,24},{48,32},{56,40},{64,48},{72,56},{80,... | collective-permute-start | bytes 393224 | tf_op jit(solution)/shard_map/ppermute | solution.py:342
  46.4 8.4 %collective-permute-start.2 = (f32[8,4,8,128]{3,2,1,0:T(8,128)S(1)}, f32[8,4,8,128]{3,2,1,0:T(8,128)S(1)}, u32[]{:S(2)}, u32[]{:S(2)}) collective-permute-start(f32[8,4,8,128]{3,2,1,0:T(8,128)S(1)} %get-tuple-element.13.applied), channel_id=1, source_target_pairs={{0,16},{8,24},{16,32},{24,40},{32,48},{40,56},{48,64},{56,72},{64,... | collective-permute-start | bytes 393224 | tf_op jit(solution)/shard_map/ppermute | solution.py:342
  57.0 9.7 %copy-start = (f32[8,2,8,128]{3,2,1,0:T(8,128)S(1)}, f32[8,2,8,128]{3,2,1,0:T(8,128)}, u32[]{:S(2)}) copy-start(f32[8,2,8,128]{3,2,1,0:T(8,128)} %rhs.1) | copy-start | bytes 196612

commit v8 on v7

--- a/solution.py
+++ b/solution.py
@@ -378,11 +378,11 @@
     rows = rhs.reshape(8 * 16, LANES)
 
     tile = pl.pallas_call(
-        gram_kernel, out_shape=f32(sizes["p"] * 4 * sizes["x"], 2, LANES), in_specs=vmem(2), out_specs=vmem(1)[0], compiler_params=PARAMS
+        gram_kernel, out_shape=f32(sizes["x"] * sizes["z"], 2, LANES), in_specs=vmem(2), out_specs=vmem(1)[0], compiler_params=PARAMS
     )(parts, rows)
-    tile = lax.all_to_all(tile, ("x", "p", "h", "c"), 0, 0).sum(0)
-    tile = jnp.broadcast_to(tile, (sizes["z"], 2, LANES))
-    tile = lax.all_to_all(tile, "z", 0, 0)
+    tile = lax.all_to_all(tile, ("x", "z"), 0, 0).sum(0)
+    tile = jnp.broadcast_to(tile, (sizes["p"] * 4, 2, LANES))
+    tile = lax.all_to_all(tile, ("p", "h", "c"), 0, 0)
     outs = pl.pallas_call(
         final_kernel,
         out_shape=[f32(128, LANES)] * 3,

time: 116 us -> 118 us (1.017)
  blocking collectives: 86.8 us -> 88.3 us
    all_to_all x2, blocking collectives: 47 us -> 48.4 us  [the longest x1 34.8 us: local(): tile = lax.all_to_all(tile, ('x', 'z'), 0, 0).sum(0)]
where the time goes in v8:
time: 118 us; the launch traced here: 117 us
  blocking collectives  88.3 us (75%)
  waiting for transfers between devices  10 us (8%)
  starting transfers between devices  9.15 us (8%)
  Pallas kernels  8.92 us (8%)
    all_to_all x1, blocking collectives, local(): tile = lax.all_to_all(tile, ('x', 'z'), 0, 0).sum(0)  34.8 us
    all_to_all x1, blocking collectives, local(): own = lax.all_to_all(packed, ('x', 'h', 'c'), 0, 0)  24.7 us
    all_to_all x1, blocking collectives, local(): tile = lax.all_to_all(tile, ('p', 'h', 'c'), 0, 0)  13.6 us
    ppermute x4, waiting for transfers between devices, moved(): lax.ppermute(v, chip, [(s, i) for i, s in enumerate(sources) if 0 <= s <...  10 us
    all_to_all x1, blocking collectives, local(): parts = lax.all_to_all(results, ('x', 'c'), 0, 0).reshape(8 * 48, LANES)  9.72 us
    ppermute x4, starting transfers between devices, moved(): lax.ppermute(v, chip, [(s, i) for i, s in enumerate(sources) if 0 <= s <...  9.15 us
    all_gather x1, blocking collectives, both_cores(): return lax.all_gather(grids, 'c')  5.44 us
    pallas_call x1, Pallas kernels, local(): pl.pallas_call(first_kernel, out_shape=[f32(8, *TILE)] * 2 + [f32(24, *TI...  3.13 us
  transfers between devices with their start and end apart: 4, of which 3 were waited for; matrix products, arithmetic and copies ran while one was open for 0% of the time, Pallas kernels for 0%

profile of v8, /device:TPU:1, one launch (start us, length us, event | category | flops | bytes accessed | tf_op | source)
XLA Modules:
  0.0 117.2 jit_solution(15895358321935944219)
XLA Ops:
  0.6 1.6 %shard_map.58 = f32[16,2,2,8,128]{4,3,2,1,0:T(8,128)} custom-call(f32[8,2,8,128]{3,2,1,0:T(8,128)} %rhs.1, s32[2,8,128]{2,1,0:T(8,128)} %classes.1, s32[2,8,128]{2,1,0:T(8,128)} %supports.1), custom_call_target="tpu_custom_call" | custom-call | tf_op jit(solution)/shard_map/pallas_call | solution.py:326
  2.2 24.7 %all_to_all.20.refs_0_.own = f32[16,2,2,8,128]{4,3,2,1,0:T(8,128)S(1)} all-to-all(f32[16,2,2,8,128]{4,3,2,1,0:T(8,128)} %shard_map.58), channel_id=1, replica_groups=mesh['z'=16,'p'=4,'h'=2,'c'=2,'x'=4] {'x','h','c'}, dimensions={0} | all-to-all | bytes 524288 | tf_op jit(solution)/shard_map/all_to_all | solution.py:339
  26.9 1.3 %collective-permute-start.1 = (f32[16,2,2,8,128]{4,3,2,1,0:T(8,128)S(1)}, f32[16,2,2,8,128]{4,3,2,1,0:T(8,128)S(1)}, u32[]{:S(2)}, u32[]{:S(2)}) collective-permute-start(f32[16,2,2,8,128]{4,3,2,1,0:T(8,128)S(1)} %all_to_all.20.refs_0_.own), channel_id=1, source_target_pairs={{16,0},{32,16},{8,24},{48,32},{24,40},{64,48},{40,56},{80,64},{56,... | collective-permute-start | bytes 786440 | tf_op jit(solution)/shard_map/ppermute | solution.py:342
  28.2 0.7 collective-permute-start
  28.9 0.1 pad_add_fusion.where
  29.0 7.5 %collective-permute-done.1.refs_2_.far = f32[16,2,2,8,128]{4,3,2,1,0:T(8,128)S(1)} collective-permute-done((f32[16,2,2,8,128]{4,3,2,1,0:T(8,128)S(1)}, f32[16,2,2,8,128]{4,3,2,1,0:T(8,128)S(1)}, u32[]{:S(2)}, u32[]{:S(2)}) %collective-permute-start.1) | collective-permute-done | bytes 262176 | tf_op jit(solution)/shard_map/ppermute | solution.py:342
  36.5 0.0 collective-permute-done.refs_1_.swap
  36.5 5.4 %all-gather = f32[6,16,2,8,128]{4,3,2,1,0:T(8,128)S(1)} all-gather(f32[3,16,2,8,128]{4,3,2,1,0:T(8,128)S(1)} %shard_map.59), channel_id=2, replica_groups=mesh['z'=16,'p'=4,'h'=2,'c'=2,'x'=4] {'c'}, dimensions={0}, use_global_device_ids=true | all-gather | bytes 1179648 | tf_op jit(solution)/shard_map/all_gather | solution.py:356
  42.0 3.1 %shard_map.60 = (f32[8,4,8,128]{3,2,1,0:T(8,128)S(1)}, f32[8,4,8,128]{3,2,1,0:T(8,128)S(1)}, f32[24,4,8,128]{3,2,1,0:T(8,128)S(1)}, f32[24,4,8,128]{3,2,1,0:T(8,...) custom-call(s32[4]{0:T(128)S(1)} %pad_add_fusion.where, ...), custom_call_target="tpu_custom_call" | custom-call | tf_op jit(solution)/shard_map/pallas_call | solution.py:359
  45.1 1.3 %collective-permute-start.3 = (f32[8,4,8,128]{3,2,1,0:T(8,128)S(1)}, f32[8,4,8,128]{3,2,1,0:T(8,128)S(1)}, u32[]{:S(2)}, u32[]{:S(2)}) collective-permute-start(f32[8,4,8,128]{3,2,1,0:T(8,128)S(1)} %get-tuple-element.13.applied), channel_id=1, source_target_pairs={{16,0},{24,8},{32,16},{40,24},{48,32},{56,40},{64,48},{72,56},{80,... | collective-permute-start | bytes 393224 | tf_op jit(solution)/shard_map/ppermute | solution.py:342
  46.4 5.9 %collective-permute-start.2 = (f32[8,4,8,128]{3,2,1,0:T(8,128)S(1)}, f32[8,4,8,128]{3,2,1,0:T(8,128)S(1)}, u32[]{:S(2)}, u32[]{:S(2)}) collective-permute-start(f32[8,4,8,128]{3,2,1,0:T(8,128)S(1)} %get-tuple-element.13.applied), channel_id=1, source_target_pairs={{0,16},{8,24},{16,32},{24,40},{32,48},{40,56},{48,64},{56,72},{64,... | collective-permute-start | bytes 393224 | tf_op jit(solution)/shard_map/ppermute | solution.py:342
  52.3 1.6 %collective-permute-done.3.above = f32[8,4,8,128]{3,2,1,0:T(8,128)S(1)} collective-permute-done((f32[8,4,8,128]{3,2,1,0:T(8,128)S(1)}, f32[8,4,8,128]{3,2,1,0:T(8,128)S(1)}, u32[]{:S(2)}, u32[]{:S(2)}) %collective-permute-start.3) | collective-permute-done | bytes 131104 | tf_op jit(solution)/shard_map/ppermute | solution.py:342
  53.9 0.9 collective-permute-done.2.below
  54.8 2.2 %shard_map.61 = f32[8,3,2,8,128]{4,3,2,1,0:T(8,128)S(1)} custom-call(s32[4]{0:T(128)S(1)} %pad_add_fusion.where, f32[8,4,8,128]{3,2,1,0:T(8,128)S(1)} %get-tuple-element.12.first, f32[8,4,8,128]{3,2,1,0:T(8,128)S(1)} %get-tuple-element.13.applied, f32[8,4,8,128]{3,2,1,0:T(8,128)S(1)} %collective-permute-done.2.below, ...), custom_call_target="tpu_custom_call" | custom-call | tf_op jit(solution)/shard_map/pallas_call | solution.py:369
  57.0 0.0 copy-start
  57.0 9.7 %all_to_all.21 = f32[8,3,2,8,128]{4,3,2,1,0:T(8,128)S(1)} all-to-all(f32[8,3,2,8,128]{4,3,2,1,0:T(8,128)S(1)} %shard_map.61), channel_id=1, replica_groups=mesh['z'=16,'p'=4,'h'=2,'c'=2,'x'=4] {'x','c'}, dimensions={0} | all-to-all | bytes 393216 | tf_op jit(solution)/shard_map/all_to_all | solution.py:377
  66.7 0.0 copy-done
  66.7 0.4 shard_map.62
  67.2 34.8 %all_to_all.22 = f32[64,2,128]{2,1,0:T(2,128)S(1)} all-to-all(f32[64,2,128]{2,1,0:T(2,128)S(1)} %shard_map.62), channel_id=1, replica_groups=mesh['z'=16,'p'=4,'h'=2,'c'=2,'x'=4] {'x','z'}, dimensions={0} | all-to-all | bytes 131072 | tf_op jit(solution)/shard_map/all_to_all | solution.py:383
  102.0 0.1 reduce_sum.9
  102.1 13.6 %all_to_all.23.sums = f32[16,2,128]{2,1,0:T(2,128)S(1)} all-to-all(f32[16,2,128]{2,1,0:T(2,128)S(1)} %broadcast_in_dim.7), channel_id=1, replica_groups=mesh['z'=16,'p'=4,'h'=2,'c'=2,'x'=4] {'p','h','c'}, dimensions={0} | all-to-all | bytes 32768 | tf_op jit(solution)/shard_map/all_to_all | solution.py:385
  115.7 1.5 %shard_map.63 = (f32[128,128]{1,0:T(8,128)}, f32[128,128]{1,0:T(8,128)}, f32[128,128]{1,0:T(8,128)}) custom-call(f32[16,2,128]{2,1,0:T(2,128)S(1)} %all_to_all.23.sums, f32[384,128]{1,0:T(8,128)S(1)} %bitcast.9, f32[128,128]{1,0:T(8,128)S(1)} %bitcast.11), custom_call_target="tpu_custom_call" | custom-call | tf_op jit(solution)/shard_map/pallas_call | solution.py:386
  (3 shorter events, 0.0 us)
Async XLA Ops:
  26.9 9.6 %collective-permute-start.1 = (f32[16,2,2,8,128]{4,3,2,1,0:T(8,128)S(1)}, f32[16,2,2,8,128]{4,3,2,1,0:T(8,128)S(1)}, u32[]{:S(2)}, u32[]{:S(2)}) collective-permute-start(f32[16,2,2,8,128]{4,3,2,1,0:T(8,128)S(1)} %all_to_all.20.refs_0_.own), channel_id=1, source_target_pairs={{16,0},{32,16},{8,24},{48,32},{24,40},{64,48},{40,56},{80,64},{56,... | collective-permute-start | bytes 786440 | tf_op jit(solution)/shard_map/ppermute | solution.py:342
  28.2 8.3 %collective-permute-start = (f32[16,2,2,8,128]{4,3,2,1,0:T(8,128)S(1)}, f32[16,2,2,8,128]{4,3,2,1,0:T(8,128)S(1)}, u32[]{:S(2)}, u32[]{:S(2)}) collective-permute-start(f32[16,2,2,8,128]{4,3,2,1,0:T(8,128)S(1)} %all_to_all.20.refs_0_.own), channel_id=1, source_target_pairs={{16,8},{8,16},{32,24},{24,32},{48,40},{40,48},{64,56},{56,64},{80,... | collective-permute-start | bytes 786440 | tf_op jit(solution)/shard_map/ppermute | solution.py:342
  45.1 8.8 %collective-permute-start.3 = (f32[8,4,8,128]{3,2,1,0:T(8,128)S(1)}, f32[8,4,8,128]{3,2,1,0:T(8,128)S(1)}, u32[]{:S(2)}, u32[]{:S(2)}) collective-permute-start(f32[8,4,8,128]{3,2,1,0:T(8,128)S(1)} %get-tuple-element.13.applied), channel_id=1, source_target_pairs={{16,0},{24,8},{32,16},{40,24},{48,32},{56,40},{64,48},{72,56},{80,... | collective-permute-start | bytes 393224 | tf_op jit(solution)/shard_map/ppermute | solution.py:342
  46.4 8.4 %collective-permute-start.2 = (f32[8,4,8,128]{3,2,1,0:T(8,128)S(1)}, f32[8,4,8,128]{3,2,1,0:T(8,128)S(1)}, u32[]{:S(2)}, u32[]{:S(2)}) collective-permute-start(f32[8,4,8,128]{3,2,1,0:T(8,128)S(1)} %get-tuple-element.13.applied), channel_id=1, source_target_pairs={{0,16},{8,24},{16,32},{24,40},{32,48},{40,56},{48,64},{56,72},{64,... | collective-permute-start | bytes 393224 | tf_op jit(solution)/shard_map/ppermute | solution.py:342
  57.0 9.7 %copy-start = (f32[8,2,8,128]{3,2,1,0:T(8,128)S(1)}, f32[8,2,8,128]{3,2,1,0:T(8,128)}, u32[]{:S(2)}) copy-start(f32[8,2,8,128]{3,2,1,0:T(8,128)} %rhs.1) | copy-start | bytes 196612

commit v9 on v7

--- a/solution.py
+++ b/solution.py
@@ -18,10 +18,6 @@
 
 def vmem(n):
     return [pl.BlockSpec(memory_space=pltpu.VMEM)] * n
-
-
-def smem():
-    return [pl.BlockSpec(memory_space=pltpu.SMEM)]
 
 
 def iota(axis, shape=TILE):
@@ -181,6 +177,11 @@
                 out[(x * 2 + h) * 2 + c, 1] = v
 
 
+def my_place():
+    pair = lax.axis_index("z") * lax.axis_size("p") + lax.axis_index("p")
+    return lax.axis_index("h"), pair, lax.axis_size("z") * lax.axis_size("p")
+
+
 def grids_kernel(*refs):
     *blocks, out = refs
     for i, ref in enumerate(blocks):
@@ -189,9 +190,11 @@
 
 
 def first_kernel(
-    where, own, swap, far, grids, first, applied, s16_out, sp8_out, dv_out, steps_out, out, source_ref, *work
+    own, swap, far, grids, first, applied, s16_out, sp8_out, dv_out, steps_out, out, source_ref, *work
 ):
-    upper_chip = where[0] != 0
+    h, pair, pairs = my_place()
+    upper_chip = h != 0
+    present = (pair > 0, pair >= 0, pair < pairs - 1)
 
     def plane(refs, p):
         q = p % 8
@@ -218,7 +221,7 @@
         if sums is not None:
             n = p - 1
             d = sp8(n) + (sums + t) * (1.0 / 3.0)
-            ok = where[1 + (n + 8) // 8] != 0
+            ok = present[(n + 8) // 8]
             dv.put(n, jnp.where(ok, OMEGA / d, 0.0))
             if n % 2 and n > -7:
                 steps.put(n // 2, jnp.where(ok, DAMP / pair_sum(kept + d), 0.0))
@@ -235,14 +238,15 @@
         applied[p] = v
 
 
-def second_kernel(where, first, applied, below, above, s16_ref, sp8_ref, dv_ref, steps_ref, packed, source_ref, *work):
-    shift = where[0] * 4
+def second_kernel(first, applied, below, above, s16_ref, sp8_ref, dv_ref, steps_ref, packed, source_ref, *work):
+    h, _, _ = my_place()
+    shift = h * 4
     for q in range(8):
         source_ref[q] = below[q]
         source_ref[8 + q] = applied[q]
         source_ref[16 + q] = above[q]
     source, s16, sp8, dv = (Planes(r, -8, shift) for r in (source_ref, s16_ref, sp8_ref, dv_ref))
-    steps = Planes(steps_ref, -4, where[0] * 2)
+    steps = Planes(steps_ref, -4, h * 2)
 
     def put(field, p, v):
         for x in range(4):
@@ -317,10 +321,6 @@
 def local(rhs, classes, supports):
     sizes = {a: lax.axis_size(a) for a in ("z", "p", "h", "c", "x")}
     chips = sizes["z"] * sizes["p"] * 2
-    upper_chip = lax.axis_index("h")
-    pair = lax.axis_index("z") * sizes["p"] + lax.axis_index("p") + jnp.arange(-1, 2, dtype=jnp.int32)
-    present = ((pair >= 0) & (pair < chips // 2)).astype(jnp.int32)
-    where = jnp.concatenate([upper_chip[None].astype(jnp.int32), present])
     chip = ("z", "p", "h")
 
     packed = pl.pallas_call(
@@ -359,21 +359,21 @@
     first, applied, *coefs = pl.pallas_call(
         first_kernel,
         out_shape=[f32(8, *TILE)] * 2 + [f32(24, *TILE)] * 3 + [f32(12, *TILE)],
-        in_specs=smem() + vmem(4),
+        in_specs=vmem(4),
         out_specs=vmem(6),
         scratch_shapes=[pltpu.VMEM((10, *TILE), jnp.float32), pltpu.VMEM((24, *TILE), jnp.float32)] + work_shapes(),
         compiler_params=PARAMS,
-    )(where, own, swap, far, grids)
+    )(own, swap, far, grids)
     below = moved(applied, [i - 2 for i in range(chips)])
     above = moved(applied, [i + 2 for i in range(chips)])
     results = pl.pallas_call(
         second_kernel,
         out_shape=f32(8, 3, 2, 8, LANES),
-        in_specs=smem() + vmem(8),
+        in_specs=vmem(8),
         out_specs=vmem(1)[0],
         scratch_shapes=[pltpu.VMEM((24, *TILE), jnp.float32)] + work_shapes(),
         compiler_params=PARAMS,
-    )(where, first, applied, below, above, *coefs)
+    )(first, applied, below, above, *coefs)
     parts = lax.all_to_all(results, ("x", "c"), 0, 0).reshape(8 * 48, LANES)
     rows = rhs.reshape(8 * 16, LANES)
 

time: 116 us -> 115 us (level)
  Pallas kernels: 8.92 us -> 7.74 us
where the time goes in v9:
time: 115 us
  blocking collectives  86.8 us (75%)
  waiting for transfers between devices  10.1 us (9%)
  starting transfers between devices  9.15 us (8%)
  Pallas kernels  7.74 us (7%)
    all_to_all x1, blocking collectives, local(): own = lax.all_to_all(packed, ('x', 'h', 'c'), 0, 0)  24.7 us
    all_to_all x1, blocking collectives, local(): tile = lax.all_to_all(tile, ('x', 'p', 'h', 'c'), 0, 0).sum(0)  23.7 us
    all_to_all x1, blocking collectives, local(): tile = lax.all_to_all(tile, 'z', 0, 0)  23.3 us
    ppermute x4, waiting for transfers between devices, moved(): lax.ppermute(v, chip, [(s, i) for i, s in enumerate(sources) if 0 <= s <...  10.1 us
    all_to_all x1, blocking collectives, local(): parts = lax.all_to_all(results, ('x', 'c'), 0, 0).reshape(8 * 48, LANES)  9.72 us
    ppermute x4, starting transfers between devices, moved(): lax.ppermute(v, chip, [(s, i) for i, s in enumerate(sources) if 0 <= s <...  9.15 us
    all_gather x1, blocking collectives, both_cores(): return lax.all_gather(grids, 'c')  5.44 us
    pallas_call x1, Pallas kernels, local(): pl.pallas_call(first_kernel, out_shape=[f32(8, *TILE)] * 2 + [f32(24, *TI...  2.51 us
  transfers between devices with their start and end apart: 4, of which 3 were waited for; matrix products, arithmetic and copies ran while one was open for 0% of the time, Pallas kernels for 0%

profile of v9, /device:TPU:1, one launch (start us, length us, event | category | flops | bytes accessed | tf_op | source)
XLA Modules:
  0.0 114.6 jit_solution(16002441288487493901)
XLA Ops:
  0.6 1.6 %shard_map.58 = f32[16,2,2,8,128]{4,3,2,1,0:T(8,128)} custom-call(f32[8,2,8,128]{3,2,1,0:T(8,128)} %rhs.1, s32[2,8,128]{2,1,0:T(8,128)} %classes.1, s32[2,8,128]{2,1,0:T(8,128)} %supports.1), custom_call_target="tpu_custom_call" | custom-call | tf_op jit(solution)/shard_map/pallas_call | solution.py:326
  2.2 24.7 %all_to_all.20.refs_0_.own = f32[16,2,2,8,128]{4,3,2,1,0:T(8,128)S(1)} all-to-all(f32[16,2,2,8,128]{4,3,2,1,0:T(8,128)} %shard_map.58), channel_id=1, replica_groups=mesh['z'=16,'p'=4,'h'=2,'c'=2,'x'=4] {'x','h','c'}, dimensions={0} | all-to-all | bytes 524288 | tf_op jit(solution)/shard_map/all_to_all | solution.py:339
  26.9 1.3 %collective-permute-start.1 = (f32[16,2,2,8,128]{4,3,2,1,0:T(8,128)S(1)}, f32[16,2,2,8,128]{4,3,2,1,0:T(8,128)S(1)}, u32[]{:S(2)}, u32[]{:S(2)}) collective-permute-start(f32[16,2,2,8,128]{4,3,2,1,0:T(8,128)S(1)} %all_to_all.20.refs_0_.own), channel_id=1, source_target_pairs={{16,0},{32,16},{8,24},{48,32},{24,40},{64,48},{40,56},{80,64},{56,... | collective-permute-start | bytes 786440 | tf_op jit(solution)/shard_map/ppermute | solution.py:342
  28.2 0.7 collective-permute-start
  28.9 7.6 %collective-permute-done.1.refs_2_.far = f32[16,2,2,8,128]{4,3,2,1,0:T(8,128)S(1)} collective-permute-done((f32[16,2,2,8,128]{4,3,2,1,0:T(8,128)S(1)}, f32[16,2,2,8,128]{4,3,2,1,0:T(8,128)S(1)}, u32[]{:S(2)}, u32[]{:S(2)}) %collective-permute-start.1) | collective-permute-done | bytes 262176 | tf_op jit(solution)/shard_map/ppermute | solution.py:342
  36.5 0.0 collective-permute-done.refs_1_.swap
  36.5 5.4 %all-gather = f32[6,16,2,8,128]{4,3,2,1,0:T(8,128)S(1)} all-gather(f32[3,16,2,8,128]{4,3,2,1,0:T(8,128)S(1)} %shard_map.59), channel_id=2, replica_groups=mesh['z'=16,'p'=4,'h'=2,'c'=2,'x'=4] {'c'}, dimensions={0}, use_global_device_ids=true | all-gather | bytes 1179648 | tf_op jit(solution)/shard_map/all_gather | solution.py:356
  42.0 2.5 %shard_map.60 = (f32[8,4,8,128]{3,2,1,0:T(8,128)S(1)}, f32[8,4,8,128]{3,2,1,0:T(8,128)S(1)}, f32[24,4,8,128]{3,2,1,0:T(8,128)S(1)}, f32[24,4,8,128]{3,2,1,0:T(8,...) custom-call(f32[16,2,2,8,128]{4,3,2,1,0:T(8,128)S(1)} %all_to_all.20.refs_0_.own, ...), custom_call_target="tpu_custom_call" | custom-call | tf_op jit(solution)/shard_map/pallas_call | solution.py:359
  44.5 1.3 %collective-permute-start.3 = (f32[8,4,8,128]{3,2,1,0:T(8,128)S(1)}, f32[8,4,8,128]{3,2,1,0:T(8,128)S(1)}, u32[]{:S(2)}, u32[]{:S(2)}) collective-permute-start(f32[8,4,8,128]{3,2,1,0:T(8,128)S(1)} %get-tuple-element.13.applied), channel_id=1, source_target_pairs={{16,0},{24,8},{32,16},{40,24},{48,32},{56,40},{64,48},{72,56},{80,... | collective-permute-start | bytes 393224 | tf_op jit(solution)/shard_map/ppermute | solution.py:342
  45.8 5.9 %collective-permute-start.2 = (f32[8,4,8,128]{3,2,1,0:T(8,128)S(1)}, f32[8,4,8,128]{3,2,1,0:T(8,128)S(1)}, u32[]{:S(2)}, u32[]{:S(2)}) collective-permute-start(f32[8,4,8,128]{3,2,1,0:T(8,128)S(1)} %get-tuple-element.13.applied), channel_id=1, source_target_pairs={{0,16},{8,24},{16,32},{24,40},{32,48},{40,56},{48,64},{56,72},{64,... | collective-permute-start | bytes 393224 | tf_op jit(solution)/shard_map/ppermute | solution.py:342
  51.7 1.6 %collective-permute-done.3.above = f32[8,4,8,128]{3,2,1,0:T(8,128)S(1)} collective-permute-done((f32[8,4,8,128]{3,2,1,0:T(8,128)S(1)}, f32[8,4,8,128]{3,2,1,0:T(8,128)S(1)}, u32[]{:S(2)}, u32[]{:S(2)}) %collective-permute-start.3) | collective-permute-done | bytes 131104 | tf_op jit(solution)/shard_map/ppermute | solution.py:342
  53.3 0.9 collective-permute-done.2.below
  54.2 1.6 %shard_map.61 = f32[8,3,2,8,128]{4,3,2,1,0:T(8,128)S(1)} custom-call(f32[8,4,8,128]{3,2,1,0:T(8,128)S(1)} %get-tuple-element.12.first, f32[8,4,8,128]{3,2,1,0:T(8,128)S(1)} %get-tuple-element.13.applied, f32[8,4,8,128]{3,2,1,0:T(8,128)S(1)} %collective-permute-done.2.below, f32[8,4,8,128]{3,2,1,0:T(8,128)S(1)} %collective-permute-done.3.above, ...), custom_call_target="tpu_custom_call" | custom-call | tf_op jit(solution)/shard_map/pallas_call | solution.py:369
  55.8 0.0 copy-start
  55.8 9.7 %all_to_all.21 = f32[8,3,2,8,128]{4,3,2,1,0:T(8,128)S(1)} all-to-all(f32[8,3,2,8,128]{4,3,2,1,0:T(8,128)S(1)} %shard_map.61), channel_id=1, replica_groups=mesh['z'=16,'p'=4,'h'=2,'c'=2,'x'=4] {'x','c'}, dimensions={0} | all-to-all | bytes 393216 | tf_op jit(solution)/shard_map/all_to_all | solution.py:377
  65.5 0.0 copy-done
  65.5 0.4 shard_map.62
  66.0 23.7 %all_to_all.22 = f32[64,2,128]{2,1,0:T(2,128)S(1)} all-to-all(f32[64,2,128]{2,1,0:T(2,128)S(1)} %shard_map.62), channel_id=1, replica_groups=mesh['z'=16,'p'=4,'h'=2,'c'=2,'x'=4] {'x','p','h','c'}, dimensions={0} | all-to-all | bytes 131072 | tf_op jit(solution)/shard_map/all_to_all | solution.py:383
  89.7 0.1 reduce_sum.9
  89.8 23.3 %all_to_all.23.sums = f32[16,2,128]{2,1,0:T(2,128)S(1)} all-to-all(f32[16,2,128]{2,1,0:T(2,128)S(1)} %broadcast_in_dim.3), channel_id=1, replica_groups=mesh['z'=16,'p'=4,'h'=2,'c'=2,'x'=4] {'z'}, dimensions={0} | all-to-all | bytes 32768 | tf_op jit(solution)/shard_map/all_to_all | solution.py:385
  113.0 1.6 %shard_map.63 = (f32[128,128]{1,0:T(8,128)}, f32[128,128]{1,0:T(8,128)}, f32[128,128]{1,0:T(8,128)}) custom-call(f32[16,2,128]{2,1,0:T(2,128)S(1)} %all_to_all.23.sums, f32[384,128]{1,0:T(8,128)S(1)} %bitcast.8, f32[128,128]{1,0:T(8,128)S(1)} %bitcast.10), custom_call_target="tpu_custom_call" | custom-call | tf_op jit(solution)/shard_map/pallas_call | solution.py:386
  (2 shorter events, 0.0 us)
Async XLA Ops:
  26.9 9.6 %collective-permute-start.1 = (f32[16,2,2,8,128]{4,3,2,1,0:T(8,128)S(1)}, f32[16,2,2,8,128]{4,3,2,1,0:T(8,128)S(1)}, u32[]{:S(2)}, u32[]{:S(2)}) collective-permute-start(f32[16,2,2,8,128]{4,3,2,1,0:T(8,128)S(1)} %all_to_all.20.refs_0_.own), channel_id=1, source_target_pairs={{16,0},{32,16},{8,24},{48,32},{24,40},{64,48},{40,56},{80,64},{56,... | collective-permute-start | bytes 786440 | tf_op jit(solution)/shard_map/ppermute | solution.py:342
  28.2 8.3 %collective-permute-start = (f32[16,2,2,8,128]{4,3,2,1,0:T(8,128)S(1)}, f32[16,2,2,8,128]{4,3,2,1,0:T(8,128)S(1)}, u32[]{:S(2)}, u32[]{:S(2)}) collective-permute-start(f32[16,2,2,8,128]{4,3,2,1,0:T(8,128)S(1)} %all_to_all.20.refs_0_.own), channel_id=1, source_target_pairs={{16,8},{8,16},{32,24},{24,32},{48,40},{40,48},{64,56},{56,64},{80,... | collective-permute-start | bytes 786440 | tf_op jit(solution)/shard_map/ppermute | solution.py:342
  44.5 8.8 %collective-permute-start.3 = (f32[8,4,8,128]{3,2,1,0:T(8,128)S(1)}, f32[8,4,8,128]{3,2,1,0:T(8,128)S(1)}, u32[]{:S(2)}, u32[]{:S(2)}) collective-permute-start(f32[8,4,8,128]{3,2,1,0:T(8,128)S(1)} %get-tuple-element.13.applied), channel_id=1, source_target_pairs={{16,0},{24,8},{32,16},{40,24},{48,32},{56,40},{64,48},{72,56},{80,... | collective-permute-start | bytes 393224 | tf_op jit(solution)/shard_map/ppermute | solution.py:342
  45.8 8.4 %collective-permute-start.2 = (f32[8,4,8,128]{3,2,1,0:T(8,128)S(1)}, f32[8,4,8,128]{3,2,1,0:T(8,128)S(1)}, u32[]{:S(2)}, u32[]{:S(2)}) collective-permute-start(f32[8,4,8,128]{3,2,1,0:T(8,128)S(1)} %get-tuple-element.13.applied), channel_id=1, source_target_pairs={{0,16},{8,24},{16,32},{24,40},{32,48},{40,56},{48,64},{56,72},{64,... | collective-permute-start | bytes 393224 | tf_op jit(solution)/shard_map/ppermute | solution.py:342
  55.8 9.7 %copy-start = (f32[8,2,8,128]{3,2,1,0:T(8,128)S(1)}, f32[8,2,8,128]{3,2,1,0:T(8,128)}, u32[]{:S(2)}) copy-start(f32[8,2,8,128]{3,2,1,0:T(8,128)} %rhs.1) | copy-start | bytes 196612

commit v10 on v9

--- a/solution.py
+++ b/solution.py
@@ -380,7 +380,7 @@
     tile = pl.pallas_call(
         gram_kernel, out_shape=f32(sizes["p"] * 4 * sizes["x"], 2, LANES), in_specs=vmem(2), out_specs=vmem(1)[0], compiler_params=PARAMS
     )(parts, rows)
-    tile = lax.all_to_all(tile, ("x", "p", "h", "c"), 0, 0).sum(0)
+    tile = lax.all_to_all(tile, ("p", "h", "c", "x"), 0, 0).sum(0)
     tile = jnp.broadcast_to(tile, (sizes["z"], 2, LANES))
     tile = lax.all_to_all(tile, "z", 0, 0)
     outs = pl.pallas_call(

time: 115 us -> 115 us (level)
  no operation moved by 1% of the time
where the time goes in v10:
time: 115 us; the launch traced here: 114 us
  blocking collectives  86.3 us (75%)
  waiting for transfers between devices  10.1 us (9%)
  starting transfers between devices  9.15 us (8%)
  Pallas kernels  7.73 us (7%)
    all_to_all x1, blocking collectives, local(): own = lax.all_to_all(packed, ('x', 'h', 'c'), 0, 0)  24.7 us
    all_to_all x1, blocking collectives, local(): tile = lax.all_to_all(tile, 'z', 0, 0)  23.3 us
    all_to_all x1, blocking collectives, local(): tile = lax.all_to_all(tile, ('p', 'h', 'c', 'x'), 0, 0).sum(0)  23.2 us
    ppermute x4, waiting for transfers between devices, moved(): lax.ppermute(v, chip, [(s, i) for i, s in enumerate(sources) if 0 <= s <...  10.1 us
    all_to_all x1, blocking collectives, local(): parts = lax.all_to_all(results, ('x', 'c'), 0, 0).reshape(8 * 48, LANES)  9.72 us
    ppermute x4, starting transfers between devices, moved(): lax.ppermute(v, chip, [(s, i) for i, s in enumerate(sources) if 0 <= s <...  9.15 us
    all_gather x1, blocking collectives, both_cores(): return lax.all_gather(grids, 'c')  5.44 us
    pallas_call x1, Pallas kernels, local(): pl.pallas_call(first_kernel, out_shape=[f32(8, *TILE)] * 2 + [f32(24, *TI...  2.51 us
  transfers between devices with their start and end apart: 4, of which 3 were waited for; matrix products, arithmetic and copies ran while one was open for 0% of the time, Pallas kernels for 0%

profile of v10, /device:TPU:1, one launch (start us, length us, event | category | flops | bytes accessed | tf_op | source)
XLA Modules:
  0.0 114.1 jit_solution(12819493740654068409)
XLA Ops:
  0.6 1.6 %shard_map.58 = f32[16,2,2,8,128]{4,3,2,1,0:T(8,128)} custom-call(f32[8,2,8,128]{3,2,1,0:T(8,128)} %rhs.1, s32[2,8,128]{2,1,0:T(8,128)} %classes.1, s32[2,8,128]{2,1,0:T(8,128)} %supports.1), custom_call_target="tpu_custom_call" | custom-call | tf_op jit(solution)/shard_map/pallas_call | solution.py:326
  2.2 24.7 %all_to_all.20.refs_0_.own = f32[16,2,2,8,128]{4,3,2,1,0:T(8,128)S(1)} all-to-all(f32[16,2,2,8,128]{4,3,2,1,0:T(8,128)} %shard_map.58), channel_id=1, replica_groups=mesh['z'=16,'p'=4,'h'=2,'c'=2,'x'=4] {'x','h','c'}, dimensions={0} | all-to-all | bytes 524288 | tf_op jit(solution)/shard_map/all_to_all | solution.py:339
  26.9 1.3 %collective-permute-start.1 = (f32[16,2,2,8,128]{4,3,2,1,0:T(8,128)S(1)}, f32[16,2,2,8,128]{4,3,2,1,0:T(8,128)S(1)}, u32[]{:S(2)}, u32[]{:S(2)}) collective-permute-start(f32[16,2,2,8,128]{4,3,2,1,0:T(8,128)S(1)} %all_to_all.20.refs_0_.own), channel_id=1, source_target_pairs={{16,0},{32,16},{8,24},{48,32},{24,40},{64,48},{40,56},{80,64},{56,... | collective-permute-start | bytes 786440 | tf_op jit(solution)/shard_map/ppermute | solution.py:342
  28.2 0.7 collective-permute-start
  28.9 7.6 %collective-permute-done.1.refs_2_.far = f32[16,2,2,8,128]{4,3,2,1,0:T(8,128)S(1)} collective-permute-done((f32[16,2,2,8,128]{4,3,2,1,0:T(8,128)S(1)}, f32[16,2,2,8,128]{4,3,2,1,0:T(8,128)S(1)}, u32[]{:S(2)}, u32[]{:S(2)}) %collective-permute-start.1) | collective-permute-done | bytes 262176 | tf_op jit(solution)/shard_map/ppermute | solution.py:342
  36.5 0.0 collective-permute-done.refs_1_.swap
  36.5 5.4 %all-gather = f32[6,16,2,8,128]{4,3,2,1,0:T(8,128)S(1)} all-gather(f32[3,16,2,8,128]{4,3,2,1,0:T(8,128)S(1)} %shard_map.59), channel_id=2, replica_groups=mesh['z'=16,'p'=4,'h'=2,'c'=2,'x'=4] {'c'}, dimensions={0}, use_global_device_ids=true | all-gather | bytes 1179648 | tf_op jit(solution)/shard_map/all_gather | solution.py:356
  42.0 2.5 %shard_map.60 = (f32[8,4,8,128]{3,2,1,0:T(8,128)S(1)}, f32[8,4,8,128]{3,2,1,0:T(8,128)S(1)}, f32[24,4,8,128]{3,2,1,0:T(8,128)S(1)}, f32[24,4,8,128]{3,2,1,0:T(8,...) custom-call(f32[16,2,2,8,128]{4,3,2,1,0:T(8,128)S(1)} %all_to_all.20.refs_0_.own, ...), custom_call_target="tpu_custom_call" | custom-call | tf_op jit(solution)/shard_map/pallas_call | solution.py:359
  44.5 1.3 %collective-permute-start.3 = (f32[8,4,8,128]{3,2,1,0:T(8,128)S(1)}, f32[8,4,8,128]{3,2,1,0:T(8,128)S(1)}, u32[]{:S(2)}, u32[]{:S(2)}) collective-permute-start(f32[8,4,8,128]{3,2,1,0:T(8,128)S(1)} %get-tuple-element.13.applied), channel_id=1, source_target_pairs={{16,0},{24,8},{32,16},{40,24},{48,32},{56,40},{64,48},{72,56},{80,... | collective-permute-start | bytes 393224 | tf_op jit(solution)/shard_map/ppermute | solution.py:342
  45.8 5.9 %collective-permute-start.2 = (f32[8,4,8,128]{3,2,1,0:T(8,128)S(1)}, f32[8,4,8,128]{3,2,1,0:T(8,128)S(1)}, u32[]{:S(2)}, u32[]{:S(2)}) collective-permute-start(f32[8,4,8,128]{3,2,1,0:T(8,128)S(1)} %get-tuple-element.13.applied), channel_id=1, source_target_pairs={{0,16},{8,24},{16,32},{24,40},{32,48},{40,56},{48,64},{56,72},{64,... | collective-permute-start | bytes 393224 | tf_op jit(solution)/shard_map/ppermute | solution.py:342
  51.7 1.6 %collective-permute-done.3.above = f32[8,4,8,128]{3,2,1,0:T(8,128)S(1)} collective-permute-done((f32[8,4,8,128]{3,2,1,0:T(8,128)S(1)}, f32[8,4,8,128]{3,2,1,0:T(8,128)S(1)}, u32[]{:S(2)}, u32[]{:S(2)}) %collective-permute-start.3) | collective-permute-done | bytes 131104 | tf_op jit(solution)/shard_map/ppermute | solution.py:342
  53.3 0.9 collective-permute-done.2.below
  54.2 1.6 %shard_map.61 = f32[8,3,2,8,128]{4,3,2,1,0:T(8,128)S(1)} custom-call(f32[8,4,8,128]{3,2,1,0:T(8,128)S(1)} %get-tuple-element.12.first, f32[8,4,8,128]{3,2,1,0:T(8,128)S(1)} %get-tuple-element.13.applied, f32[8,4,8,128]{3,2,1,0:T(8,128)S(1)} %collective-permute-done.2.below, f32[8,4,8,128]{3,2,1,0:T(8,128)S(1)} %collective-permute-done.3.above, ...), custom_call_target="tpu_custom_call" | custom-call | tf_op jit(solution)/shard_map/pallas_call | solution.py:369
  55.8 0.0 copy-start
  55.8 9.7 %all_to_all.21 = f32[8,3,2,8,128]{4,3,2,1,0:T(8,128)S(1)} all-to-all(f32[8,3,2,8,128]{4,3,2,1,0:T(8,128)S(1)} %shard_map.61), channel_id=1, replica_groups=mesh['z'=16,'p'=4,'h'=2,'c'=2,'x'=4] {'x','c'}, dimensions={0} | all-to-all | bytes 393216 | tf_op jit(solution)/shard_map/all_to_all | solution.py:377
  65.5 0.0 copy-done
  65.5 0.4 shard_map.62
  66.0 23.2 %all_to_all.22 = f32[64,2,128]{2,1,0:T(2,128)S(1)} all-to-all(f32[64,2,128]{2,1,0:T(2,128)S(1)} %shard_map.62), channel_id=1, replica_groups=mesh['z'=16,'p'=4,'h'=2,'c'=2,'x'=4] {'p','h','c','x'}, dimensions={0} | all-to-all | bytes 131072 | tf_op jit(solution)/shard_map/all_to_all | solution.py:383
  89.2 0.1 reduce_sum.9
  89.2 23.3 %all_to_all.23.sums = f32[16,2,128]{2,1,0:T(2,128)S(1)} all-to-all(f32[16,2,128]{2,1,0:T(2,128)S(1)} %broadcast_in_dim.3), channel_id=1, replica_groups=mesh['z'=16,'p'=4,'h'=2,'c'=2,'x'=4] {'z'}, dimensions={0} | all-to-all | bytes 32768 | tf_op jit(solution)/shard_map/all_to_all | solution.py:385
  112.5 1.5 %shard_map.63 = (f32[128,128]{1,0:T(8,128)}, f32[128,128]{1,0:T(8,128)}, f32[128,128]{1,0:T(8,128)}) custom-call(f32[16,2,128]{2,1,0:T(2,128)S(1)} %all_to_all.23.sums, f32[384,128]{1,0:T(8,128)S(1)} %bitcast.8, f32[128,128]{1,0:T(8,128)S(1)} %bitcast.10), custom_call_target="tpu_custom_call" | custom-call | tf_op jit(solution)/shard_map/pallas_call | solution.py:386
  (2 shorter events, 0.0 us)
Async XLA Ops:
  26.9 9.6 %collective-permute-start.1 = (f32[16,2,2,8,128]{4,3,2,1,0:T(8,128)S(1)}, f32[16,2,2,8,128]{4,3,2,1,0:T(8,128)S(1)}, u32[]{:S(2)}, u32[]{:S(2)}) collective-permute-start(f32[16,2,2,8,128]{4,3,2,1,0:T(8,128)S(1)} %all_to_all.20.refs_0_.own), channel_id=1, source_target_pairs={{16,0},{32,16},{8,24},{48,32},{24,40},{64,48},{40,56},{80,64},{56,... | collective-permute-start | bytes 786440 | tf_op jit(solution)/shard_map/ppermute | solution.py:342
  28.2 8.3 %collective-permute-start = (f32[16,2,2,8,128]{4,3,2,1,0:T(8,128)S(1)}, f32[16,2,2,8,128]{4,3,2,1,0:T(8,128)S(1)}, u32[]{:S(2)}, u32[]{:S(2)}) collective-permute-start(f32[16,2,2,8,128]{4,3,2,1,0:T(8,128)S(1)} %all_to_all.20.refs_0_.own), channel_id=1, source_target_pairs={{16,8},{8,16},{32,24},{24,32},{48,40},{40,48},{64,56},{56,64},{80,... | collective-permute-start | bytes 786440 | tf_op jit(solution)/shard_map/ppermute | solution.py:342
  44.5 8.8 %collective-permute-start.3 = (f32[8,4,8,128]{3,2,1,0:T(8,128)S(1)}, f32[8,4,8,128]{3,2,1,0:T(8,128)S(1)}, u32[]{:S(2)}, u32[]{:S(2)}) collective-permute-start(f32[8,4,8,128]{3,2,1,0:T(8,128)S(1)} %get-tuple-element.13.applied), channel_id=1, source_target_pairs={{16,0},{24,8},{32,16},{40,24},{48,32},{56,40},{64,48},{72,56},{80,... | collective-permute-start | bytes 393224 | tf_op jit(solution)/shard_map/ppermute | solution.py:342
  45.8 8.4 %collective-permute-start.2 = (f32[8,4,8,128]{3,2,1,0:T(8,128)S(1)}, f32[8,4,8,128]{3,2,1,0:T(8,128)S(1)}, u32[]{:S(2)}, u32[]{:S(2)}) collective-permute-start(f32[8,4,8,128]{3,2,1,0:T(8,128)S(1)} %get-tuple-element.13.applied), channel_id=1, source_target_pairs={{0,16},{8,24},{16,32},{24,40},{32,48},{40,56},{48,64},{56,72},{64,... | collective-permute-start | bytes 393224 | tf_op jit(solution)/shard_map/ppermute | solution.py:342
  55.8 9.7 %copy-start = (f32[8,2,8,128]{3,2,1,0:T(8,128)S(1)}, f32[8,2,8,128]{3,2,1,0:T(8,128)}, u32[]{:S(2)}) copy-start(f32[8,2,8,128]{3,2,1,0:T(8,128)} %rhs.1) | copy-start | bytes 196612

commit v11 on v10

--- a/solution.py
+++ b/solution.py
@@ -378,11 +378,11 @@
     rows = rhs.reshape(8 * 16, LANES)
 
     tile = pl.pallas_call(
-        gram_kernel, out_shape=f32(sizes["p"] * 4 * sizes["x"], 2, LANES), in_specs=vmem(2), out_specs=vmem(1)[0], compiler_params=PARAMS
+        gram_kernel, out_shape=f32(sizes["z"], 2, LANES), in_specs=vmem(2), out_specs=vmem(1)[0], compiler_params=PARAMS
     )(parts, rows)
-    tile = lax.all_to_all(tile, ("p", "h", "c", "x"), 0, 0).sum(0)
-    tile = jnp.broadcast_to(tile, (sizes["z"], 2, LANES))
-    tile = lax.all_to_all(tile, "z", 0, 0)
+    tile = lax.all_to_all(tile, "z", 0, 0).sum(0)
+    tile = jnp.broadcast_to(tile, (sizes["p"] * 4 * sizes["x"], 2, LANES))
+    tile = lax.all_to_all(tile, ("p", "h", "c", "x"), 0, 0)
     outs = pl.pallas_call(
         final_kernel,
         out_shape=[f32(128, LANES)] * 3,

time: 115 us -> 116 us (level)
  blocking collectives: 86.3 us -> 87.7 us
    all_to_all x2, blocking collectives: 46.4 us -> 47.8 us  [the longest x1 31.2 us: local(): tile = lax.all_to_all(tile, 'z', 0, 0).sum(0)]
where the time goes in v11:
time: 116 us; the launch traced here: 115 us
  blocking collectives  87.7 us (76%)
  waiting for transfers between devices  10.1 us (9%)
  starting transfers between devices  9.15 us (8%)
  Pallas kernels  7.76 us (7%)
    all_to_all x1, blocking collectives, local(): tile = lax.all_to_all(tile, 'z', 0, 0).sum(0)  31.2 us
    all_to_all x1, blocking collectives, local(): own = lax.all_to_all(packed, ('x', 'h', 'c'), 0, 0)  24.7 us
    all_to_all x1, blocking collectives, local(): tile = lax.all_to_all(tile, ('p', 'h', 'c', 'x'), 0, 0)  16.6 us
    ppermute x4, waiting for transfers between devices, moved(): lax.ppermute(v, chip, [(s, i) for i, s in enumerate(sources) if 0 <= s <...  10.1 us
    all_to_all x1, blocking collectives, local(): parts = lax.all_to_all(results, ('x', 'c'), 0, 0).reshape(8 * 48, LANES)  9.72 us
    ppermute x4, starting transfers between devices, moved(): lax.ppermute(v, chip, [(s, i) for i, s in enumerate(sources) if 0 <= s <...  9.15 us
    all_gather x1, blocking collectives, both_cores(): return lax.all_gather(grids, 'c')  5.44 us
    pallas_call x1, Pallas kernels, local(): pl.pallas_call(first_kernel, out_shape=[f32(8, *TILE)] * 2 + [f32(24, *TI...  2.51 us
  transfers between devices with their start and end apart: 4, of which 3 were waited for; matrix products, arithmetic and copies ran while one was open for 0% of the time, Pallas kernels for 0%

profile of v11, /device:TPU:1, one launch (start us, length us, event | category | flops | bytes accessed | tf_op | source)
XLA Modules:
  0.0 115.5 jit_solution(7068506812243716175)
XLA Ops:
  0.6 1.6 %shard_map.58 = f32[16,2,2,8,128]{4,3,2,1,0:T(8,128)} custom-call(f32[8,2,8,128]{3,2,1,0:T(8,128)} %rhs.1, s32[2,8,128]{2,1,0:T(8,128)} %classes.1, s32[2,8,128]{2,1,0:T(8,128)} %supports.1), custom_call_target="tpu_custom_call" | custom-call | tf_op jit(solution)/shard_map/pallas_call | solution.py:326
  2.2 24.7 %all_to_all.20.refs_0_.own = f32[16,2,2,8,128]{4,3,2,1,0:T(8,128)S(1)} all-to-all(f32[16,2,2,8,128]{4,3,2,1,0:T(8,128)} %shard_map.58), channel_id=1, replica_groups=mesh['z'=16,'p'=4,'h'=2,'c'=2,'x'=4] {'x','h','c'}, dimensions={0} | all-to-all | bytes 524288 | tf_op jit(solution)/shard_map/all_to_all | solution.py:339
  26.9 1.3 %collective-permute-start.1 = (f32[16,2,2,8,128]{4,3,2,1,0:T(8,128)S(1)}, f32[16,2,2,8,128]{4,3,2,1,0:T(8,128)S(1)}, u32[]{:S(2)}, u32[]{:S(2)}) collective-permute-start(f32[16,2,2,8,128]{4,3,2,1,0:T(8,128)S(1)} %all_to_all.20.refs_0_.own), channel_id=1, source_target_pairs={{16,0},{32,16},{8,24},{48,32},{24,40},{64,48},{40,56},{80,64},{56,... | collective-permute-start | bytes 786440 | tf_op jit(solution)/shard_map/ppermute | solution.py:342
  28.2 0.7 collective-permute-start
  28.9 7.6 %collective-permute-done.1.refs_2_.far = f32[16,2,2,8,128]{4,3,2,1,0:T(8,128)S(1)} collective-permute-done((f32[16,2,2,8,128]{4,3,2,1,0:T(8,128)S(1)}, f32[16,2,2,8,128]{4,3,2,1,0:T(8,128)S(1)}, u32[]{:S(2)}, u32[]{:S(2)}) %collective-permute-start.1) | collective-permute-done | bytes 262176 | tf_op jit(solution)/shard_map/ppermute | solution.py:342
  36.5 0.0 collective-permute-done.refs_1_.swap
  36.5 5.4 %all-gather = f32[6,16,2,8,128]{4,3,2,1,0:T(8,128)S(1)} all-gather(f32[3,16,2,8,128]{4,3,2,1,0:T(8,128)S(1)} %shard_map.59), channel_id=2, replica_groups=mesh['z'=16,'p'=4,'h'=2,'c'=2,'x'=4] {'c'}, dimensions={0}, use_global_device_ids=true | all-gather | bytes 1179648 | tf_op jit(solution)/shard_map/all_gather | solution.py:356
  42.0 2.5 %shard_map.60 = (f32[8,4,8,128]{3,2,1,0:T(8,128)S(1)}, f32[8,4,8,128]{3,2,1,0:T(8,128)S(1)}, f32[24,4,8,128]{3,2,1,0:T(8,128)S(1)}, f32[24,4,8,128]{3,2,1,0:T(8,...) custom-call(f32[16,2,2,8,128]{4,3,2,1,0:T(8,128)S(1)} %all_to_all.20.refs_0_.own, ...), custom_call_target="tpu_custom_call" | custom-call | tf_op jit(solution)/shard_map/pallas_call | solution.py:359
  44.5 1.3 %collective-permute-start.3 = (f32[8,4,8,128]{3,2,1,0:T(8,128)S(1)}, f32[8,4,8,128]{3,2,1,0:T(8,128)S(1)}, u32[]{:S(2)}, u32[]{:S(2)}) collective-permute-start(f32[8,4,8,128]{3,2,1,0:T(8,128)S(1)} %get-tuple-element.13.applied), channel_id=1, source_target_pairs={{16,0},{24,8},{32,16},{40,24},{48,32},{56,40},{64,48},{72,56},{80,... | collective-permute-start | bytes 393224 | tf_op jit(solution)/shard_map/ppermute | solution.py:342
  45.8 5.9 %collective-permute-start.2 = (f32[8,4,8,128]{3,2,1,0:T(8,128)S(1)}, f32[8,4,8,128]{3,2,1,0:T(8,128)S(1)}, u32[]{:S(2)}, u32[]{:S(2)}) collective-permute-start(f32[8,4,8,128]{3,2,1,0:T(8,128)S(1)} %get-tuple-element.13.applied), channel_id=1, source_target_pairs={{0,16},{8,24},{16,32},{24,40},{32,48},{40,56},{48,64},{56,72},{64,... | collective-permute-start | bytes 393224 | tf_op jit(solution)/shard_map/ppermute | solution.py:342
  51.7 1.6 %collective-permute-done.3.above = f32[8,4,8,128]{3,2,1,0:T(8,128)S(1)} collective-permute-done((f32[8,4,8,128]{3,2,1,0:T(8,128)S(1)}, f32[8,4,8,128]{3,2,1,0:T(8,128)S(1)}, u32[]{:S(2)}, u32[]{:S(2)}) %collective-permute-start.3) | collective-permute-done | bytes 131104 | tf_op jit(solution)/shard_map/ppermute | solution.py:342
  53.3 0.9 collective-permute-done.2.below
  54.2 1.6 %shard_map.61 = f32[8,3,2,8,128]{4,3,2,1,0:T(8,128)S(1)} custom-call(f32[8,4,8,128]{3,2,1,0:T(8,128)S(1)} %get-tuple-element.12.first, f32[8,4,8,128]{3,2,1,0:T(8,128)S(1)} %get-tuple-element.13.applied, f32[8,4,8,128]{3,2,1,0:T(8,128)S(1)} %collective-permute-done.2.below, f32[8,4,8,128]{3,2,1,0:T(8,128)S(1)} %collective-permute-done.3.above, ...), custom_call_target="tpu_custom_call" | custom-call | tf_op jit(solution)/shard_map/pallas_call | solution.py:369
  55.8 0.0 copy-start
  55.8 9.7 %all_to_all.21 = f32[8,3,2,8,128]{4,3,2,1,0:T(8,128)S(1)} all-to-all(f32[8,3,2,8,128]{4,3,2,1,0:T(8,128)S(1)} %shard_map.61), channel_id=1, replica_groups=mesh['z'=16,'p'=4,'h'=2,'c'=2,'x'=4] {'x','c'}, dimensions={0} | all-to-all | bytes 393216 | tf_op jit(solution)/shard_map/all_to_all | solution.py:377
  65.5 0.0 copy-done
  65.5 0.4 shard_map.62
  66.0 31.2 %all_to_all.22 = f32[16,2,128]{2,1,0:T(2,128)S(1)} all-to-all(f32[16,2,128]{2,1,0:T(2,128)S(1)} %shard_map.62), channel_id=1, replica_groups=mesh['z'=16,'p'=4,'h'=2,'c'=2,'x'=4] {'z'}, dimensions={0} | all-to-all | bytes 32768 | tf_op jit(solution)/shard_map/all_to_all | solution.py:383
  97.2 16.6 %all_to_all.23.sums = f32[64,2,128]{2,1,0:T(2,128)S(1)} all-to-all(f32[64,2,128]{2,1,0:T(2,128)S(1)} %broadcast_in_dim.3), channel_id=1, replica_groups=mesh['z'=16,'p'=4,'h'=2,'c'=2,'x'=4] {'p','h','c','x'}, dimensions={0} | all-to-all | bytes 131072 | tf_op jit(solution)/shard_map/all_to_all | solution.py:385
  113.9 1.6 %shard_map.63 = (f32[128,128]{1,0:T(8,128)}, f32[128,128]{1,0:T(8,128)}, f32[128,128]{1,0:T(8,128)}) custom-call(f32[64,2,128]{2,1,0:T(2,128)S(1)} %all_to_all.23.sums, f32[384,128]{1,0:T(8,128)S(1)} %bitcast.8, f32[128,128]{1,0:T(8,128)S(1)} %bitcast.10), custom_call_target="tpu_custom_call" | custom-call | tf_op jit(solution)/shard_map/pallas_call | solution.py:386
  (3 shorter events, 0.1 us)
Async XLA Ops:
  26.9 9.6 %collective-permute-start.1 = (f32[16,2,2,8,128]{4,3,2,1,0:T(8,128)S(1)}, f32[16,2,2,8,128]{4,3,2,1,0:T(8,128)S(1)}, u32[]{:S(2)}, u32[]{:S(2)}) collective-permute-start(f32[16,2,2,8,128]{4,3,2,1,0:T(8,128)S(1)} %all_to_all.20.refs_0_.own), channel_id=1, source_target_pairs={{16,0},{32,16},{8,24},{48,32},{24,40},{64,48},{40,56},{80,64},{56,... | collective-permute-start | bytes 786440 | tf_op jit(solution)/shard_map/ppermute | solution.py:342
  28.2 8.3 %collective-permute-start = (f32[16,2,2,8,128]{4,3,2,1,0:T(8,128)S(1)}, f32[16,2,2,8,128]{4,3,2,1,0:T(8,128)S(1)}, u32[]{:S(2)}, u32[]{:S(2)}) collective-permute-start(f32[16,2,2,8,128]{4,3,2,1,0:T(8,128)S(1)} %all_to_all.20.refs_0_.own), channel_id=1, source_target_pairs={{16,8},{8,16},{32,24},{24,32},{48,40},{40,48},{64,56},{56,64},{80,... | collective-permute-start | bytes 786440 | tf_op jit(solution)/shard_map/ppermute | solution.py:342
  44.5 8.8 %collective-permute-start.3 = (f32[8,4,8,128]{3,2,1,0:T(8,128)S(1)}, f32[8,4,8,128]{3,2,1,0:T(8,128)S(1)}, u32[]{:S(2)}, u32[]{:S(2)}) collective-permute-start(f32[8,4,8,128]{3,2,1,0:T(8,128)S(1)} %get-tuple-element.13.applied), channel_id=1, source_target_pairs={{16,0},{24,8},{32,16},{40,24},{48,32},{56,40},{64,48},{72,56},{80,... | collective-permute-start | bytes 393224 | tf_op jit(solution)/shard_map/ppermute | solution.py:342
  45.8 8.4 %collective-permute-start.2 = (f32[8,4,8,128]{3,2,1,0:T(8,128)S(1)}, f32[8,4,8,128]{3,2,1,0:T(8,128)S(1)}, u32[]{:S(2)}, u32[]{:S(2)}) collective-permute-start(f32[8,4,8,128]{3,2,1,0:T(8,128)S(1)} %get-tuple-element.13.applied), channel_id=1, source_target_pairs={{0,16},{8,24},{16,32},{24,40},{32,48},{40,56},{48,64},{56,72},{64,... | collective-permute-start | bytes 393224 | tf_op jit(solution)/shard_map/ppermute | solution.py:342
  55.8 9.7 %copy-start = (f32[8,2,8,128]{3,2,1,0:T(8,128)S(1)}, f32[8,2,8,128]{3,2,1,0:T(8,128)}, u32[]{:S(2)}) copy-start(f32[8,2,8,128]{3,2,1,0:T(8,128)} %rhs.1) | copy-start | bytes 196612
